TPU v7x, 512 devices: a whole 4x8x8 slice. The times are simulated.
512 devices in a mesh: dom: 128 (over z, y, core), grp: 4 (over x).
Axes of the slice: x: 4, y: 8, z: 8, core: 2. Of those that a mesh axis runs over, the one named last changes fastest.
Arguments:
- source_emb: float32 [400, 65536], P(None, ('dom', 'grp')), may hold values from -2.5 to 2.5
- source_state: float32 [65536], P(('dom', 'grp')), may hold values from 0.005 to 0.1
- dest_emb: float32 [400, 65536], P(None, ('dom', 'grp')), may hold values from -2.5 to 2.5
- dest_state: float32 [65536], P(('dom', 'grp')), may hold values from 0.005 to 0.1
- relations: float32 [400, 768], replicated, may hold values from -4 to 4
- relation_state: float32 [768], replicated, may hold values from 1 to 30
- partner: int32 [128, 4], P('dom', 'grp'), may hold values from 0 to 127, as said below
- edge_count: int32 [128, 4], P('dom', 'grp'), may hold values from 1 to 1024, as said below
- source_rows: int32 [128, 4, 1024], P('dom', 'grp'), may hold values from 0 to 127
- target_rows: int32 [128, 4, 1024], P('dom', 'grp'), may hold values from 0 to 127
- relation_index: int32 [128, 4, 1024], P('dom', 'grp'), may hold values from 0 to 767
- negative_rows: int32 [128, 4, 2048], P('dom', 'grp'), may hold values from 0 to 127
Outputs:
- source_out: float32 [400, 65536], P(None, ('dom', 'grp'))
- source_state_out: float32 [65536], P(('dom', 'grp'))
- dest_out: float32 [400, 65536], P(None, ('dom', 'grp'))
- dest_state_out: float32 [65536], P(('dom', 'grp'))
- relations_out: float32 [400, 768], replicated
- relation_state_out: float32 [768], replicated
Inputs may be any that keep to these rules, and one draw needn't show every extreme that they name: For each grp index g, partner[:, g] is a permutation of 0 .. 127. `edge_count`: some device has all 1024 edges live.
All inputs are finite; a program needn't handle non-finite values.
Results may differ from a plain program's by a relative error of at most 0.0013.
The roundings to bfloat16 on the way count: a program that leaves them out, or rounds other values in their place, can miss the bound.
Values sent between devices are 32-bit elements; how exact they have to be, the bound alone decides.
No kernel may reach another device: no remote copies, remote signals or barrier semaphores. Data moves between devices by JAX's collectives and lax.ppermute only.
A program may use at most 64 MiB of HBM per device.

v0:
```python
import jax
import jax.numpy as jnp
from jax import lax
from jax.sharding import PartitionSpec as P

SPAN = 512
SPANS = 2
NEG = 1024
EDGES = 1024


learn_rate = 0.3
epsilon = 1e-08


def passed_along(value, axis, steps):
    count = lax.axis_size(axis)
    pairs = [(source, (source + steps) % count) for source in range(count)]
    return lax.ppermute(value, axis, pairs)


def adagrad(param, state, grad):
    new_state = state + jnp.mean(grad * grad, axis=0)
    return (param - learn_rate * grad / (jnp.sqrt(new_state) + epsilon), new_state)


def contract_last(left, right):
    return lax.dot_general(
        left, right, (((1,), (1,)), ((), ())), preferred_element_type=jnp.float32
    )


def selector(count, rows):
    return (jnp.arange(count, dtype=jnp.int32)[:, None] == rows[None, :]).astype(jnp.bfloat16)


def train_block(
    source, source_acc, target, target_acc, relation_bf, rows_s, rows_t, rows_r, rows_n, live
):
    width = source.shape[0]
    half = width // 2
    block = source.shape[1]
    pick_source = selector(block, rows_s)
    pick_target = selector(block, rows_t)
    pick_noise = selector(block, rows_n)
    pick_relation = selector(relation_bf.shape[1], rows_r)
    source_bf = source.astype(jnp.bfloat16)
    target_bf = target.astype(jnp.bfloat16)
    subject = jnp.dot(source_bf, pick_source, preferred_element_type=jnp.float32)
    operator = jnp.dot(relation_bf, pick_relation, preferred_element_type=jnp.float32)
    objects = jnp.dot(target_bf, pick_target, preferred_element_type=jnp.float32)
    noise = jnp.dot(target_bf, pick_noise, preferred_element_type=jnp.float32).astype(jnp.bfloat16)
    subject_re, subject_im = (subject[:half], subject[half:])
    operator_re, operator_im = (operator[:half], operator[half:])
    query = jnp.concatenate(
        [
            subject_re * operator_re - subject_im * operator_im,
            subject_re * operator_im + subject_im * operator_re,
        ],
        0,
    )
    positive = jnp.sum(query * objects, axis=0)
    query_bf = query.astype(jnp.bfloat16)
    negative = lax.dot_general(
        query_bf, noise, (((0,), (0,)), ((), ())), preferred_element_type=jnp.float32
    )
    grad_pos = -jax.nn.sigmoid(-positive) * live
    grad_neg = (jax.nn.sigmoid(negative) * (live[:, None] / NEG)).astype(jnp.bfloat16)
    grad_query = grad_pos[None, :] * objects + contract_last(noise, grad_neg)
    grad_objects = grad_pos[None, :] * query
    grad_noise = jnp.dot(query_bf, grad_neg, preferred_element_type=jnp.float32)
    query_gre, query_gim = (grad_query[:half], grad_query[half:])
    grad_subject = jnp.concatenate(
        [
            query_gre * operator_re + query_gim * operator_im,
            query_gim * operator_re - query_gre * operator_im,
        ],
        0,
    )
    grad_operator = jnp.concatenate(
        [
            query_gre * subject_re + query_gim * subject_im,
            query_gim * subject_re - query_gre * subject_im,
        ],
        0,
    )
    grad_source = contract_last(grad_subject.astype(jnp.bfloat16), pick_source)
    grad_target = contract_last(grad_objects.astype(jnp.bfloat16), pick_target)
    grad_target = grad_target + contract_last(grad_noise.astype(jnp.bfloat16), pick_noise)
    grad_local = contract_last(grad_operator.astype(jnp.bfloat16), pick_relation)
    new_source, new_source_acc = adagrad(source, source_acc, grad_source)
    new_target, new_target_acc = adagrad(target, target_acc, grad_target)
    return (new_source, new_source_acc, new_target, new_target_acc, grad_local)


def relation_step(relations, relation_state, grad_local):
    total = lax.psum(grad_local, ("dom", "grp"))
    return adagrad(relations, relation_state, total)


def local(
    source_emb,
    source_state,
    dest_emb,
    dest_state,
    relations,
    relation_state,
    partner,
    edge_count,
    source_rows,
    target_rows,
    relation_index,
    negative_rows,
):
    width = source_emb.shape[0]
    block = source_emb.shape[1]
    members = lax.axis_size("dom")
    piece = block // members
    cargo = jnp.concatenate([dest_emb, dest_state[None, :]], 0)
    cargo = passed_along(cargo, "grp", 1)
    partners = lax.all_gather(partner[0], "dom", axis=0, tiled=True)
    spread = lax.all_to_all(
        cargo.reshape(width + 1, members, piece), "dom", split_axis=1, concat_axis=1, tiled=True
    )
    spread = jnp.take(spread, partners, axis=1)
    arrived = lax.all_to_all(spread, "dom", split_axis=1, concat_axis=1, tiled=True).reshape(
        width + 1, block
    )
    target = arrived[:width]
    target_acc = arrived[width]
    source = source_emb
    source_acc = source_state
    live_all = (jnp.arange(EDGES, dtype=jnp.int32) < edge_count[0, 0]).astype(jnp.float32)
    for step in range(SPANS):
        first = step * SPAN
        first_neg = step * NEG
        relation_bf = relations.astype(jnp.bfloat16)
        source, source_acc, target, target_acc, grad_local = train_block(
            source,
            source_acc,
            target,
            target_acc,
            relation_bf,
            source_rows[0, 0, first : first + SPAN],
            target_rows[0, 0, first : first + SPAN],
            relation_index[0, 0, first : first + SPAN],
            negative_rows[0, 0, first_neg : first_neg + NEG],
            live_all[first : first + SPAN],
        )
        relations, relation_state = relation_step(relations, relation_state, grad_local)
    cargo = jnp.concatenate([target, target_acc[None, :]], 0).reshape(width + 1, members, piece)
    collected = lax.all_to_all(cargo, "dom", split_axis=1, concat_axis=1, tiled=True)
    inverse = (
        jnp.zeros((members,), jnp.int32).at[partners].set(jnp.arange(members, dtype=jnp.int32))
    )
    collected = jnp.take(collected, inverse, axis=1)
    returned = lax.all_to_all(collected, "dom", split_axis=1, concat_axis=1, tiled=True).reshape(
        width + 1, block
    )
    settled = passed_along(returned, "grp", -1)
    return (source, source_acc, settled[:width], settled[width], relations, relation_state)


def solution(mesh):
    in_specs = (
        P(None, ("dom", "grp")),
        P(("dom", "grp")),
        P(None, ("dom", "grp")),
        P(("dom", "grp")),
        P(),
        P(),
        P("dom", "grp"),
        P("dom", "grp"),
        P("dom", "grp", None),
        P("dom", "grp", None),
        P("dom", "grp", None),
        P("dom", "grp", None),
    )
    out_specs = (
        P(None, ("dom", "grp")),
        P(("dom", "grp")),
        P(None, ("dom", "grp")),
        P(("dom", "grp")),
        P(),
        P(),
    )
    return jax.shard_map(local, mesh=mesh, in_specs=in_specs, out_specs=out_specs, check_vma=False)
```

profile of v0, /device:TPU:1, one launch (start us, length us, event | category | flops | bytes accessed | tf_op | source)
XLA Modules:
  0.0 704.8 jit_solution(11849376523727967690)
XLA Ops:
  8.2 3.9 collective-permute-start
  12.8 1.3 dynamic-slice
  14.8 27.5 %all-reduce = s32[128]{0:T(128)S(1)} all-reduce(s32[128]{0:T(128)S(1)} %bitcast_dynamic-update-slice_fusion), channel_id=2, replica_groups=mesh['dom'=128,'grp'=4] {'dom'}, use_global_device_ids=true, to_apply=%add | all-reduce | flops 128 | bytes 1024 | tf_op jit(solution)/shard_map/all_gather | solution.py:121
  46.1 1.2 convolution_bitcast_fusion
  48.2 10.6 %all-to-all-start = ((f32[401,128,1]{0,2,1:T(1,128)}), f32[401,128,1]{0,2,1:T(1,128)S(1)}, u32[]{:S(2)}, u32[]{:S(2)}) async-start(f32[401,128,1]{0,2,1:T(1,128)} %copy.35), calls=%async_computation | async-start | bytes 524288 | tf_op jit(solution)/shard_map/all_to_all | solution.py:122
  60.1 14.0 %all-to-all-done = f32[401,128,1]{0,2,1:T(1,128)S(1)} async-done(((f32[401,128,1]{0,2,1:T(1,128)}), f32[401,128,1]{0,2,1:T(1,128)S(1)}, u32[]{:S(2)}, u32[]{:S(2)}) %all-to-all-start) | async-done | bytes 205344 | tf_op jit(solution)/shard_map/all_to_all | solution.py:122
  76.0 6.6 all-to-all-start.1
  83.7 13.8 %all-to-all-done.1 = f32[401,128,1]{0,2,1:T(1,128)} async-done(((f32[401,128,1]{0,2,1:T(1,128)}), f32[401,128,1]{0,2,1:T(1,128)}, u32[]{:S(2)}, u32[]{:S(2)}) %all-to-all-start.1) | async-done | bytes 205344 | tf_op jit(solution)/shard_map/all_to_all | solution.py:126
  97.6 1.1 copy.47
  99.7 1.2 multiply_reduce_fusion.3
  101.8 2.0 multiply_convert_fusion.1
  103.8 2.9 multiply_reduce_fusion.6
  106.7 2.3 convolution_add_fusion.1
  109.4 1.6 fusion.2
  111.3 2.7 slice_reduce_fusion
  114.1 1.3 convolution_convert_fusion.1
  115.7 261.2 %all-reduce.4.cloned.1.call-done = f32[400,768]{1,0:T(8,128)} async-done(((f32[400,768]{1,0:T(8,128)}), f32[400,768]{1,0:T(8,128)}) %all-reduce.4.cloned.1.call-update) | async-done | bytes 1228816 | tf_op jit(solution)/shard_map/psum | solution.py:97
  377.0 1.5 multiply_reduce_fusion.1
  380.1 1.2 multiply_reduce_fusion.2
  382.3 2.0 multiply_convert_fusion
  384.3 3.0 multiply_reduce_fusion.4
  387.3 2.4 convolution_add_fusion
  389.7 1.3 add_convert_fusion
  391.9 10.2 %all-to-all-start.2 = ((f32[401,128,1]{0,2,1:T(1,128)}), f32[401,128,1]{0,2,1:T(1,128)S(1)}, u32[]{:S(2)}, u32[]{:S(2)}) async-start(f32[401,128,1]{0,2,1:T(1,128)} %copy.40), calls=%async_computation.2 | async-start | bytes 524288 | tf_op jit(solution)/shard_map/all_to_all | solution.py:152
  402.2 2.6 fusion
  405.6 11.8 %all-to-all-done.2 = f32[401,128,1]{0,2,1:T(1,128)S(1)} async-done(((f32[401,128,1]{0,2,1:T(1,128)}), f32[401,128,1]{0,2,1:T(1,128)S(1)}, u32[]{:S(2)}, u32[]{:S(2)}) %all-to-all-start.2) | async-done | bytes 205344 | tf_op jit(solution)/shard_map/all_to_all | solution.py:152
  419.2 5.5 all-to-all-start.3
  425.5 260.5 %all-reduce.6.cloned.1.call-done = f32[400,768]{1,0:T(8,128)} async-done(((f32[400,768]{1,0:T(8,128)}), f32[400,768]{1,0:T(8,128)}) %all-reduce.6.cloned.1.call-update) | async-done | bytes 1228816 | tf_op jit(solution)/shard_map/psum | solution.py:97
  686.0 1.4 multiply_reduce_fusion
  688.1 3.1 collective-permute-start.1
  691.3 2.6 divide_subtract_fusion
  693.9 2.9 collective-permute-done.1
  (99 shorter events, 21.8 us)
Async XLA Ops:
  7.2 52.4 %copy-start = (f32[400,768]{1,0:T(8,128)S(1)}, f32[400,768]{1,0:T(8,128)}, u32[]{:S(2)}) copy-start(f32[400,768]{1,0:T(8,128)} %param.18) | copy-start | bytes 3686404
  8.2 39.1 %collective-permute-start = (f32[401,128]{1,0:T(8,128)S(1)}, f32[401,128]{1,0:T(8,128)S(1)}, u32[]{:S(2)}, u32[]{:S(2)}) collective-permute-start(f32[401,128]{1,0:T(8,128)S(1)} %pad_maximum_fusion.2), channel_id=1, source_target_pairs={{0,1},{1,2},{2,3},{3,0},{4,5},{5,6},{6,7},{7,4},{8,9},{9,10},{10,1... | collective-permute-start | bytes 615944 | tf_op jit(solution)/shard_map/ppermute | solution.py:19
  48.2 25.9 %all-to-all-start = ((f32[401,128,1]{0,2,1:T(1,128)}), f32[401,128,1]{0,2,1:T(1,128)S(1)}, u32[]{:S(2)}, u32[]{:S(2)}) async-start(f32[401,128,1]{0,2,1:T(1,128)} %copy.35), calls=%async_computation | async-start | bytes 524288 | tf_op jit(solution)/shard_map/all_to_all | solution.py:122
  76.0 21.6 %all-to-all-start.1 = ((f32[401,128,1]{0,2,1:T(1,128)}), f32[401,128,1]{0,2,1:T(1,128)}, u32[]{:S(2)}, u32[]{:S(2)}) async-start(f32[401,128,1]{0,2,1:T(1,128)} %copy.38), calls=%async_computation.1 | async-start | bytes 524288 | tf_op jit(solution)/shard_map/all_to_all | solution.py:126
  82.6 294.4 %all-reduce.4.cloned.1.call-start = ((), (), s32[]{:S(2)}) async-start(), calls=%async_computation.4 | async-start | bytes 2457600 | tf_op jit(solution)/shard_map/psum | solution.py:97
  98.7 1.0 copy-start.8
  99.1 2.8 copy-start.5
  111.0 3.1 copy-start.16
  111.0 3.1 copy-start.19
  111.0 4.4 copy-start.6
  111.3 4.1 copy-start.11
  115.4 263.0 %copy-start.18 = (f32[768]{0:T(1024)S(1)}, f32[768]{0:T(1024)}, u32[]{:S(2)}) copy-start(f32[768]{0:T(1024)} %param.19) | copy-start | bytes 9220
  377.0 1.7 copy-start.1
  379.2 0.9 copy-start.2
  379.4 2.9 copy-start.9
  379.4 2.9 copy-start.10
  380.1 2.2 copy-start.4
  387.3 2.4 copy-start.3
  389.7 1.3 copy-start.17
  391.1 11.1 %copy-start.15 = (bf16[200,512]{1,0:T(8,128)(2,1)S(1)}, bf16[200,512]{1,0:T(8,128)(2,1)}, u32[]{:S(2)}) copy-start(bf16[200,512]{1,0:T(8,128)(2,1)} %get-tuple-element.29) | copy-start | bytes 614404
  391.9 25.4 %all-to-all-start.2 = ((f32[401,128,1]{0,2,1:T(1,128)}), f32[401,128,1]{0,2,1:T(1,128)S(1)}, u32[]{:S(2)}, u32[]{:S(2)}) async-start(f32[401,128,1]{0,2,1:T(1,128)} %copy.40), calls=%async_computation.2 | async-start | bytes 524288 | tf_op jit(solution)/shard_map/all_to_all | solution.py:152
  402.1 283.9 %all-reduce.6.cloned.1.call-start = ((), (), s32[]{:S(2)}) async-start(), calls=%async_computation.5 | async-start | bytes 2457600 | tf_op jit(solution)/shard_map/psum | solution.py:97
  402.2 2.6 copy-start.13
  402.2 2.6 copy-start.14
  418.2 6.6 copy-start.7
  418.2 6.6 copy-start.12
  419.2 268.8 %all-to-all-start.3 = ((f32[401,128,1]{0,2,1:T(1,128)}), f32[401,128,1]{0,2,1:T(1,128)S(1)}, u32[]{:S(2)}, u32[]{:S(2)}) async-start(f32[401,128,1]{0,2,1:T(1,128)} %copy.43), calls=%async_computation.3 | async-start | bytes 524288 | tf_op jit(solution)/shard_map/all_to_all | solution.py:157
  688.1 8.6 %collective-permute-start.1 = (f32[401,128]{1,0:T(8,128)S(1)}, f32[401,128]{1,0:T(8,128)S(1)}, u32[]{:S(2)}, u32[]{:S(2)}) collective-permute-start(f32[401,128]{1,0:T(8,128)S(1)} %bitcast.84), channel_id=1, source_target_pairs={{0,3},{1,0},{2,1},{3,2},{4,7},{5,4},{6,5},{7,6},{8,11},{9,8},{10,9... | collective-permute-start | bytes 615944 | tf_op jit(solution)/shard_map/ppermute | solution.py:19
Sparse Core Ops, SparseCore 0:
  111.1 265.8 all-reduce.3
  409.4 276.5 all-reduce.5
where the time goes:
time: 706 us; the launch traced here: 705 us
  waiting for transfers between devices  564 us (80%)
  starting transfers between devices  40.2 us (6%)
  matrix products  27.9 us (4%)
  blocking collectives  27.5 us (4%)
  local copies, waits for them, and re-layouts  17.5 us (2%)
  between operations  15.8 us (2%)
  other arithmetic  11.5 us (2%)
    psum x2, waiting for transfers between devices, relation_step(): total = lax.psum(grad_local, ('dom', 'grp'))  522 us
    all_gather x1, blocking collectives, local(): partners = lax.all_gather(partner[0], 'dom', axis=0, tiled=True)  27.5 us
    dot_general x10, matrix products, contract_last(): lax.dot_general(left, right, (((1,), (1,)), ((), ())), preferred_element_...  17.3 us
  transfers between devices with their start and end apart: 8, of which 6 were waited for; matrix products, arithmetic and copies ran while one was open for 3% of the time, Pallas kernels for 0%

commit v1 on v0

v1 whole, which is shorter than its diff:
```python
import jax
import jax.numpy as jnp
from jax import lax
from jax.experimental import pallas as pl
from jax.experimental.pallas import tpu as pltpu
from jax.sharding import Mesh
from jax.sharding import PartitionSpec as P

SPAN = 512
SPANS = 2
NEG = 1024
EDGES = 1024

ALL = ("z", "y", "core", "x")
DOM = ("z", "y", "core")

learn_rate = 0.3
epsilon = 1e-08


def passed_along(value, axis, steps):
    count = lax.axis_size(axis)
    pairs = [(source, (source + steps) % count) for source in range(count)]
    return lax.ppermute(value, axis, pairs)


def exchange(value, axis):
    return lax.all_to_all(value, axis, split_axis=0, concat_axis=0, tiled=True)


def gathered(value, axis):
    count = lax.axis_size(axis)
    return exchange(jnp.broadcast_to(value[None], (count,) + value.shape), axis)


def pick_body(index_ref, from_ref, to_ref):
    def one(i, _):
        to_ref[i] = from_ref[index_ref[i]]
        return 0

    lax.fori_loop(0, to_ref.shape[0], one, 0, unroll=8)


def place_body(index_ref, from_ref, to_ref):
    def one(i, _):
        to_ref[index_ref[i]] = from_ref[i]
        return 0

    lax.fori_loop(0, to_ref.shape[0], one, 0, unroll=8)


def rearranged(body, value, index):
    return pl.pallas_call(
        body,
        out_shape=jax.ShapeDtypeStruct(value.shape, value.dtype),
        in_specs=[
            pl.BlockSpec(memory_space=pltpu.SMEM),
            pl.BlockSpec(memory_space=pltpu.VMEM),
        ],
        out_specs=pl.BlockSpec(memory_space=pltpu.VMEM),
    )(index, value)


def adagrad(param, state, grad):
    new_state = state + jnp.mean(grad * grad, axis=0)
    return (param - learn_rate * grad / (jnp.sqrt(new_state) + epsilon), new_state)


def contract_last(left, right):
    return lax.dot_general(
        left, right, (((1,), (1,)), ((), ())), preferred_element_type=jnp.float32
    )


def selector(count, rows):
    return (jnp.arange(count, dtype=jnp.int32)[:, None] == rows[None, :]).astype(jnp.bfloat16)


def train_block(
    source, source_acc, target, target_acc, relation_bf, rows_s, rows_t, rows_r, rows_n, live
):
    half = source.shape[0] // 2
    block = source.shape[1]
    pick_source = selector(block, rows_s)
    pick_target = selector(block, rows_t)
    pick_relation = selector(relation_bf.shape[1], rows_r)
    count = jnp.sum(
        (jnp.arange(block, dtype=jnp.int32)[:, None] == rows_n[None, :]).astype(jnp.float32), axis=1
    )
    source_bf = source.astype(jnp.bfloat16)
    target_bf = target.astype(jnp.bfloat16)
    subject = jnp.dot(source_bf, pick_source, preferred_element_type=jnp.float32)
    operator = jnp.dot(relation_bf, pick_relation, preferred_element_type=jnp.float32)
    objects = jnp.dot(target_bf, pick_target, preferred_element_type=jnp.float32)
    subject_re, subject_im = (subject[:half], subject[half:])
    operator_re, operator_im = (operator[:half], operator[half:])
    query = jnp.concatenate(
        [
            subject_re * operator_re - subject_im * operator_im,
            subject_re * operator_im + subject_im * operator_re,
        ],
        0,
    )
    positive = jnp.sum(query * objects, axis=0)
    query_bf = query.astype(jnp.bfloat16)
    score = lax.dot_general(
        target_bf, query_bf, (((0,), (0,)), ((), ())), preferred_element_type=jnp.float32
    )
    grad_pos = -jax.nn.sigmoid(-positive) * live
    slope = lax.reduce_precision(jax.nn.sigmoid(score) * (live[None, :] / NEG), 8, 7)
    slope = slope.astype(jnp.bfloat16)
    weighted = lax.reduce_precision(slope.astype(jnp.float32), 8, 7) * count[:, None]
    upper = weighted.astype(jnp.bfloat16)
    lower = (weighted - upper.astype(jnp.float32)).astype(jnp.bfloat16)
    twice = jnp.concatenate([target_bf, target_bf], 1)
    grad_query = grad_pos[None, :] * objects + jnp.dot(
        twice, jnp.concatenate([upper, lower], 0), preferred_element_type=jnp.float32
    )
    grad_objects = grad_pos[None, :] * query
    grad_noise = contract_last(query_bf, slope)
    query_gre, query_gim = (grad_query[:half], grad_query[half:])
    grad_subject = jnp.concatenate(
        [
            query_gre * operator_re + query_gim * operator_im,
            query_gim * operator_re - query_gre * operator_im,
        ],
        0,
    )
    grad_operator = jnp.concatenate(
        [
            query_gre * subject_re + query_gim * subject_im,
            query_gim * subject_re - query_gre * subject_im,
        ],
        0,
    )
    grad_source = contract_last(grad_subject.astype(jnp.bfloat16), pick_source)
    grad_target = contract_last(grad_objects.astype(jnp.bfloat16), pick_target)
    grad_target = grad_target + lax.reduce_precision(grad_noise, 8, 7) * count[None, :]
    grad_local = contract_last(grad_operator.astype(jnp.bfloat16), pick_relation)
    new_source, new_source_acc = adagrad(source, source_acc, grad_source)
    new_target, new_target_acc = adagrad(target, target_acc, grad_target)
    return (new_source, new_source_acc, new_target, new_target_acc, grad_local)


def summed(grad):
    width, count = grad.shape
    lanes = 128
    chunks = count // lanes
    n_core, n_x, n_y = (lax.axis_size("core"), lax.axis_size("x"), lax.axis_size("y"))
    parts = n_core * n_x * n_y
    rows = -(-(width * chunks) // (parts * 8)) * 8
    flat = jnp.concatenate([grad[:, k * lanes : (k + 1) * lanes] for k in range(chunks)], 0)
    flat = jnp.pad(flat, ((0, parts * rows - width * chunks), (0, 0)))
    mine = lax.axis_index("core")
    flat = flat.reshape(n_core, n_x * n_y * rows, lanes)
    keep = lax.dynamic_index_in_dim(flat, mine, 0, keepdims=False)
    give = lax.dynamic_index_in_dim(flat, 1 - mine, 0, keepdims=False)
    part = keep + passed_along(give, "core", 1)
    part = jnp.sum(exchange(part.reshape(n_x, n_y * rows, lanes), "x"), 0)
    part = jnp.sum(exchange(part.reshape(n_y, rows, lanes), "y"), 0)
    part = jnp.sum(gathered(part, "z"), 0)
    part = gathered(part, "y").reshape(n_y * rows, lanes)
    part = gathered(part, "x").reshape(n_x * n_y * rows, lanes)
    other = passed_along(part, "core", 1)
    first = jnp.where(mine == 0, part, other)
    second = jnp.where(mine == 0, other, part)
    flat = jnp.concatenate([first, second], 0)
    return jnp.concatenate([flat[k * width : (k + 1) * width] for k in range(chunks)], 1)


def local(
    source_emb,
    source_state,
    dest_emb,
    dest_state,
    relations,
    relation_state,
    partner,
    edge_count,
    source_rows,
    target_rows,
    relation_index,
    negative_rows,
):
    width = source_emb.shape[0]
    block = source_emb.shape[1]
    members = block
    padded = 512
    arriving = passed_along(dest_emb, "x", 1)
    arriving_acc = passed_along(dest_state, "x", 1)
    own = jnp.broadcast_to(partner.reshape(1, 1).astype(jnp.float32), (members, 1))
    cargo = jnp.concatenate([arriving.T, arriving_acc[:, None], own], 1)
    cargo = jnp.pad(cargo, ((0, 0), (0, padded - width - 2))).reshape(members, padded // 128, 128)
    spread = exchange(cargo, DOM)
    partners = spread.reshape(members, padded)[:, width + 1].astype(jnp.int32)
    partners = jnp.clip(partners, 0, members - 1)
    spread = rearranged(pick_body, spread, partners)
    arrived = exchange(spread, DOM).reshape(members, padded)
    target = arrived[:, :width].T
    target_acc = arrived[:, width]
    source = source_emb
    source_acc = source_state
    live_all = (jnp.arange(EDGES, dtype=jnp.int32) < edge_count[0, 0]).astype(jnp.float32)
    for step in range(SPANS):
        first = step * SPAN
        first_neg = step * NEG
        relation_bf = relations.astype(jnp.bfloat16)
        source, source_acc, target, target_acc, grad_local = train_block(
            source,
            source_acc,
            target,
            target_acc,
            relation_bf,
            source_rows[0, 0, first : first + SPAN],
            target_rows[0, 0, first : first + SPAN],
            relation_index[0, 0, first : first + SPAN],
            negative_rows[0, 0, first_neg : first_neg + NEG],
            live_all[first : first + SPAN],
        )
        relations, relation_state = adagrad(relations, relation_state, summed(grad_local))
    cargo = jnp.concatenate([target.T, target_acc[:, None]], 1)
    cargo = jnp.pad(cargo, ((0, 0), (0, padded - width - 1))).reshape(members, padded // 128, 128)
    collected = exchange(cargo, DOM)
    collected = rearranged(place_body, collected, partners)
    returned = exchange(collected, DOM).reshape(members, padded)
    settled = passed_along(returned[:, :width].T, "x", -1)
    settled_acc = passed_along(returned[:, width], "x", -1)
    return (source, source_acc, settled, settled_acc, relations, relation_state)


def solution(mesh):
    fine = Mesh(mesh.devices.reshape(8, 8, 2, 4), ALL)
    in_specs = (
        P(None, ALL),
        P(ALL),
        P(None, ALL),
        P(ALL),
        P(),
        P(),
        P(DOM, "x"),
        P(DOM, "x"),
        P(DOM, "x", None),
        P(DOM, "x", None),
        P(DOM, "x", None),
        P(DOM, "x", None),
    )
    out_specs = (P(None, ALL), P(ALL), P(None, ALL), P(ALL), P(), P())
    return jax.shard_map(local, mesh=fine, in_specs=in_specs, out_specs=out_specs, check_vma=False)
```

time: 706 us -> 300 us (0.42)
  waiting for transfers between devices: 564 us -> 106 us
  starting transfers between devices: 40.2 us -> 92.3 us
  blocking collectives: 27.5 us -> 46.1 us
  matrix products: 27.9 us -> 14.4 us
  between operations: 15.8 us -> 2.96 us
    psum x2 -> x0, waiting for transfers between devices: 522 us -> none  [relation_step(): total = lax.psum(grad_local, ('dom', 'grp'))]
    all_to_all x4 -> x10, waiting for transfers between devices: 39.6 us -> 96.7 us  [exchange(): return lax.all_to_all(value, axis, split_axis=0, concat_axis=0, tiled=True)]
    all_to_all x0 -> x4, blocking collectives: none -> 46.1 us  [exchange(): return lax.all_to_all(value, axis, split_axis=0, concat_axis=0, tiled=True)]
    all_to_all x4 -> x10, starting transfers between devices: 32.9 us -> 62.5 us  [exchange(): return lax.all_to_all(value, axis, split_axis=0, concat_axis=0, tiled=True)]
    all_gather x1 -> x0, blocking collectives: 27.5 us -> none  [local(): partners = lax.all_gather(partner[0], 'dom', axis=0, tiled=True)]
    ppermute x2 -> x8, starting transfers between devices: 7.07 us -> 29.9 us  [passed_along(): return lax.ppermute(value, axis, pairs)]
    dot_general x10 -> x8, matrix products: 17.3 us -> 7.97 us  [contract_last(): lax.dot_general(left, right, (((1,), (1,)), ((), ())), preferred_element_...]
  transfers between devices with their start and end apart: 8 -> 18, of which waited for: 6 -> 15; matrix products, arithmetic and copies ran while one was open for 3% -> 7% of each run, Pallas kernels for 0% -> 1%
where the time goes in v1:
time: 300 us; the launch traced here: 298 us
  waiting for transfers between devices  106 us (35%)
  starting transfers between devices  92.3 us (31%)
  blocking collectives  46.1 us (15%)
  local copies, waits for them, and re-layouts  17.2 us (6%)
  other arithmetic  14.7 us (5%)
  matrix products  14.4 us (5%)
  Pallas kernels  3.74 us (1%)
    all_to_all x10, waiting for transfers between devices, exchange(): return lax.all_to_all(value, axis, split_axis=0, concat_axis=0, tiled=True)  96.7 us
    all_to_all x10, starting transfers between devices, exchange(): return lax.all_to_all(value, axis, split_axis=0, concat_axis=0, tiled=True)  62.5 us
    all_to_all x4, blocking collectives, exchange(): return lax.all_to_all(value, axis, split_axis=0, concat_axis=0, tiled=True)  46.1 us
    ppermute x8, starting transfers between devices, passed_along(): return lax.ppermute(value, axis, pairs)  29.9 us
    ppermute x8, waiting for transfers between devices, passed_along(): return lax.ppermute(value, axis, pairs)  9.83 us
    dot_general x8, matrix products, contract_last(): lax.dot_general(left, right, (((1,), (1,)), ((), ())), preferred_element_...  7.97 us
  transfers between devices with their start and end apart: 18, of which 15 were waited for; matrix products, arithmetic and copies ran while one was open for 7% of the time, Pallas kernels for 1%

profile of v1, /device:TPU:1, one launch (start us, length us, event | category | flops | bytes accessed | tf_op | source)
XLA Modules:
  0.0 297.9 jit_solution(985315757735795335)
XLA Ops:
  0.7 4.1 %collective-permute-start.1 = (f32[128]{0:T(128)}, f32[128]{0:T(128)S(1)}, u32[]{:S(2)}, u32[]{:S(2)}) collective-permute-start(f32[128]{0:T(128)} %param.15), channel_id=1, source_target_pairs={{0,1},{1,2},{2,3},{3,0},{4,5},{5,6},{6,7},{7,4},{8,9},{9,10},{10,1... | collective-permute-start | bytes 1544 | tf_op jit(solution)/shard_map/ppermute | solution.py:24
  4.7 3.1 %collective-permute-start = (f32[400,128]{1,0:T(8,128)}, f32[400,128]{1,0:T(8,128)S(1)}, u32[]{:S(2)}, u32[]{:S(2)}) collective-permute-start(f32[400,128]{1,0:T(8,128)} %param.14), channel_id=1, source_target_pairs={{0,1},{1,2},{2,3},{3,0},{4,5},{5,6},{6,7},{7,4},{8,9},{9,10},{10,1... | collective-permute-start | bytes 614408 | tf_op jit(solution)/shard_map/ppermute | solution.py:24
  13.7 19.8 %all-to-all-start = ((f32[128,4,128]{2,1,0:T(4,128)}), f32[128,4,128]{2,1,0:T(4,128)S(1)}, u32[]{:S(2)}, u32[]{:S(2)}) async-start(f32[128,4,128]{2,1,0:T(4,128)} %copy.32), calls=%async_computation | async-start | bytes 524288 | tf_op jit(solution)/shard_map/all_to_all | solution.py:28
  36.0 12.7 %all-to-all-done.from_ref = f32[128,4,128]{2,1,0:T(4,128)S(1)} async-done(((f32[128,4,128]{2,1,0:T(4,128)}), f32[128,4,128]{2,1,0:T(4,128)S(1)}, u32[]{:S(2)}, u32[]{:S(2)}) %all-to-all-start) | async-done | bytes 262176 | tf_op jit(solution)/shard_map/all_to_all | solution.py:28
  51.3 6.5 %all-to-all-start.1 = ((f32[128,4,128]{2,1,0:T(4,128)}), f32[128,4,128]{2,1,0:T(4,128)}, u32[]{:S(2)}, u32[]{:S(2)}) async-start(f32[128,4,128]{2,1,0:T(4,128)} %shard_map.163), calls=%async_computation.1 | async-start | bytes 524288 | tf_op jit(solution)/shard_map/all_to_all | solution.py:28
  59.1 13.7 %all-to-all-done.1 = f32[128,4,128]{2,1,0:T(4,128)} async-done(((f32[128,4,128]{2,1,0:T(4,128)}), f32[128,4,128]{2,1,0:T(4,128)}, u32[]{:S(2)}, u32[]{:S(2)}) %all-to-all-start.1) | async-done | bytes 262176 | tf_op jit(solution)/shard_map/all_to_all | solution.py:28
  80.6 2.3 collective-permute-start.2
  86.1 12.8 %all_to_all.70 = f32[4,320,128]{2,1,0:T(8,128)S(1)} all-to-all(f32[4,320,128]{2,1,0:T(8,128)S(1)} %bitcast.94), channel_id=1, replica_groups=mesh['z'=8,'y'=8,'core'=2,'x'=4] {'x'}, dimensions={0} | all-to-all | bytes 1310720 | tf_op jit(solution)/shard_map/all_to_all | solution.py:28
  98.9 11.2 %all_to_all.71 = f32[8,40,128]{2,1,0:T(8,128)S(1)} all-to-all(f32[8,40,128]{2,1,0:T(8,128)S(1)} %bitcast.102), channel_id=1, replica_groups=mesh['z'=8,'y'=8,'core'=2,'x'=4] {'y'}, dimensions={0} | all-to-all | bytes 327680 | tf_op jit(solution)/shard_map/all_to_all | solution.py:28
  110.1 10.8 %all_to_all.72 = f32[8,40,128]{2,1,0:T(8,128)S(1)} all-to-all(f32[8,40,128]{2,1,0:T(8,128)S(1)} %broadcast_in_dim.25), channel_id=1, replica_groups=mesh['z'=8,'y'=8,'core'=2,'x'=4] {'z'}, dimensions={0} | all-to-all | bytes 327680 | tf_op jit(solution)/shard_map/all_to_all | solution.py:28
  121.6 3.4 %all-to-all-start.5 = ((f32[8,40,128]{2,1,0:T(8,128)}), f32[8,40,128]{2,1,0:T(8,128)S(1)}, u32[]{:S(2)}, u32[]{:S(2)}) async-start(f32[8,40,128]{2,1,0:T(8,128)} %broadcast_in_dim.26), calls=%async_computation.5 | async-start | bytes 327680 | tf_op jit(solution)/shard_map/all_to_all | solution.py:28
  126.6 6.6 %all-to-all-done.5 = f32[8,40,128]{2,1,0:T(8,128)S(1)} async-done(((f32[8,40,128]{2,1,0:T(8,128)}), f32[8,40,128]{2,1,0:T(8,128)S(1)}, u32[]{:S(2)}, u32[]{:S(2)}) %all-to-all-start.5) | async-done | bytes 163872 | tf_op jit(solution)/shard_map/all_to_all | solution.py:28
  134.1 3.5 %all-to-all-start.6 = ((f32[4,320,128]{2,1,0:T(8,128)}), f32[4,320,128]{2,1,0:T(8,128)S(1)}, u32[]{:S(2)}, u32[]{:S(2)}) async-start(f32[4,320,128]{2,1,0:T(8,128)} %broadcast_in_dim.28), calls=%async_computation.6 | async-start | bytes 1310720 | tf_op jit(solution)/shard_map/all_to_all | solution.py:28
  139.3 5.8 %all-to-all-done.6 = f32[4,320,128]{2,1,0:T(8,128)S(1)} async-done(((f32[4,320,128]{2,1,0:T(8,128)}), f32[4,320,128]{2,1,0:T(8,128)S(1)}, u32[]{:S(2)}, u32[]{:S(2)}) %all-to-all-start.6) | async-done | bytes 655392 | tf_op jit(solution)/shard_map/all_to_all | solution.py:28
  145.2 8.2 %collective-permute-start.3 = (f32[1280,128]{1,0:T(8,128)S(1)}, f32[1280,128]{1,0:T(8,128)S(1)}, u32[]{:S(2)}, u32[]{:S(2)}) collective-permute-start(f32[1280,128]{1,0:T(8,128)S(1)} %bitcast.96), channel_id=1, source_target_pairs={{0,4},{4,0},{1,5},{5,1},{2,6},{6,2},{3,7},{7,3},{8,12},{12,8},{9,1... | collective-permute-start | bytes 1966088 | tf_op jit(solution)/shard_map/ppermute | solution.py:24
  160.6 2.3 collective-permute-start.6
  165.5 4.3 %all-to-all-start.9 = ((f32[4,320,128]{2,1,0:T(8,128)}), f32[4,320,128]{2,1,0:T(8,128)}, u32[]{:S(2)}, u32[]{:S(2)}) async-start(f32[4,320,128]{2,1,0:T(8,128)} %bitcast.93), calls=%async_computation.9 | async-start | bytes 1310720 | tf_op jit(solution)/shard_map/all_to_all | solution.py:28
  171.7 8.8 %all-to-all-done.9 = f32[4,320,128]{2,1,0:T(8,128)} async-done(((f32[4,320,128]{2,1,0:T(8,128)}), f32[4,320,128]{2,1,0:T(8,128)}, u32[]{:S(2)}, u32[]{:S(2)}) %all-to-all-start.9) | async-done | bytes 655392 | tf_op jit(solution)/shard_map/all_to_all | solution.py:28
  182.2 3.4 %all-to-all-start.10 = ((f32[8,40,128]{2,1,0:T(8,128)}), f32[8,40,128]{2,1,0:T(8,128)S(1)}, u32[]{:S(2)}, u32[]{:S(2)}) async-start(f32[8,40,128]{2,1,0:T(8,128)} %bitcast.37), calls=%async_computation.10 | async-start | bytes 327680 | tf_op jit(solution)/shard_map/all_to_all | solution.py:28
  186.5 7.1 %all-to-all-done.10 = f32[8,40,128]{2,1,0:T(8,128)S(1)} async-done(((f32[8,40,128]{2,1,0:T(8,128)}), f32[8,40,128]{2,1,0:T(8,128)S(1)}, u32[]{:S(2)}, u32[]{:S(2)}) %all-to-all-start.10) | async-done | bytes 163872 | tf_op jit(solution)/shard_map/all_to_all | solution.py:28
  193.6 7.9 %all-to-all-start.7 = ((f32[128,4,128]{2,1,0:T(4,128)}), f32[128,4,128]{2,1,0:T(4,128)S(1)}, u32[]{:S(2)}, u32[]{:S(2)}) async-start(f32[128,4,128]{2,1,0:T(4,128)} %copy.34), calls=%async_computation.7 | async-start | bytes 524288 | tf_op jit(solution)/shard_map/all_to_all | solution.py:28
  201.5 15.3 %all-to-all-done.7.from_ref = f32[128,4,128]{2,1,0:T(4,128)S(1)} async-done(((f32[128,4,128]{2,1,0:T(4,128)}), f32[128,4,128]{2,1,0:T(4,128)S(1)}, u32[]{:S(2)}, u32[]{:S(2)}) %all-to-all-start.7) | async-done | bytes 262176 | tf_op jit(solution)/shard_map/all_to_all | solution.py:28
  217.5 3.4 %all-to-all-start.11 = ((f32[8,40,128]{2,1,0:T(8,128)}), f32[8,40,128]{2,1,0:T(8,128)S(1)}, u32[]{:S(2)}, u32[]{:S(2)}) async-start(f32[8,40,128]{2,1,0:T(8,128)} %broadcast_in_dim.29), calls=%async_computation.11 | async-start | bytes 327680 | tf_op jit(solution)/shard_map/all_to_all | solution.py:28
  222.8 7.2 %all-to-all-done.11 = f32[8,40,128]{2,1,0:T(8,128)S(1)} async-done(((f32[8,40,128]{2,1,0:T(8,128)}), f32[8,40,128]{2,1,0:T(8,128)S(1)}, u32[]{:S(2)}, u32[]{:S(2)}) %all-to-all-start.11) | async-done | bytes 163872 | tf_op jit(solution)/shard_map/all_to_all | solution.py:28
  230.0 6.7 %all-to-all-start.8 = ((f32[128,4,128]{2,1,0:T(4,128)}), f32[128,4,128]{2,1,0:T(4,128)S(1)}, u32[]{:S(2)}, u32[]{:S(2)}) async-start(f32[128,4,128]{2,1,0:T(4,128)} %shard_map.164), calls=%async_computation.8 | async-start | bytes 524288 | tf_op jit(solution)/shard_map/all_to_all | solution.py:28
  236.7 15.3 %all-to-all-done.8 = f32[128,4,128]{2,1,0:T(4,128)S(1)} async-done(((f32[128,4,128]{2,1,0:T(4,128)}), f32[128,4,128]{2,1,0:T(4,128)S(1)}, u32[]{:S(2)}, u32[]{:S(2)}) %all-to-all-start.8) | async-done | bytes 262176 | tf_op jit(solution)/shard_map/all_to_all | solution.py:28
  252.1 11.3 %all_to_all.73 = f32[8,40,128]{2,1,0:T(8,128)S(1)} all-to-all(f32[8,40,128]{2,1,0:T(8,128)S(1)} %broadcast_in_dim.30), channel_id=1, replica_groups=mesh['z'=8,'y'=8,'core'=2,'x'=4] {'y'}, dimensions={0} | all-to-all | bytes 327680 | tf_op jit(solution)/shard_map/all_to_all | solution.py:28
  264.3 3.6 %all-to-all-start.13 = ((f32[4,320,128]{2,1,0:T(8,128)}), f32[4,320,128]{2,1,0:T(8,128)S(1)}, u32[]{:S(2)}, u32[]{:S(2)}) async-start(f32[4,320,128]{2,1,0:T(8,128)} %broadcast_in_dim.32), calls=%async_computation.13 | async-start | bytes 1310720 | tf_op jit(solution)/shard_map/all_to_all | solution.py:28
  272.3 4.1 %all-to-all-done.13 = f32[4,320,128]{2,1,0:T(8,128)S(1)} async-done(((f32[4,320,128]{2,1,0:T(8,128)}), f32[4,320,128]{2,1,0:T(8,128)S(1)}, u32[]{:S(2)}, u32[]{:S(2)}) %all-to-all-start.13) | async-done | bytes 655392 | tf_op jit(solution)/shard_map/all_to_all | solution.py:28
  276.4 5.3 %collective-permute-start.7 = (f32[1280,128]{1,0:T(8,128)S(1)}, f32[1280,128]{1,0:T(8,128)S(1)}, u32[]{:S(2)}, u32[]{:S(2)}) collective-permute-start(f32[1280,128]{1,0:T(8,128)S(1)} %bitcast.95), channel_id=1, source_target_pairs={{0,4},{4,0},{1,5},{5,1},{2,6},{6,2},{3,7},{7,3},{8,12},{12,8},{9,1... | collective-permute-start | bytes 1966088 | tf_op jit(solution)/shard_map/ppermute | solution.py:24
  282.3 2.8 collective-permute-start.5
  289.8 4.6 %collective-permute-done.4 = f32[400,128]{1,0:T(8,128)S(1)} collective-permute-done((f32[400,128]{1,0:T(8,128)S(1)}, f32[400,128]{1,0:T(8,128)S(1)}, u32[]{:S(2)}, u32[]{:S(2)}) %collective-permute-start.4) | collective-permute-done | bytes 204832 | tf_op jit(solution)/shard_map/ppermute | solution.py:24
  (195 shorter events, 57.2 us)
Async XLA Ops:
  0.6 34.2 %copy-start.28 = (s32[1,1,1024]{2,1,0:T(1,128)S(1)}, s32[1,1,1024]{2,1,0:T(1,128)}, u32[]{:S(2)}) copy-start(s32[1,1,1024]{2,1,0:T(1,128)} %param.22) | copy-start | bytes 12292
  0.6 34.8 %copy-start = (f32[400,768]{1,0:T(8,128)S(1)}, f32[400,768]{1,0:T(8,128)}, u32[]{:S(2)}) copy-start(f32[400,768]{1,0:T(8,128)} %param.16) | copy-start | bytes 3686404
  0.7 10.7 %collective-permute-start.1 = (f32[128]{0:T(128)}, f32[128]{0:T(128)S(1)}, u32[]{:S(2)}, u32[]{:S(2)}) collective-permute-start(f32[128]{0:T(128)} %param.15), channel_id=1, source_target_pairs={{0,1},{1,2},{2,3},{3,0},{4,5},{5,6},{6,7},{7,4},{8,9},{9,10},{10,1... | collective-permute-start | bytes 1544 | tf_op jit(solution)/shard_map/ppermute | solution.py:24
  4.7 7.9 %collective-permute-start = (f32[400,128]{1,0:T(8,128)}, f32[400,128]{1,0:T(8,128)S(1)}, u32[]{:S(2)}, u32[]{:S(2)}) collective-permute-start(f32[400,128]{1,0:T(8,128)} %param.14), channel_id=1, source_target_pairs={{0,1},{1,2},{2,3},{3,0},{4,5},{5,6},{6,7},{7,4},{8,9},{9,10},{10,1... | collective-permute-start | bytes 614408 | tf_op jit(solution)/shard_map/ppermute | solution.py:24
  8.6 144.8 %copy-start.16 = (s32[1,1,512]{2,1,0:T(1,128)}, s32[1,1,512]{2,1,0:T(1,128)S(1)}, u32[]{:S(2)}) copy-start(s32[1,1,512]{2,1,0:T(1,128)S(1)} %get-tuple-element.39) | copy-start | bytes 6148
  13.7 35.1 %all-to-all-start = ((f32[128,4,128]{2,1,0:T(4,128)}), f32[128,4,128]{2,1,0:T(4,128)S(1)}, u32[]{:S(2)}, u32[]{:S(2)}) async-start(f32[128,4,128]{2,1,0:T(4,128)} %copy.32), calls=%async_computation | async-start | bytes 524288 | tf_op jit(solution)/shard_map/all_to_all | solution.py:28
  36.0 21.9 %copy-start.6 = (f32[400,128]{1,0:T(8,128)S(1)}, f32[400,128]{1,0:T(8,128)}, u32[]{:S(2)}) copy-start(f32[400,128]{1,0:T(8,128)} %param.12) | copy-start | bytes 614404
  51.3 21.6 %all-to-all-start.1 = ((f32[128,4,128]{2,1,0:T(4,128)}), f32[128,4,128]{2,1,0:T(4,128)}, u32[]{:S(2)}, u32[]{:S(2)}) async-start(f32[128,4,128]{2,1,0:T(4,128)} %shard_map.163), calls=%async_computation.1 | async-start | bytes 524288 | tf_op jit(solution)/shard_map/all_to_all | solution.py:28
  80.6 4.3 %collective-permute-start.2 = (f32[1280,128]{1,0:T(8,128)}, f32[1280,128]{1,0:T(8,128)}, u32[]{:S(2)}, u32[]{:S(2)}) collective-permute-start(f32[1280,128]{1,0:T(8,128)} %dynamic-slice_bitcast_fusion.1), channel_id=1, source_target_pairs={{0,4},{4,0},{1,5},{5,1},{2,6},{6,2},{3,7},{7,3},{8,12},{12,8},{9,1... | collective-permute-start | bytes 1966088 | tf_op jit(solution)/shard_map/ppermute | solution.py:24
  98.9 26.7 %copy-start.2 = (f32[200,512]{1,0:T(8,128)S(1)}, f32[200,512]{1,0:T(8,128)}, u32[]{:S(2)}) copy-start(f32[200,512]{1,0:T(8,128)} %get-tuple-element.21) | copy-start | bytes 1228804
  98.9 26.7 %copy-start.19 = (s32[1,1,512]{2,1,0:T(1,128)S(1)}, s32[1,1,512]{2,1,0:T(1,128)}, u32[]{:S(2)}) copy-start(s32[1,1,512]{2,1,0:T(1,128)} %get-tuple-element.44) | copy-start | bytes 6148
  98.9 26.7 %copy-start.21 = (f32[512]{0:T(512)S(1)}, f32[512]{0:T(512)}, u32[]{:S(2)}) copy-start(f32[512]{0:T(512)} %copy-done.20) | copy-start | bytes 6148
  121.6 11.6 %all-to-all-start.5 = ((f32[8,40,128]{2,1,0:T(8,128)}), f32[8,40,128]{2,1,0:T(8,128)S(1)}, u32[]{:S(2)}, u32[]{:S(2)}) async-start(f32[8,40,128]{2,1,0:T(8,128)} %broadcast_in_dim.26), calls=%async_computation.5 | async-start | bytes 327680 | tf_op jit(solution)/shard_map/all_to_all | solution.py:28
  134.1 11.1 %all-to-all-start.6 = ((f32[4,320,128]{2,1,0:T(8,128)}), f32[4,320,128]{2,1,0:T(8,128)S(1)}, u32[]{:S(2)}, u32[]{:S(2)}) async-start(f32[4,320,128]{2,1,0:T(8,128)} %broadcast_in_dim.28), calls=%async_computation.6 | async-start | bytes 1310720 | tf_op jit(solution)/shard_map/all_to_all | solution.py:28
  137.6 15.7 %copy-start.37 = (f32[128]{0:T(128)S(1)}, f32[128]{0:T(128)}, u32[]{:S(2)}) copy-start(f32[128]{0:T(128)} %param.13) | copy-start | bytes 1540
  137.6 15.8 %copy-start.7 = (f32[400,128]{1,0:T(8,128)S(1)}, f32[400,128]{1,0:T(8,128)}, u32[]{:S(2)}) copy-start(f32[400,128]{1,0:T(8,128)} %param.12) | copy-start | bytes 614404
  139.3 15.6 %copy-start.11 = (f32[400,128]{1,0:T(8,128)}, f32[400,128]{1,0:T(8,128)S(1)}, u32[]{:S(2)}) copy-start(f32[400,128]{1,0:T(8,128)S(1)} %get-tuple-element.51) | copy-start | bytes 614404
  139.3 15.7 %copy-start.39 = (f32[128]{0:T(128)}, f32[128]{0:T(128)S(1)}, u32[]{:S(2)}) copy-start(f32[128]{0:T(128)S(1)} %get-tuple-element.50) | copy-start | bytes 1540
  145.2 9.7 %collective-permute-start.3 = (f32[1280,128]{1,0:T(8,128)S(1)}, f32[1280,128]{1,0:T(8,128)S(1)}, u32[]{:S(2)}, u32[]{:S(2)}) collective-permute-start(f32[1280,128]{1,0:T(8,128)S(1)} %bitcast.96), channel_id=1, source_target_pairs={{0,4},{4,0},{1,5},{5,1},{2,6},{6,2},{3,7},{7,3},{8,12},{12,8},{9,1... | collective-permute-start | bytes 1966088 | tf_op jit(solution)/shard_map/ppermute | solution.py:24
  160.6 4.0 %collective-permute-start.6 = (f32[1280,128]{1,0:T(8,128)S(1)}, f32[1280,128]{1,0:T(8,128)S(1)}, u32[]{:S(2)}, u32[]{:S(2)}) collective-permute-start(f32[1280,128]{1,0:T(8,128)S(1)} %dynamic-slice_bitcast_fusion), channel_id=1, source_target_pairs={{0,4},{4,0},{1,5},{5,1},{2,6},{6,2},{3,7},{7,3},{8,12},{12,8},{9,1... | collective-permute-start | bytes 1966088 | tf_op jit(solution)/shard_map/ppermute | solution.py:24
  165.5 15.0 %all-to-all-start.9 = ((f32[4,320,128]{2,1,0:T(8,128)}), f32[4,320,128]{2,1,0:T(8,128)}, u32[]{:S(2)}, u32[]{:S(2)}) async-start(f32[4,320,128]{2,1,0:T(8,128)} %bitcast.93), calls=%async_computation.9 | async-start | bytes 1310720 | tf_op jit(solution)/shard_map/all_to_all | solution.py:28
  182.2 11.4 %all-to-all-start.10 = ((f32[8,40,128]{2,1,0:T(8,128)}), f32[8,40,128]{2,1,0:T(8,128)S(1)}, u32[]{:S(2)}, u32[]{:S(2)}) async-start(f32[8,40,128]{2,1,0:T(8,128)} %bitcast.37), calls=%async_computation.10 | async-start | bytes 327680 | tf_op jit(solution)/shard_map/all_to_all | solution.py:28
  193.6 23.2 %all-to-all-start.7 = ((f32[128,4,128]{2,1,0:T(4,128)}), f32[128,4,128]{2,1,0:T(4,128)S(1)}, u32[]{:S(2)}, u32[]{:S(2)}) async-start(f32[128,4,128]{2,1,0:T(4,128)} %copy.34), calls=%async_computation.7 | async-start | bytes 524288 | tf_op jit(solution)/shard_map/all_to_all | solution.py:28
  217.5 12.4 %all-to-all-start.11 = ((f32[8,40,128]{2,1,0:T(8,128)}), f32[8,40,128]{2,1,0:T(8,128)S(1)}, u32[]{:S(2)}, u32[]{:S(2)}) async-start(f32[8,40,128]{2,1,0:T(8,128)} %broadcast_in_dim.29), calls=%async_computation.11 | async-start | bytes 327680 | tf_op jit(solution)/shard_map/all_to_all | solution.py:28
  230.0 22.1 %all-to-all-start.8 = ((f32[128,4,128]{2,1,0:T(4,128)}), f32[128,4,128]{2,1,0:T(4,128)S(1)}, u32[]{:S(2)}, u32[]{:S(2)}) async-start(f32[128,4,128]{2,1,0:T(4,128)} %shard_map.164), calls=%async_computation.8 | async-start | bytes 524288 | tf_op jit(solution)/shard_map/all_to_all | solution.py:28
  252.1 15.9 %copy-start.17 = (s32[1,1,512]{2,1,0:T(1,128)S(1)}, s32[1,1,512]{2,1,0:T(1,128)}, u32[]{:S(2)}) copy-start(s32[1,1,512]{2,1,0:T(1,128)} %copy-done.16) | copy-start | bytes 6148
  264.3 12.1 %all-to-all-start.13 = ((f32[4,320,128]{2,1,0:T(8,128)}), f32[4,320,128]{2,1,0:T(8,128)S(1)}, u32[]{:S(2)}, u32[]{:S(2)}) async-start(f32[4,320,128]{2,1,0:T(8,128)} %broadcast_in_dim.32), calls=%async_computation.13 | async-start | bytes 1310720 | tf_op jit(solution)/shard_map/all_to_all | solution.py:28
  267.9 20.1 %copy-start.8 = (f32[400,128]{1,0:T(8,128)S(1)}, f32[400,128]{1,0:T(8,128)}, u32[]{:S(2)}) copy-start(f32[400,128]{1,0:T(8,128)} %param.12) | copy-start | bytes 614404
  268.0 20.1 %copy-start.30 = (f32[128]{0:T(128)S(1)}, f32[128]{0:T(128)}, u32[]{:S(2)}) copy-start(f32[128]{0:T(128)} %copy-done.29) | copy-start | bytes 1540
  276.4 18.0 %collective-permute-start.7 = (f32[1280,128]{1,0:T(8,128)S(1)}, f32[1280,128]{1,0:T(8,128)S(1)}, u32[]{:S(2)}, u32[]{:S(2)}) collective-permute-start(f32[1280,128]{1,0:T(8,128)S(1)} %bitcast.95), channel_id=1, source_target_pairs={{0,4},{4,0},{1,5},{5,1},{2,6},{6,2},{3,7},{7,3},{8,12},{12,8},{9,1... | collective-permute-start | bytes 1966088 | tf_op jit(solution)/shard_map/ppermute | solution.py:24
  282.3 7.4 %collective-permute-start.5 = (f32[128]{0:T(128)S(1)}, f32[128]{0:T(128)S(1)}, u32[]{:S(2)}, u32[]{:S(2)}) collective-permute-start(f32[128]{0:T(128)S(1)} %slice_bitcast_fusion.1), channel_id=1, source_target_pairs={{0,3},{1,0},{2,1},{3,2},{4,7},{5,4},{6,5},{7,6},{8,11},{9,8},{10,9... | collective-permute-start | bytes 1544 | tf_op jit(solution)/shard_map/ppermute | solution.py:24
  286.1 8.3 %collective-permute-start.4 = (f32[400,128]{1,0:T(8,128)S(1)}, f32[400,128]{1,0:T(8,128)S(1)}, u32[]{:S(2)}, u32[]{:S(2)}) collective-permute-start(f32[400,128]{1,0:T(8,128)S(1)} %slice_bitcast_fusion), channel_id=1, source_target_pairs={{0,3},{1,0},{2,1},{3,2},{4,7},{5,4},{6,5},{7,6},{8,11},{9,8},{10,9... | collective-permute-start | bytes 614408 | tf_op jit(solution)/shard_map/ppermute | solution.py:24
  (27 other events, 145.0 us)

commit v2 on v0

v2 whole, which is shorter than its diff:
```python
import jax
import jax.numpy as jnp
from jax import lax
from jax.experimental import pallas as pl
from jax.experimental.pallas import tpu as pltpu
from jax.sharding import Mesh
from jax.sharding import PartitionSpec as P

DIM = 400
HALF = 200
NREL = 768
BLOCK = 128
SPAN = 512
NEG = 1024
LANES = 128
CHUNKS = NREL // LANES
FLAT = 2560
HALF_FLAT = FLAT // 2
PIECE = 4

ALL = ("z", "y", "core", "x")
DOM = ("z", "y", "core")

learn_rate = 0.3
epsilon = 1e-08

f32 = jnp.float32
bf16 = jnp.bfloat16


def passed_along(value, axis, steps):
    count = lax.axis_size(axis)
    pairs = [(source, (source + steps) % count) for source in range(count)]
    return lax.ppermute(value, axis, pairs)


def exchange(value, axis):
    return lax.all_to_all(value, axis, split_axis=0, concat_axis=0, tiled=True)


def dealt(value, axis, count):
    rows, lanes = value.shape
    return exchange(value.reshape(count, rows // count, lanes), axis).reshape(rows, lanes)


def gathered(value, axis):
    count = lax.axis_size(axis)
    return exchange(jnp.broadcast_to(value[None], (count,) + value.shape), axis)


def kernel_call(body, outs, args, scratch=(), scalars=0):
    specs = [pl.BlockSpec(memory_space=pltpu.SMEM)] * scalars
    specs += [pl.BlockSpec(memory_space=pltpu.VMEM)] * (len(args) - scalars)
    return pl.pallas_call(
        body,
        out_shape=[jax.ShapeDtypeStruct(shape, dtype) for shape, dtype in outs],
        in_specs=specs,
        out_specs=[pl.BlockSpec(memory_space=pltpu.VMEM)] * len(outs),
        scratch_shapes=[pltpu.VMEM(shape, dtype) for shape, dtype in scratch],
        compiler_params=pltpu.CompilerParams(vmem_limit_bytes=40 * 2**20),
    )(*args)


def dot(left, right):
    return lax.dot_general(left, right, (((1,), (0,)), ((), ())), preferred_element_type=f32)


def dot_last(left, right):
    return lax.dot_general(left, right, (((1,), (1,)), ((), ())), preferred_element_type=f32)


def moved(pick, value):
    upper = value.astype(bf16)
    rest = value - upper.astype(f32)
    middle = rest.astype(bf16)
    lower = (rest - middle.astype(f32)).astype(bf16)
    return (dot(pick, upper) + dot(pick, middle)) + dot(pick, lower)


def one_hot(count, rows):
    hit = lax.broadcasted_iota(jnp.int32, (count, rows.shape[1]), 0) == rows
    return jnp.where(hit, 1.0, 0.0).astype(bf16)


def sigmoid(value):
    return 1.0 / (1.0 + jnp.exp(-value))


def stepped(param, state, grad):
    new_state = state + jnp.sum(grad * grad, axis=0, keepdims=True) * (1.0 / DIM)
    return (param - learn_rate * grad / (jnp.sqrt(new_state) + epsilon), new_state)


def spaced(start, size, stride):
    return pl.ds(start, size, stride=stride)


def pack_body(partner_ref, arriving_ref, state_ref, out_ref):
    for k in range(PIECE - 1):
        out_ref[spaced(k, BLOCK, PIECE), :] = arriving_ref[LANES * k : LANES * (k + 1), :].T
    tail = arriving_ref[LANES * (PIECE - 1) : DIM, :]
    state = jnp.broadcast_to(state_ref[...], (8, LANES))
    own = jnp.full((8, LANES), partner_ref[0, 0].astype(f32))
    zero = jnp.zeros((LANES - tail.shape[0] - 16, LANES), f32)
    out_ref[spaced(PIECE - 1, BLOCK, PIECE), :] = jnp.concatenate([tail, state, own, zero], 0).T


STATE_LANE = DIM - LANES * (PIECE - 1)
OWN_LANE = STATE_LANE + 8


def partner_pick(last):
    own = last[:, OWN_LANE : OWN_LANE + 1].astype(jnp.int32)
    lane = lax.broadcasted_iota(jnp.int32, (BLOCK, BLOCK), 1)
    return jnp.where(lane == own, 1.0, 0.0)


def pick_body(spread_ref, out_ref):
    last = spread_ref[spaced(PIECE - 1, BLOCK, PIECE), :]
    pick = partner_pick(last).astype(bf16)
    for k in range(PIECE - 1):
        rows = spaced(k, BLOCK, PIECE)
        out_ref[rows, :] = moved(pick, spread_ref[rows, :])
    out_ref[spaced(PIECE - 1, BLOCK, PIECE), :] = moved(pick, last)


def train(
    first,
    live_count,
    source,
    source_state,
    target,
    target_state,
    relation_bf,
    rows_s,
    rows_t,
    rows_r,
    rows_n,
    subject_ref,
    operator_ref,
    objects_ref,
    query_ref,
    slope_ref,
    flat_ref,
):
    pick_s = one_hot(BLOCK, rows_s)
    pick_t = one_hot(BLOCK, rows_t)
    pick_r = one_hot(NREL, rows_r)
    hits = lax.broadcasted_iota(jnp.int32, (BLOCK, NEG), 0) == rows_n
    count = jnp.sum(jnp.where(hits, 1.0, 0.0), axis=1, keepdims=True)
    count_row = jnp.broadcast_to(count, (BLOCK, BLOCK)).T[0:1, :]
    edge = lax.broadcasted_iota(jnp.int32, (1, SPAN), 1) + first
    live = jnp.where(edge < live_count, 1.0, 0.0)
    target_bf = target.astype(bf16)
    subject_ref[...] = dot(source.astype(bf16), pick_s)
    operator_ref[...] = dot(relation_bf, pick_r)
    objects_ref[...] = dot(target_bf, pick_t)

    def form(i, total):
        re = pl.ds(pl.multiple_of(8 * i, 8), 8)
        im = pl.ds(pl.multiple_of(HALF + 8 * i, 8), 8)
        subject_re, subject_im = (subject_ref[re, :], subject_ref[im, :])
        operator_re, operator_im = (operator_ref[re, :], operator_ref[im, :])
        query_re = subject_re * operator_re - subject_im * operator_im
        query_im = subject_re * operator_im + subject_im * operator_re
        query_ref[re, :] = query_re
        query_ref[im, :] = query_im
        return total + query_re * objects_ref[re, :] + query_im * objects_ref[im, :]

    total = lax.fori_loop(0, HALF // 8, form, jnp.zeros((8, SPAN), f32), unroll=5)
    positive = jnp.sum(total, axis=0, keepdims=True)
    query_bf = query_ref[...].astype(bf16)
    score = dot(target.T.astype(bf16), query_bf)
    grad_pos = -sigmoid(-positive) * live
    slope = (sigmoid(score) * (live * (1.0 / NEG))).astype(bf16)
    weighted = slope.astype(f32) * count
    upper = weighted.astype(bf16)
    lower = (weighted - upper.astype(f32)).astype(bf16)
    slope_ref[...] = dot(target_bf, upper) + dot(target_bf, lower)
    grad_noise = dot_last(query_bf, slope)

    def push(i, _):
        re = pl.ds(pl.multiple_of(8 * i, 8), 8)
        im = pl.ds(pl.multiple_of(HALF + 8 * i, 8), 8)
        query_gre = grad_pos * objects_ref[re, :] + slope_ref[re, :]
        query_gim = grad_pos * objects_ref[im, :] + slope_ref[im, :]
        subject_re, subject_im = (subject_ref[re, :], subject_ref[im, :])
        operator_re, operator_im = (operator_ref[re, :], operator_ref[im, :])
        subject_ref[re, :] = query_gre * operator_re + query_gim * operator_im
        subject_ref[im, :] = query_gim * operator_re - query_gre * operator_im
        operator_ref[re, :] = query_gre * subject_re + query_gim * subject_im
        operator_ref[im, :] = query_gim * subject_re - query_gre * subject_im
        query_ref[re, :] = grad_pos * query_ref[re, :]
        query_ref[im, :] = grad_pos * query_ref[im, :]
        return 0

    lax.fori_loop(0, HALF // 8, push, 0, unroll=5)
    grad_operator = operator_ref[...].astype(bf16)
    for k in range(0, CHUNKS, 2):
        pair = dot_last(grad_operator, pick_r[LANES * k : LANES * (k + 2), :])
        flat_ref[DIM * k : DIM * (k + 1), :] = pair[:, :LANES]
        flat_ref[DIM * (k + 1) : DIM * (k + 2), :] = pair[:, LANES:]
    flat_ref[DIM * CHUNKS : FLAT, :] = jnp.zeros((FLAT - DIM * CHUNKS, LANES), f32)
    grad_source = dot_last(subject_ref[...].astype(bf16), pick_s)
    grad_target = dot_last(query_ref[...].astype(bf16), pick_t)
    grad_target = grad_target + grad_noise.astype(bf16).astype(f32) * count_row
    source, source_state = stepped(source, source_state, grad_source)
    target, target_state = stepped(target, target_state, grad_target)
    return source, source_state, target, target_state


TRAIN_SCRATCH = [((DIM, SPAN), f32)] * 5 + [((FLAT, LANES), f32)]


def halves(mine, flat_ref, keep_ref, give_ref):
    keep_ref[0:HALF_FLAT, :] = flat_ref[pl.ds(pl.multiple_of(mine * HALF_FLAT, 8), HALF_FLAT), :]
    give_ref[0:HALF_FLAT, :] = flat_ref[
        pl.ds(pl.multiple_of((1 - mine) * HALF_FLAT, 8), HALF_FLAT), :
    ]


def first_body(
    mine_ref,
    live_ref,
    arrived_ref,
    source_ref,
    source_state_ref,
    relations_ref,
    rows_s_ref,
    rows_t_ref,
    rows_r_ref,
    rows_n_ref,
    source_out,
    source_state_out,
    target_out,
    target_state_out,
    keep_out,
    give_out,
    subject_ref,
    operator_ref,
    objects_ref,
    query_ref,
    slope_ref,
    flat_ref,
):
    last = arrived_ref[spaced(PIECE - 1, BLOCK, PIECE), :].T
    target = jnp.concatenate(
        [arrived_ref[spaced(k, BLOCK, PIECE), :].T for k in range(PIECE - 1)] + [last[:STATE_LANE, :]], 0
    )
    source, source_state, target, target_state = train(
        0,
        live_ref[0, 0],
        source_ref[...],
        source_state_ref[...],
        target,
        last[STATE_LANE : STATE_LANE + 1, :],
        relations_ref[...].astype(bf16),
        rows_s_ref[:, 0:SPAN],
        rows_t_ref[:, 0:SPAN],
        rows_r_ref[:, 0:SPAN],
        rows_n_ref[:, 0:NEG],
        subject_ref,
        operator_ref,
        objects_ref,
        query_ref,
        slope_ref,
        flat_ref,
    )
    source_out[...] = source
    source_state_out[...] = source_state
    target_out[...] = target
    target_state_out[...] = target_state
    halves(mine_ref[0, 0], flat_ref, keep_out, give_out)


def relation_update(mine, part_ref, other_ref, relations_ref, state_ref, out, state_out, flat_ref):
    flat_ref[pl.ds(pl.multiple_of(mine * HALF_FLAT, 8), HALF_FLAT), :] = part_ref[...]
    flat_ref[pl.ds(pl.multiple_of((1 - mine) * HALF_FLAT, 8), HALF_FLAT), :] = other_ref[...]
    for k in range(CHUNKS):
        lanes = slice(LANES * k, LANES * (k + 1))
        grad = flat_ref[DIM * k : DIM * (k + 1), :]
        new, new_state = stepped(relations_ref[:, lanes], state_ref[:, lanes], grad)
        out[:, lanes] = new
        state_out[:, lanes] = new_state


def second_body(
    mine_ref,
    live_ref,
    partner_ref,
    part_ref,
    other_ref,
    source_ref,
    source_state_ref,
    target_ref,
    target_state_ref,
    relations_ref,
    relation_state_ref,
    rows_s_ref,
    rows_t_ref,
    rows_r_ref,
    rows_n_ref,
    source_out,
    source_state_out,
    relations_out,
    relation_state_out,
    keep_out,
    give_out,
    subject_ref,
    operator_ref,
    objects_ref,
    query_ref,
    slope_ref,
    flat_ref,
    turned_ref,
):
    mine = mine_ref[0, 0]
    relation_update(
        mine,
        part_ref,
        other_ref,
        relations_ref,
        relation_state_ref,
        relations_out,
        relation_state_out,
        flat_ref,
    )
    source, source_state, target, target_state = train(
        SPAN,
        live_ref[0, 0],
        source_ref[...],
        source_state_ref[...],
        target_ref[...],
        target_state_ref[...],
        relations_out[...].astype(bf16),
        rows_s_ref[:, SPAN : 2 * SPAN],
        rows_t_ref[:, SPAN : 2 * SPAN],
        rows_r_ref[:, SPAN : 2 * SPAN],
        rows_n_ref[:, NEG : 2 * NEG],
        subject_ref,
        operator_ref,
        objects_ref,
        query_ref,
        slope_ref,
        flat_ref,
    )
    source_out[...] = source
    source_state_out[...] = source_state
    halves(mine, flat_ref, keep_out, give_out)
    for k in range(PIECE):
        if k < PIECE - 1:
            turned_ref[...] = target[LANES * k : LANES * (k + 1), :].T
        else:
            state = jnp.broadcast_to(target_state, (8, LANES))
            own = jnp.full((8, LANES), partner_ref[0, 0].astype(f32))
            zero = jnp.zeros((LANES - STATE_LANE - 16, LANES), f32)
            turned_ref[...] = jnp.concatenate([target[LANES * k : DIM, :], state, own, zero], 0).T
        rows = slice(HALF_FLAT + 64 * k, HALF_FLAT + 64 * (k + 1))
        keep_out[rows, :] = turned_ref[pl.ds(mine, 64, stride=2), :]
        give_out[rows, :] = turned_ref[pl.ds(1 - mine, 64, stride=2), :]


ROWS = 16
SUM_ROW = 8
SUM_ROWS = 5


def join_body(keep_ref, got_ref, sums_ref, block_ref):
    sums_ref[...] = keep_ref[0:HALF_FLAT, :] + got_ref[0:HALF_FLAT, :]
    block_ref[0 : 64 * PIECE, :] = keep_ref[HALF_FLAT:, :]
    block_ref[64 * PIECE :, :] = got_ref[HALF_FLAT:, :]


def merge_body(received_ref, block_ref, out_ref):
    for k in range(2 * PIECE):
        out_ref[spaced(k, 64, ROWS), :] = block_ref[64 * k : 64 * (k + 1), :]
    for k in range(SUM_ROWS):
        rows = slice(64 * k, 64 * (k + 1))
        total = received_ref[0, rows, :] + received_ref[1, rows, :]
        total = total + received_ref[2, rows, :] + received_ref[3, rows, :]
        out_ref[spaced(SUM_ROW + k, 64, ROWS), :] = total
    for k in range(SUM_ROW + SUM_ROWS, ROWS):
        out_ref[spaced(k, 64, ROWS), :] = jnp.zeros((64, LANES), f32)


def middle_body(mine_ref, received_ref, out_ref, turned_ref):
    mine = mine_ref[0, 0]
    here, there = (spaced(mine, 64, 2), spaced(1 - mine, 64, 2))
    back = None
    for k in reversed(range(PIECE)):
        turned_ref[here, :] = received_ref[spaced(k, 64, ROWS), :]
        turned_ref[there, :] = received_ref[spaced(PIECE + k, 64, ROWS), :]
        if back is None:
            back = partner_pick(turned_ref[...]).T.astype(bf16)
        turned_ref[...] = moved(back, turned_ref[...])
        out_ref[spaced(k, 64, ROWS), :] = turned_ref[here, :]
        out_ref[spaced(PIECE + k, 64, ROWS), :] = turned_ref[there, :]
    total = received_ref[SUM_ROW:ROWS, :]
    for q in range(1, 64):
        total = total + received_ref[ROWS * q + SUM_ROW : ROWS * (q + 1), :]
    for q in range(64):
        out_ref[ROWS * q + SUM_ROW : ROWS * (q + 1), :] = total


def parting_body(received_ref, sums_ref, block_ref):
    for k in range(2 * PIECE):
        block_ref[64 * k : 64 * (k + 1), :] = received_ref[spaced(k, 64, ROWS), :]
    for k in range(SUM_ROWS):
        rows = received_ref[spaced(SUM_ROW + k, 64, ROWS), :]
        for x in range(4):
            sums_ref[x, 64 * k : 64 * (k + 1), :] = rows


def settle_body(mine_ref, block_ref, other_ref, out_ref, state_out, turned_ref):
    mine = mine_ref[0, 0]
    for k in range(PIECE):
        rows = slice(64 * k, 64 * (k + 1))
        turned_ref[pl.ds(mine, 64, stride=2), :] = block_ref[rows, :]
        turned_ref[pl.ds(1 - mine, 64, stride=2), :] = other_ref[rows, :]
        turned = turned_ref[...].T
        if k < PIECE - 1:
            out_ref[LANES * k : LANES * (k + 1), :] = turned
        else:
            out_ref[LANES * k : DIM, :] = turned[:STATE_LANE, :]
            state_out[...] = turned[STATE_LANE : STATE_LANE + 1, :]


def final_body(
    mine_ref, part_ref, other_ref, relations_ref, state_ref, out_ref, state_out, flat_ref
):
    relation_update(
        mine_ref[0, 0], part_ref, other_ref, relations_ref, state_ref, out_ref, state_out, flat_ref
    )


def local(
    source_emb,
    source_state,
    dest_emb,
    dest_state,
    relations,
    relation_state,
    partner,
    edge_count,
    source_rows,
    target_rows,
    relation_index,
    negative_rows,
):
    mine = lax.axis_index("core").astype(jnp.int32).reshape(1, 1)
    turned = ((BLOCK, LANES), f32)
    arriving = passed_along(dest_emb, "x", 1)
    arriving_state = passed_along(dest_state.reshape(1, BLOCK), "x", 1)
    tile = ((BLOCK * PIECE, LANES), f32)
    (cargo,) = kernel_call(pack_body, [tile], [partner, arriving, arriving_state], scalars=1)
    spread = dealt(cargo, DOM, BLOCK)
    (spread,) = kernel_call(pick_body, [tile], [spread])
    arrived = dealt(spread, DOM, BLOCK)
    lists = [
        rows.reshape(1, -1) for rows in (source_rows, target_rows, relation_index, negative_rows)
    ]
    block = ((DIM, BLOCK), f32)
    line = ((1, BLOCK), f32)
    half = ((HALF_FLAT, LANES), f32)
    source, source_acc, target, target_acc, keep, give = kernel_call(
        first_body,
        [block, line, block, line, half, half],
        [mine, edge_count, arrived, source_emb, source_state.reshape(1, -1), relations] + lists,
        TRAIN_SCRATCH,
        scalars=2,
    )
    part = keep + passed_along(give, "core", 1)
    part = jnp.sum(exchange(part.reshape(4, 320, LANES), "x"), 0)
    part = jnp.sum(exchange(part.reshape(8, 40, LANES), "y"), 0)
    part = jnp.sum(gathered(part, "z"), 0)
    part = gathered(part, "y").reshape(320, LANES)
    part = gathered(part, "x").reshape(HALF_FLAT, LANES)
    other = passed_along(part, "core", 1)
    table = ((DIM, NREL), f32)
    types = ((1, NREL), f32)
    longer = ((HALF_FLAT + 64 * PIECE, LANES), f32)
    source, source_acc, relations, relation_acc, keep, give = kernel_call(
        second_body,
        [block, line, table, types, longer, longer],
        [mine, edge_count, partner, part, other, source, source_acc, target, target_acc, relations]
        + [relation_state.reshape(1, -1)]
        + lists,
        TRAIN_SCRATCH + [turned],
        scalars=3,
    )
    got = passed_along(give, "core", 1)
    part, leaving = kernel_call(join_body, [half, ((128 * PIECE, LANES), f32)], [keep, got])
    leaving = passed_along(leaving, "x", -1)
    received = exchange(part.reshape(4, 320, LANES), "x")
    packet = ((64 * ROWS, LANES), f32)
    (packed,) = kernel_call(merge_body, [packet], [received, leaving])
    packed = dealt(packed, ("z", "y"), 64)
    (packed,) = kernel_call(middle_body, [packet], [mine, packed], [turned], scalars=1)
    packed = dealt(packed, ("z", "y"), 64)
    sums, returned = kernel_call(
        parting_body, [((4, 320, LANES), f32), ((128 * PIECE, LANES), f32)], [packed]
    )
    sibling = passed_along(returned[64 * PIECE :], "core", 1)
    part = exchange(sums, "x").reshape(HALF_FLAT, LANES)
    other = passed_along(part, "core", 1)
    settled, settled_acc = kernel_call(
        settle_body, [block, line], [mine, returned, sibling], [turned], scalars=1
    )
    relations, relation_acc = kernel_call(
        final_body,
        [table, types],
        [mine, part, other, relations, relation_acc],
        [((FLAT, LANES), f32)],
        scalars=1,
    )
    return (
        source,
        source_acc.reshape(-1),
        settled,
        settled_acc.reshape(-1),
        relations,
        relation_acc.reshape(-1),
    )


def solution(mesh):
    fine = Mesh(mesh.devices.reshape(8, 8, 2, 4), ALL)
    in_specs = (
        P(None, ALL),
        P(ALL),
        P(None, ALL),
        P(ALL),
        P(),
        P(),
        P(DOM, "x"),
        P(DOM, "x"),
        P(DOM, "x", None),
        P(DOM, "x", None),
        P(DOM, "x", None),
        P(DOM, "x", None),
    )
    out_specs = (P(None, ALL), P(ALL), P(None, ALL), P(ALL), P(), P())
    return jax.shard_map(local, mesh=fine, in_specs=in_specs, out_specs=out_specs, check_vma=False)
```

time: 706 us -> 238 us (0.34)
  waiting for transfers between devices: 564 us -> 33.4 us
  blocking collectives: 27.5 us -> 143 us
  matrix products: 27.9 us -> 0 us
  local copies, waits for them, and re-layouts: 17.5 us -> 0.12 us
  between operations: 15.8 us -> 2.22 us
  Pallas kernels: 0 us -> 13.1 us
  other arithmetic: 11.5 us -> 0.73 us
    psum x2 -> x0, waiting for transfers between devices: 522 us -> none  [relation_step(): total = lax.psum(grad_local, ('dom', 'grp'))]
    all_to_all x0 -> x9, blocking collectives: none -> 143 us  [exchange(): return lax.all_to_all(value, axis, split_axis=0, concat_axis=0, tiled=True)]
    dot_general x20 -> x0, matrix products: 27.9 us -> none  [the longest x10 17.3 us: contract_last(): lax.dot_general(left, right, (((1,), (1,)), ((), ())), preferred_element_...]
    ppermute x2 -> x8, starting transfers between devices: 7.07 us -> 34.9 us  [passed_along(): return lax.ppermute(value, axis, pairs)]
    all_gather x1 -> x0, blocking collectives: 27.5 us -> none  [local(): partners = lax.all_gather(partner[0], 'dom', axis=0, tiled=True)]
    all_to_all x4 -> x2, waiting for transfers between devices: 39.6 us -> 14.7 us  [exchange(): return lax.all_to_all(value, axis, split_axis=0, concat_axis=0, tiled=True)]
    all_to_all x4 -> x2, starting transfers between devices: 32.9 us -> 9.02 us  [exchange(): return lax.all_to_all(value, axis, split_axis=0, concat_axis=0, tiled=True)]
    ppermute x2 -> x8, waiting for transfers between devices: 2.93 us -> 18.7 us  [passed_along(): return lax.ppermute(value, axis, pairs)]
  transfers between devices with their start and end apart: 8 -> 10, of which waited for: 6 -> 7; matrix products, arithmetic and copies ran while one was open for 3% -> 0% of each run, Pallas kernels for 0% -> 0%
where the time goes in v2:
time: 238 us; the launch traced here: 237 us
  blocking collectives  143 us (60%)
  starting transfers between devices  43.9 us (18%)
  waiting for transfers between devices  33.4 us (14%)
  Pallas kernels  13.1 us (6%)
    all_to_all x9, blocking collectives, exchange(): return lax.all_to_all(value, axis, split_axis=0, concat_axis=0, tiled=True)  143 us
    ppermute x8, starting transfers between devices, passed_along(): return lax.ppermute(value, axis, pairs)  34.9 us
    ppermute x8, waiting for transfers between devices, passed_along(): return lax.ppermute(value, axis, pairs)  18.7 us
    all_to_all x2, waiting for transfers between devices, exchange(): return lax.all_to_all(value, axis, split_axis=0, concat_axis=0, tiled=True)  14.7 us
    pallas_call x10, Pallas kernels, kernel_call(): pl.pallas_call(body, out_shape=[jax.ShapeDtypeStruct(shape, dtype) for sh...  13.1 us
    all_to_all x2, starting transfers between devices, exchange(): return lax.all_to_all(value, axis, split_axis=0, concat_axis=0, tiled=True)  9.02 us
  transfers between devices with their start and end apart: 10, of which 7 were waited for; matrix products, arithmetic and copies ran while one was open for 0% of the time, Pallas kernels for 0%

profile of v2, /device:TPU:1, one launch (start us, length us, event | category | flops | bytes accessed | tf_op | source)
XLA Modules:
  0.0 236.8 jit_solution(9380465883998711033)
XLA Ops:
  0.7 4.1 %collective-permute-start = (f32[400,128]{1,0:T(8,128)}, f32[400,128]{1,0:T(8,128)S(1)}, u32[]{:S(2)}, u32[]{:S(2)}) collective-permute-start(f32[400,128]{1,0:T(8,128)} %param.14), channel_id=1, source_target_pairs={{0,1},{1,2},{2,3},{3,0},{4,5},{5,6},{6,7},{7,4},{8,9},{9,10},{10,1... | collective-permute-start | bytes 614408 | tf_op jit(solution)/shard_map/ppermute | solution.py:34
  4.8 3.1 %collective-permute-start.1 = (f32[1,128]{1,0:T(1,128)}, f32[1,128]{1,0:T(1,128)S(1)}, u32[]{:S(2)}, u32[]{:S(2)}) collective-permute-start(f32[1,128]{1,0:T(1,128)} %bitcast.46), channel_id=1, source_target_pairs={{0,1},{1,2},{2,3},{3,0},{4,5},{5,6},{6,7},{7,4},{8,9},{9,10},{10,1... | collective-permute-start | bytes 1544 | tf_op jit(solution)/shard_map/ppermute | solution.py:34
  8.6 1.9 collective-permute-done.1.state_ref
  10.6 34.2 %all_to_all.55 = f32[128,4,128]{2,1,0:T(4,128)S(1)} all-to-all(f32[128,4,128]{2,1,0:T(4,128)S(1)} %bitcast.31), channel_id=1, replica_groups=mesh['z'=8,'y'=8,'core'=2,'x'=4] {'z','y','core'}, dimensions={0} | all-to-all | bytes 524288 | tf_op jit(solution)/shard_map/all_to_all | solution.py:38
  44.7 1.0 shard_map.164
  45.7 5.5 %all-to-all-start.1 = ((f32[128,4,128]{2,1,0:T(4,128)}), f32[128,4,128]{2,1,0:T(4,128)S(1)}, u32[]{:S(2)}, u32[]{:S(2)}) async-start(f32[128,4,128]{2,1,0:T(4,128)} %bitcast.4), calls=%async_computation.1 | async-start | bytes 524288 | tf_op jit(solution)/shard_map/all_to_all | solution.py:38
  51.9 14.7 %all-to-all-done.1 = f32[128,4,128]{2,1,0:T(4,128)S(1)} async-done(((f32[128,4,128]{2,1,0:T(4,128)}), f32[128,4,128]{2,1,0:T(4,128)S(1)}, u32[]{:S(2)}, u32[]{:S(2)}) %all-to-all-start.1) | async-done | bytes 262176 | tf_op jit(solution)/shard_map/all_to_all | solution.py:38
  66.7 3.2 %shard_map.165 = (f32[400,128]{1,0:T(8,128)S(1)}, f32[1,128]{1,0:T(1,128)S(1)}, f32[400,128]{1,0:T(8,128)S(1)}, f32[1,128]{1,0:T(1,128)S(1)}, f32[1280,128]{1,0:T(8,128)S(1)}, /*index=5*/f32[1280,128]{1,0:T(8,128)S(1)}) custom-call(s32[1,1]{1,0:T(1,128)} %bitcast.mine_ref, s32[1,1]{1,0:T(1,128)S(6)} %copy.19.live_ref, f32[512,128]{1,0:T(8,128)S(1)} %bitcast.33, ...), custom_call_target="tpu_custom_call" | custom-call | tf_op jit(solution)/shard_map/pallas_call | solution.py:54
  69.9 2.3 collective-permute-start.2
  72.2 1.7 collective-permute-done.2
  74.0 12.6 %all_to_all.56 = f32[4,320,128]{2,1,0:T(8,128)S(1)} all-to-all(f32[4,320,128]{2,1,0:T(8,128)S(1)} %bitcast.43), channel_id=1, replica_groups=mesh['z'=8,'y'=8,'core'=2,'x'=4] {'x'}, dimensions={0} | all-to-all | bytes 1310720 | tf_op jit(solution)/shard_map/all_to_all | solution.py:38
  86.6 11.0 %all_to_all.57 = f32[8,40,128]{2,1,0:T(8,128)S(1)} all-to-all(f32[8,40,128]{2,1,0:T(8,128)S(1)} %bitcast.44), channel_id=1, replica_groups=mesh['z'=8,'y'=8,'core'=2,'x'=4] {'y'}, dimensions={0} | all-to-all | bytes 327680 | tf_op jit(solution)/shard_map/all_to_all | solution.py:38
  97.6 10.7 %all_to_all.58 = f32[8,40,128]{2,1,0:T(8,128)S(1)} all-to-all(f32[8,40,128]{2,1,0:T(8,128)S(1)} %broadcast_in_dim.8), channel_id=1, replica_groups=mesh['z'=8,'y'=8,'core'=2,'x'=4] {'z'}, dimensions={0} | all-to-all | bytes 327680 | tf_op jit(solution)/shard_map/all_to_all | solution.py:38
  108.4 10.7 %all_to_all.59 = f32[8,40,128]{2,1,0:T(8,128)S(1)} all-to-all(f32[8,40,128]{2,1,0:T(8,128)S(1)} %broadcast_in_dim.9), channel_id=1, replica_groups=mesh['z'=8,'y'=8,'core'=2,'x'=4] {'y'}, dimensions={0} | all-to-all | bytes 327680 | tf_op jit(solution)/shard_map/all_to_all | solution.py:38
  119.1 10.0 %all_to_all.60 = f32[4,320,128]{2,1,0:T(8,128)S(1)} all-to-all(f32[4,320,128]{2,1,0:T(8,128)S(1)} %broadcast_in_dim.22), channel_id=1, replica_groups=mesh['z'=8,'y'=8,'core'=2,'x'=4] {'x'}, dimensions={0} | all-to-all | bytes 1310720 | tf_op jit(solution)/shard_map/all_to_all | solution.py:38
  129.1 8.5 %collective-permute-start.3 = (f32[1280,128]{1,0:T(8,128)S(1)}, f32[1280,128]{1,0:T(8,128)S(1)}, u32[]{:S(2)}, u32[]{:S(2)}) collective-permute-start(f32[1280,128]{1,0:T(8,128)S(1)} %bitcast.25), channel_id=1, source_target_pairs={{0,4},{4,0},{1,5},{5,1},{2,6},{6,2},{3,7},{7,3},{8,12},{12,8},{9,1... | collective-permute-start | bytes 1966088 | tf_op jit(solution)/shard_map/ppermute | solution.py:34
  137.6 1.7 collective-permute-done.3.other_ref
  139.3 4.1 %shard_map.166 = (f32[400,128]{1,0:T(8,128)}, f32[1,128]{1,0:T(1,128)}, f32[400,768]{1,0:T(8,128)S(1)}, f32[1,768]{1,0:T(1,128)S(1)}, f32[1536,128]{1,0:T(8,128)S(1)}, /*index=5*/f32[1536,128]{1,0:T(8,128)S(1)}) custom-call(s32[1,1]{1,0:T(1,128)} %bitcast.mine_ref, s32[1,1]{1,0:T(1,128)S(6)} %copy.19.live_ref, s32[1,1]{1,0:T(1,128)S(6)} %copy.18.partner_ref, ...), custom_call_target="tpu_custom_call" | custom-call | tf_op jit(solution)/shard_map/pallas_call | solution.py:54
  143.4 2.3 collective-permute-start.4
  145.6 1.9 collective-permute-done.4.got_ref
  147.5 0.9 shard_map.167
  148.5 3.5 %all-to-all-start.7 = ((f32[4,320,128]{2,1,0:T(8,128)}), f32[4,320,128]{2,1,0:T(8,128)S(1)}, u32[]{:S(2)}, u32[]{:S(2)}) async-start(f32[4,320,128]{2,1,0:T(8,128)} %bitcast.16), calls=%async_computation.7 | async-start | bytes 1310720 | tf_op jit(solution)/shard_map/all_to_all | solution.py:38
  152.0 4.5 %collective-permute-start.5 = (f32[512,128]{1,0:T(8,128)S(1)}, f32[512,128]{1,0:T(8,128)S(1)}, u32[]{:S(2)}, u32[]{:S(2)}) collective-permute-start(f32[512,128]{1,0:T(8,128)S(1)} %get-tuple-element.37), channel_id=1, source_target_pairs={{0,3},{1,0},{2,1},{3,2},{4,7},{5,4},{6,5},{7,6},{8,11},{9,8},{10,9... | collective-permute-start | bytes 786440 | tf_op jit(solution)/shard_map/ppermute | solution.py:34
  156.5 10.2 %collective-permute-done.5.block_ref = f32[512,128]{1,0:T(8,128)S(1)} collective-permute-done((f32[512,128]{1,0:T(8,128)S(1)}, f32[512,128]{1,0:T(8,128)S(1)}, u32[]{:S(2)}, u32[]{:S(2)}) %collective-permute-start.5) | collective-permute-done | bytes 262176 | tf_op jit(solution)/shard_map/ppermute | solution.py:34
  167.0 20.5 %all_to_all.61 = f32[64,16,128]{2,1,0:T(8,128)S(1)} all-to-all(f32[64,16,128]{2,1,0:T(8,128)S(1)} %bitcast.30), channel_id=1, replica_groups=mesh['z'=8,'y'=8,'core'=2,'x'=4] {'z','y'}, dimensions={0} | all-to-all | bytes 1048576 | tf_op jit(solution)/shard_map/all_to_all | solution.py:38
  187.5 1.1 shard_map.169
  188.6 22.6 %all_to_all.62 = f32[64,16,128]{2,1,0:T(8,128)S(1)} all-to-all(f32[64,16,128]{2,1,0:T(8,128)S(1)} %bitcast.29), channel_id=1, replica_groups=mesh['z'=8,'y'=8,'core'=2,'x'=4] {'z','y'}, dimensions={0} | all-to-all | bytes 1048576 | tf_op jit(solution)/shard_map/all_to_all | solution.py:38
  211.3 11.1 %all_to_all.63 = f32[4,320,128]{2,1,0:T(8,128)S(1)} all-to-all(f32[4,320,128]{2,1,0:T(8,128)S(1)} %get-tuple-element.41), channel_id=1, replica_groups=mesh['z'=8,'y'=8,'core'=2,'x'=4] {'x'}, dimensions={0} | all-to-all | bytes 1310720 | tf_op jit(solution)/shard_map/all_to_all | solution.py:38
  222.4 8.2 %collective-permute-start.7 = (f32[1280,128]{1,0:T(8,128)S(1)}, f32[1280,128]{1,0:T(8,128)S(1)}, u32[]{:S(2)}, u32[]{:S(2)}) collective-permute-start(f32[1280,128]{1,0:T(8,128)S(1)} %bitcast.23), channel_id=1, source_target_pairs={{0,4},{4,0},{1,5},{5,1},{2,6},{6,2},{3,7},{7,3},{8,12},{12,8},{9,1... | collective-permute-start | bytes 1966088 | tf_op jit(solution)/shard_map/ppermute | solution.py:34
  230.7 1.9 collective-permute-start.6
  232.6 1.3 collective-permute-done.6.other_ref
  234.7 1.5 shard_map.172
  (33 shorter events, 2.2 us)
Async XLA Ops:
  0.6 66.0 %copy-start = (f32[400,768]{1,0:T(8,128)S(1)}, f32[400,768]{1,0:T(8,128)}, u32[]{:S(2)}) copy-start(f32[400,768]{1,0:T(8,128)} %relations_ref.3) | copy-start | bytes 3686404
  0.6 66.0 %copy-start.2 = (s32[1,1,2048]{2,1,0:T(1,128)S(1)}, s32[1,1,2048]{2,1,0:T(1,128)}, u32[]{:S(2)}) copy-start(s32[1,1,2048]{2,1,0:T(1,128)} %param.23) | copy-start | bytes 24580
  0.7 66.0 %copy-start.5 = (s32[1,1,1024]{2,1,0:T(1,128)S(1)}, s32[1,1,1024]{2,1,0:T(1,128)}, u32[]{:S(2)}) copy-start(s32[1,1,1024]{2,1,0:T(1,128)} %param.22) | copy-start | bytes 12292
  0.7 66.0 %copy-start.4 = (s32[1,1,1024]{2,1,0:T(1,128)S(1)}, s32[1,1,1024]{2,1,0:T(1,128)}, u32[]{:S(2)}) copy-start(s32[1,1,1024]{2,1,0:T(1,128)} %param.21) | copy-start | bytes 12292
  0.7 66.0 %copy-start.3 = (s32[1,1,1024]{2,1,0:T(1,128)S(1)}, s32[1,1,1024]{2,1,0:T(1,128)}, u32[]{:S(2)}) copy-start(s32[1,1,1024]{2,1,0:T(1,128)} %param.20) | copy-start | bytes 12292
  0.7 66.0 %copy-start.6 = (f32[128]{0:T(128)S(1)}, f32[128]{0:T(128)}, u32[]{:S(2)}) copy-start(f32[128]{0:T(128)} %param.13) | copy-start | bytes 1540
  0.7 66.0 %copy-start.1 = (f32[400,128]{1,0:T(8,128)S(1)}, f32[400,128]{1,0:T(8,128)}, u32[]{:S(2)}) copy-start(f32[400,128]{1,0:T(8,128)} %source_ref.1) | copy-start | bytes 614404
  0.7 9.7 %collective-permute-start = (f32[400,128]{1,0:T(8,128)}, f32[400,128]{1,0:T(8,128)S(1)}, u32[]{:S(2)}, u32[]{:S(2)}) collective-permute-start(f32[400,128]{1,0:T(8,128)} %param.14), channel_id=1, source_target_pairs={{0,1},{1,2},{2,3},{3,0},{4,5},{5,6},{6,7},{7,4},{8,9},{9,10},{10,1... | collective-permute-start | bytes 614408 | tf_op jit(solution)/shard_map/ppermute | solution.py:34
  4.8 5.6 %collective-permute-start.1 = (f32[1,128]{1,0:T(1,128)}, f32[1,128]{1,0:T(1,128)S(1)}, u32[]{:S(2)}, u32[]{:S(2)}) collective-permute-start(f32[1,128]{1,0:T(1,128)} %bitcast.46), channel_id=1, source_target_pairs={{0,1},{1,2},{2,3},{3,0},{4,5},{5,6},{6,7},{7,4},{8,9},{9,10},{10,1... | collective-permute-start | bytes 1544 | tf_op jit(solution)/shard_map/ppermute | solution.py:34
  45.7 20.9 %all-to-all-start.1 = ((f32[128,4,128]{2,1,0:T(4,128)}), f32[128,4,128]{2,1,0:T(4,128)S(1)}, u32[]{:S(2)}, u32[]{:S(2)}) async-start(f32[128,4,128]{2,1,0:T(4,128)} %bitcast.4), calls=%async_computation.1 | async-start | bytes 524288 | tf_op jit(solution)/shard_map/all_to_all | solution.py:38
  69.9 4.0 %collective-permute-start.2 = (f32[1280,128]{1,0:T(8,128)S(1)}, f32[1280,128]{1,0:T(8,128)S(1)}, u32[]{:S(2)}, u32[]{:S(2)}) collective-permute-start(f32[1280,128]{1,0:T(8,128)S(1)} %get-tuple-element.27), channel_id=1, source_target_pairs={{0,4},{4,0},{1,5},{5,1},{2,6},{6,2},{3,7},{7,3},{8,12},{12,8},{9,1... | collective-permute-start | bytes 1966088 | tf_op jit(solution)/shard_map/ppermute | solution.py:34
  108.4 29.2 %copy-start.7 = (f32[768]{0:T(1024)S(1)}, f32[768]{0:T(1024)}, u32[]{:S(2)}) copy-start(f32[768]{0:T(1024)} %param.17) | copy-start | bytes 9220
  129.1 10.2 %collective-permute-start.3 = (f32[1280,128]{1,0:T(8,128)S(1)}, f32[1280,128]{1,0:T(8,128)S(1)}, u32[]{:S(2)}, u32[]{:S(2)}) collective-permute-start(f32[1280,128]{1,0:T(8,128)S(1)} %bitcast.25), channel_id=1, source_target_pairs={{0,4},{4,0},{1,5},{5,1},{2,6},{6,2},{3,7},{7,3},{8,12},{12,8},{9,1... | collective-permute-start | bytes 1966088 | tf_op jit(solution)/shard_map/ppermute | solution.py:34
  143.4 4.2 %collective-permute-start.4 = (f32[1536,128]{1,0:T(8,128)S(1)}, f32[1536,128]{1,0:T(8,128)S(1)}, u32[]{:S(2)}, u32[]{:S(2)}) collective-permute-start(f32[1536,128]{1,0:T(8,128)S(1)} %get-tuple-element.35), channel_id=1, source_target_pairs={{0,4},{4,0},{1,5},{5,1},{2,6},{6,2},{3,7},{7,3},{8,12},{12,8},{9,1... | collective-permute-start | bytes 2359304 | tf_op jit(solution)/shard_map/ppermute | solution.py:34
  148.5 18.2 %all-to-all-start.7 = ((f32[4,320,128]{2,1,0:T(8,128)}), f32[4,320,128]{2,1,0:T(8,128)S(1)}, u32[]{:S(2)}, u32[]{:S(2)}) async-start(f32[4,320,128]{2,1,0:T(8,128)} %bitcast.16), calls=%async_computation.7 | async-start | bytes 1310720 | tf_op jit(solution)/shard_map/all_to_all | solution.py:38
  152.0 14.8 %collective-permute-start.5 = (f32[512,128]{1,0:T(8,128)S(1)}, f32[512,128]{1,0:T(8,128)S(1)}, u32[]{:S(2)}, u32[]{:S(2)}) collective-permute-start(f32[512,128]{1,0:T(8,128)S(1)} %get-tuple-element.37), channel_id=1, source_target_pairs={{0,3},{1,0},{2,1},{3,2},{4,7},{5,4},{6,5},{7,6},{8,11},{9,8},{10,9... | collective-permute-start | bytes 786440 | tf_op jit(solution)/shard_map/ppermute | solution.py:34
  222.4 12.3 %collective-permute-start.7 = (f32[1280,128]{1,0:T(8,128)S(1)}, f32[1280,128]{1,0:T(8,128)S(1)}, u32[]{:S(2)}, u32[]{:S(2)}) collective-permute-start(f32[1280,128]{1,0:T(8,128)S(1)} %bitcast.23), channel_id=1, source_target_pairs={{0,4},{4,0},{1,5},{5,1},{2,6},{6,2},{3,7},{7,3},{8,12},{12,8},{9,1... | collective-permute-start | bytes 1966088 | tf_op jit(solution)/shard_map/ppermute | solution.py:34
  230.7 3.2 %collective-permute-start.6 = (f32[256,128]{1,0:T(8,128)S(1)}, f32[256,128]{1,0:T(8,128)S(1)}, u32[]{:S(2)}, u32[]{:S(2)}) collective-permute-start(f32[256,128]{1,0:T(8,128)S(1)} %slice.3), channel_id=1, source_target_pairs={{0,4},{4,0},{1,5},{5,1},{2,6},{6,2},{3,7},{7,3},{8,12},{12,8},{9,1... | collective-permute-start | bytes 393224 | tf_op jit(solution)/shard_map/ppermute | solution.py:34

commit v3 on v2

--- a/solution.py
+++ b/solution.py
@@ -43,6 +43,12 @@
     return exchange(value.reshape(count, rows // count, lanes), axis).reshape(rows, lanes)
 
 
+def packets(value, axis, count):
+    rows, lanes = value.shape
+    parts = rows // (count * PIECE)
+    return exchange(value.reshape(count, parts, PIECE, lanes), axis).reshape(rows, lanes)
+
+
 def gathered(value, axis):
     count = lax.axis_size(axis)
     return exchange(jnp.broadcast_to(value[None], (count,) + value.shape), axis)
@@ -57,7 +63,7 @@
         in_specs=specs,
         out_specs=[pl.BlockSpec(memory_space=pltpu.VMEM)] * len(outs),
         scratch_shapes=[pltpu.VMEM(shape, dtype) for shape, dtype in scratch],
-        compiler_params=pltpu.CompilerParams(vmem_limit_bytes=40 * 2**20),
+        compiler_params=pltpu.CompilerParams(vmem_limit_bytes=24 * 2**20),
     )(*args)
 
 
@@ -124,41 +130,38 @@
     out_ref[spaced(PIECE - 1, BLOCK, PIECE), :] = moved(pick, last)
 
 
-def train(
+def counted(rows_n):
+    hits = lax.broadcasted_iota(jnp.int32, (BLOCK, NEG), 0) == rows_n
+    count = jnp.sum(jnp.where(hits, 1.0, 0.0), axis=1, keepdims=True)
+    return jnp.broadcast_to(count, (BLOCK, BLOCK))
+
+
+def span_rows(i):
+    re = pl.ds(pl.multiple_of(8 * i, 8), 8)
+    im = pl.ds(pl.multiple_of(HALF + 8 * i, 8), 8)
+    return re, im
+
+
+def gradients(
     first,
     live_count,
-    source,
-    source_state,
     target,
-    target_state,
-    relation_bf,
-    rows_s,
-    rows_t,
-    rows_r,
-    rows_n,
+    pick_r,
+    count_wide,
     subject_ref,
     operator_ref,
     objects_ref,
     query_ref,
     slope_ref,
     flat_ref,
+    grad_subject_ref,
 ):
-    pick_s = one_hot(BLOCK, rows_s)
-    pick_t = one_hot(BLOCK, rows_t)
-    pick_r = one_hot(NREL, rows_r)
-    hits = lax.broadcasted_iota(jnp.int32, (BLOCK, NEG), 0) == rows_n
-    count = jnp.sum(jnp.where(hits, 1.0, 0.0), axis=1, keepdims=True)
-    count_row = jnp.broadcast_to(count, (BLOCK, BLOCK)).T[0:1, :]
     edge = lax.broadcasted_iota(jnp.int32, (1, SPAN), 1) + first
     live = jnp.where(edge < live_count, 1.0, 0.0)
     target_bf = target.astype(bf16)
-    subject_ref[...] = dot(source.astype(bf16), pick_s)
-    operator_ref[...] = dot(relation_bf, pick_r)
-    objects_ref[...] = dot(target_bf, pick_t)
 
     def form(i, total):
-        re = pl.ds(pl.multiple_of(8 * i, 8), 8)
-        im = pl.ds(pl.multiple_of(HALF + 8 * i, 8), 8)
+        re, im = span_rows(i)
         subject_re, subject_im = (subject_ref[re, :], subject_ref[im, :])
         operator_re, operator_im = (operator_ref[re, :], operator_ref[im, :])
         query_re = subject_re * operator_re - subject_im * operator_im
@@ -173,21 +176,20 @@
     score = dot(target.T.astype(bf16), query_bf)
     grad_pos = -sigmoid(-positive) * live
     slope = (sigmoid(score) * (live * (1.0 / NEG))).astype(bf16)
-    weighted = slope.astype(f32) * count
+    weighted = slope.astype(f32) * count_wide[:, 0:1]
     upper = weighted.astype(bf16)
     lower = (weighted - upper.astype(f32)).astype(bf16)
     slope_ref[...] = dot(target_bf, upper) + dot(target_bf, lower)
-    grad_noise = dot_last(query_bf, slope)
+    noise = dot_last(query_bf, slope).astype(bf16).astype(f32) * count_wide.T[0:1, :]
 
     def push(i, _):
-        re = pl.ds(pl.multiple_of(8 * i, 8), 8)
-        im = pl.ds(pl.multiple_of(HALF + 8 * i, 8), 8)
+        re, im = span_rows(i)
         query_gre = grad_pos * objects_ref[re, :] + slope_ref[re, :]
         query_gim = grad_pos * objects_ref[im, :] + slope_ref[im, :]
         subject_re, subject_im = (subject_ref[re, :], subject_ref[im, :])
         operator_re, operator_im = (operator_ref[re, :], operator_ref[im, :])
-        subject_ref[re, :] = query_gre * operator_re + query_gim * operator_im
-        subject_ref[im, :] = query_gim * operator_re - query_gre * operator_im
+        grad_subject_ref[re, :] = query_gre * operator_re + query_gim * operator_im
+        grad_subject_ref[im, :] = query_gim * operator_re - query_gre * operator_im
         operator_ref[re, :] = query_gre * subject_re + query_gim * subject_im
         operator_ref[im, :] = query_gim * subject_re - query_gre * subject_im
         query_ref[re, :] = grad_pos * query_ref[re, :]
@@ -201,15 +203,11 @@
         flat_ref[DIM * k : DIM * (k + 1), :] = pair[:, :LANES]
         flat_ref[DIM * (k + 1) : DIM * (k + 2), :] = pair[:, LANES:]
     flat_ref[DIM * CHUNKS : FLAT, :] = jnp.zeros((FLAT - DIM * CHUNKS, LANES), f32)
-    grad_source = dot_last(subject_ref[...].astype(bf16), pick_s)
-    grad_target = dot_last(query_ref[...].astype(bf16), pick_t)
-    grad_target = grad_target + grad_noise.astype(bf16).astype(f32) * count_row
-    source, source_state = stepped(source, source_state, grad_source)
-    target, target_state = stepped(target, target_state, grad_target)
-    return source, source_state, target, target_state
-
-
-TRAIN_SCRATCH = [((DIM, SPAN), f32)] * 5 + [((FLAT, LANES), f32)]
+    return noise
+
+
+WIDE = ((DIM, SPAN), f32)
+FLAT_TABLE = ((FLAT, LANES), f32)
 
 
 def halves(mine, flat_ref, keep_ref, give_ref):
@@ -245,32 +243,58 @@
 ):
     last = arrived_ref[spaced(PIECE - 1, BLOCK, PIECE), :].T
     target = jnp.concatenate(
-        [arrived_ref[spaced(k, BLOCK, PIECE), :].T for k in range(PIECE - 1)] + [last[:STATE_LANE, :]], 0
-    )
-    source, source_state, target, target_state = train(
+        [arrived_ref[spaced(k, BLOCK, PIECE), :].T for k in range(PIECE - 1)]
+        + [last[:STATE_LANE, :]],
+        0,
+    )
+    source = source_ref[...]
+    pick_s = one_hot(BLOCK, rows_s_ref[:, 0:SPAN])
+    pick_t = one_hot(BLOCK, rows_t_ref[:, 0:SPAN])
+    pick_r = one_hot(NREL, rows_r_ref[:, 0:SPAN])
+    subject_ref[...] = dot(source.astype(bf16), pick_s)
+    operator_ref[...] = dot(relations_ref[...].astype(bf16), pick_r)
+    objects_ref[...] = dot(target.astype(bf16), pick_t)
+    noise = gradients(
         0,
         live_ref[0, 0],
-        source_ref[...],
-        source_state_ref[...],
         target,
-        last[STATE_LANE : STATE_LANE + 1, :],
-        relations_ref[...].astype(bf16),
-        rows_s_ref[:, 0:SPAN],
-        rows_t_ref[:, 0:SPAN],
-        rows_r_ref[:, 0:SPAN],
-        rows_n_ref[:, 0:NEG],
+        pick_r,
+        counted(rows_n_ref[:, 0:NEG]),
         subject_ref,
         operator_ref,
         objects_ref,
         query_ref,
         slope_ref,
         flat_ref,
-    )
-    source_out[...] = source
-    source_state_out[...] = source_state
-    target_out[...] = target
-    target_state_out[...] = target_state
+        subject_ref,
+    )
     halves(mine_ref[0, 0], flat_ref, keep_out, give_out)
+    grad_source = dot_last(subject_ref[...].astype(bf16), pick_s)
+    source_out[...], source_state_out[...] = stepped(source, source_state_ref[...], grad_source)
+    grad_target = dot_last(query_ref[...].astype(bf16), pick_t) + noise
+    target_out[...], target_state_out[...] = stepped(
+        target, last[STATE_LANE : STATE_LANE + 1, :], grad_target
+    )
+
+
+def lookup_body(
+    source_ref,
+    target_ref,
+    rows_s_ref,
+    rows_t_ref,
+    rows_r_ref,
+    rows_n_ref,
+    subject_ref,
+    objects_ref,
+    pick_r_ref,
+    count_ref,
+):
+    pick_s = one_hot(BLOCK, rows_s_ref[:, SPAN : 2 * SPAN])
+    pick_t = one_hot(BLOCK, rows_t_ref[:, SPAN : 2 * SPAN])
+    subject_ref[...] = dot(source_ref[...].astype(bf16), pick_s)
+    objects_ref[...] = dot(target_ref[...].astype(bf16), pick_t)
+    pick_r_ref[...] = one_hot(NREL, rows_r_ref[:, SPAN : 2 * SPAN])
+    count_ref[...] = counted(rows_n_ref[:, NEG : 2 * NEG])
 
 
 def relation_update(mine, part_ref, other_ref, relations_ref, state_ref, out, state_out, flat_ref):
@@ -296,10 +320,12 @@
     target_state_ref,
     relations_ref,
     relation_state_ref,
+    first_subject_ref,
+    objects_ref,
+    pick_r_ref,
+    count_ref,
     rows_s_ref,
     rows_t_ref,
-    rows_r_ref,
-    rows_n_ref,
     source_out,
     source_state_out,
     relations_out,
@@ -308,7 +334,6 @@
     give_out,
     subject_ref,
     operator_ref,
-    objects_ref,
     query_ref,
     slope_ref,
     flat_ref,
@@ -325,86 +350,111 @@
         relation_state_out,
         flat_ref,
     )
-    source, source_state, target, target_state = train(
+    pick_r = pick_r_ref[...]
+    operator_ref[...] = dot(relations_out[...].astype(bf16), pick_r)
+    target = target_ref[...]
+    noise = gradients(
         SPAN,
         live_ref[0, 0],
-        source_ref[...],
-        source_state_ref[...],
-        target_ref[...],
-        target_state_ref[...],
-        relations_out[...].astype(bf16),
-        rows_s_ref[:, SPAN : 2 * SPAN],
-        rows_t_ref[:, SPAN : 2 * SPAN],
-        rows_r_ref[:, SPAN : 2 * SPAN],
-        rows_n_ref[:, NEG : 2 * NEG],
-        subject_ref,
+        target,
+        pick_r,
+        count_ref[...],
+        first_subject_ref,
         operator_ref,
         objects_ref,
         query_ref,
         slope_ref,
         flat_ref,
-    )
-    source_out[...] = source
-    source_state_out[...] = source_state
+        subject_ref,
+    )
     halves(mine, flat_ref, keep_out, give_out)
+    pick_s = one_hot(BLOCK, rows_s_ref[:, SPAN : 2 * SPAN])
+    pick_t = one_hot(BLOCK, rows_t_ref[:, SPAN : 2 * SPAN])
+    grad_source = dot_last(subject_ref[...].astype(bf16), pick_s)
+    source_out[...], source_state_out[...] = stepped(
+        source_ref[...], source_state_ref[...], grad_source
+    )
+    grad_target = dot_last(query_ref[...].astype(bf16), pick_t) + noise
+    target, target_state = stepped(target, target_state_ref[...], grad_target)
     for k in range(PIECE):
         if k < PIECE - 1:
             turned_ref[...] = target[LANES * k : LANES * (k + 1), :].T
         else:
             state = jnp.broadcast_to(target_state, (8, LANES))
             own = jnp.full((8, LANES), partner_ref[0, 0].astype(f32))
-            zero = jnp.zeros((LANES - STATE_LANE - 16, LANES), f32)
-            turned_ref[...] = jnp.concatenate([target[LANES * k : DIM, :], state, own, zero], 0).T
+            zero = jnp.zeros((LANES // 2 - STATE_LANE - 16, LANES), f32)
+            tail = [target[LANES * k : DIM, :], state, own, zero]
+            turned_ref[...] = jnp.concatenate(tail + tail, 0).T
         rows = slice(HALF_FLAT + 64 * k, HALF_FLAT + 64 * (k + 1))
-        keep_out[rows, :] = turned_ref[pl.ds(mine, 64, stride=2), :]
-        give_out[rows, :] = turned_ref[pl.ds(1 - mine, 64, stride=2), :]
-
-
-ROWS = 16
-SUM_ROW = 8
+        keep_out[rows, :] = turned_ref[spaced(mine, 64, 2), :]
+        give_out[rows, :] = turned_ref[spaced(1 - mine, 64, 2), :]
+
+
+FULL = PIECE - 1
+TAIL = 2 * FULL
+SUM_ROW = TAIL + 1
 SUM_ROWS = 5
+ROWS = SUM_ROW + SUM_ROWS
+
+
+def low_lanes(shape):
+    return lax.broadcasted_iota(jnp.int32, shape, 1) < LANES // 2
+
+
+def swapped(value):
+    return pltpu.roll(value, LANES // 2, 1)
 
 
 def join_body(keep_ref, got_ref, sums_ref, block_ref):
     sums_ref[...] = keep_ref[0:HALF_FLAT, :] + got_ref[0:HALF_FLAT, :]
-    block_ref[0 : 64 * PIECE, :] = keep_ref[HALF_FLAT:, :]
-    block_ref[64 * PIECE :, :] = got_ref[HALF_FLAT:, :]
+    full = 64 * FULL
+    block_ref[0:full, :] = keep_ref[HALF_FLAT : HALF_FLAT + full, :]
+    block_ref[full : 2 * full, :] = got_ref[HALF_FLAT : HALF_FLAT + full, :]
+    block_ref[2 * full :, :] = jnp.where(
+        low_lanes((64, LANES)), keep_ref[HALF_FLAT + full :, :], got_ref[HALF_FLAT + full :, :]
+    )
 
 
 def merge_body(received_ref, block_ref, out_ref):
-    for k in range(2 * PIECE):
+    for k in range(SUM_ROW):
         out_ref[spaced(k, 64, ROWS), :] = block_ref[64 * k : 64 * (k + 1), :]
     for k in range(SUM_ROWS):
         rows = slice(64 * k, 64 * (k + 1))
         total = received_ref[0, rows, :] + received_ref[1, rows, :]
         total = total + received_ref[2, rows, :] + received_ref[3, rows, :]
         out_ref[spaced(SUM_ROW + k, 64, ROWS), :] = total
-    for k in range(SUM_ROW + SUM_ROWS, ROWS):
-        out_ref[spaced(k, 64, ROWS), :] = jnp.zeros((64, LANES), f32)
 
 
 def middle_body(mine_ref, received_ref, out_ref, turned_ref):
     mine = mine_ref[0, 0]
     here, there = (spaced(mine, 64, 2), spaced(1 - mine, 64, 2))
-    back = None
-    for k in reversed(range(PIECE)):
+    tail = received_ref[spaced(TAIL, 64, ROWS), :]
+    turned_ref[here, :] = tail
+    turned_ref[there, :] = swapped(tail)
+    back = partner_pick(turned_ref[...]).T.astype(bf16)
+    turned_ref[...] = moved(back, turned_ref[...])
+    out_ref[spaced(TAIL, 64, ROWS), :] = jnp.where(
+        low_lanes((64, LANES)), turned_ref[here, :], swapped(turned_ref[there, :])
+    )
+    for k in range(FULL):
         turned_ref[here, :] = received_ref[spaced(k, 64, ROWS), :]
-        turned_ref[there, :] = received_ref[spaced(PIECE + k, 64, ROWS), :]
-        if back is None:
-            back = partner_pick(turned_ref[...]).T.astype(bf16)
+        turned_ref[there, :] = received_ref[spaced(FULL + k, 64, ROWS), :]
         turned_ref[...] = moved(back, turned_ref[...])
         out_ref[spaced(k, 64, ROWS), :] = turned_ref[here, :]
-        out_ref[spaced(PIECE + k, 64, ROWS), :] = turned_ref[there, :]
-    total = received_ref[SUM_ROW:ROWS, :]
-    for q in range(1, 64):
-        total = total + received_ref[ROWS * q + SUM_ROW : ROWS * (q + 1), :]
-    for q in range(64):
-        out_ref[ROWS * q + SUM_ROW : ROWS * (q + 1), :] = total
-
-
-def parting_body(received_ref, sums_ref, block_ref):
-    for k in range(2 * PIECE):
-        block_ref[64 * k : 64 * (k + 1), :] = received_ref[spaced(k, 64, ROWS), :]
+        out_ref[spaced(FULL + k, 64, ROWS), :] = turned_ref[there, :]
+    for k in range(SUM_ROW, ROWS):
+        total = jnp.sum(received_ref[spaced(k, 64, ROWS), :], axis=0, keepdims=True)
+        out_ref[spaced(k, 64, ROWS), :] = jnp.broadcast_to(total, (64, LANES))
+
+
+def parting_body(received_ref, sums_ref, block_ref, give_ref):
+    for k in range(FULL):
+        rows = slice(64 * k, 64 * (k + 1))
+        block_ref[rows, :] = received_ref[spaced(k, 64, ROWS), :]
+        give_ref[rows, :] = received_ref[spaced(FULL + k, 64, ROWS), :]
+    tail = received_ref[spaced(TAIL, 64, ROWS), :]
+    block_ref[64 * FULL :, :] = tail
+    give_ref[64 * FULL :, :] = swapped(tail)
     for k in range(SUM_ROWS):
         rows = received_ref[spaced(SUM_ROW + k, 64, ROWS), :]
         for x in range(4):
@@ -415,8 +465,8 @@
     mine = mine_ref[0, 0]
     for k in range(PIECE):
         rows = slice(64 * k, 64 * (k + 1))
-        turned_ref[pl.ds(mine, 64, stride=2), :] = block_ref[rows, :]
-        turned_ref[pl.ds(1 - mine, 64, stride=2), :] = other_ref[rows, :]
+        turned_ref[spaced(mine, 64, 2), :] = block_ref[rows, :]
+        turned_ref[spaced(1 - mine, 64, 2), :] = other_ref[rows, :]
         turned = turned_ref[...].T
         if k < PIECE - 1:
             out_ref[LANES * k : LANES * (k + 1), :] = turned
@@ -462,12 +512,17 @@
     block = ((DIM, BLOCK), f32)
     line = ((1, BLOCK), f32)
     half = ((HALF_FLAT, LANES), f32)
+    picks_r = ((NREL, SPAN), bf16)
+    square = ((BLOCK, BLOCK), f32)
     source, source_acc, target, target_acc, keep, give = kernel_call(
         first_body,
         [block, line, block, line, half, half],
         [mine, edge_count, arrived, source_emb, source_state.reshape(1, -1), relations] + lists,
-        TRAIN_SCRATCH,
+        [WIDE] * 5 + [FLAT_TABLE],
         scalars=2,
+    )
+    subject, objects, pick_r, count = kernel_call(
+        lookup_body, [WIDE, WIDE, picks_r, square], [source, target] + lists
     )
     part = keep + passed_along(give, "core", 1)
     part = jnp.sum(exchange(part.reshape(4, 320, LANES), "x"), 0)
@@ -482,30 +537,32 @@
     source, source_acc, relations, relation_acc, keep, give = kernel_call(
         second_body,
         [block, line, table, types, longer, longer],
-        [mine, edge_count, partner, part, other, source, source_acc, target, target_acc, relations]
-        + [relation_state.reshape(1, -1)]
-        + lists,
-        TRAIN_SCRATCH + [turned],
+        [mine, edge_count, partner, part, other, source, source_acc, target, target_acc]
+        + [relations, relation_state.reshape(1, -1), subject, objects, pick_r, count]
+        + lists[:2],
+        [WIDE] * 4 + [FLAT_TABLE, turned],
         scalars=3,
     )
     got = passed_along(give, "core", 1)
-    part, leaving = kernel_call(join_body, [half, ((128 * PIECE, LANES), f32)], [keep, got])
+    part, leaving = kernel_call(join_body, [half, ((64 * SUM_ROW, LANES), f32)], [keep, got])
     leaving = passed_along(leaving, "x", -1)
     received = exchange(part.reshape(4, 320, LANES), "x")
     packet = ((64 * ROWS, LANES), f32)
     (packed,) = kernel_call(merge_body, [packet], [received, leaving])
-    packed = dealt(packed, ("z", "y"), 64)
+    packed = packets(packed, ("z", "y"), 64)
     (packed,) = kernel_call(middle_body, [packet], [mine, packed], [turned], scalars=1)
-    packed = dealt(packed, ("z", "y"), 64)
-    sums, returned = kernel_call(
-        parting_body, [((4, 320, LANES), f32), ((128 * PIECE, LANES), f32)], [packed]
-    )
-    sibling = passed_along(returned[64 * PIECE :], "core", 1)
+    packed = packets(packed, ("z", "y"), 64)
+    pieces = ((64 * PIECE, LANES), f32)
+    sums, returned, sibling = kernel_call(
+        parting_body, [((4, 320, LANES), f32), pieces, pieces], [packed]
+    )
+    sibling = passed_along(sibling, "core", 1)
     part = exchange(sums, "x").reshape(HALF_FLAT, LANES)
-    other = passed_along(part, "core", 1)
     settled, settled_acc = kernel_call(
         settle_body, [block, line], [mine, returned, sibling], [turned], scalars=1
     )
+    part, settled, settled_acc = lax.optimization_barrier((part, settled, settled_acc))
+    other = passed_along(part, "core", 1)
     relations, relation_acc = kernel_call(
         final_body,
         [table, types],

time: 238 us -> 230 us (0.966)
  blocking collectives: 143 us -> 128 us
  starting transfers between devices: 43.9 us -> 51 us
    all_to_all x9 -> x8, blocking collectives: 143 us -> 128 us  [exchange(): return lax.all_to_all(value, axis, split_axis=0, concat_axis=0, tiled=True)]
    all_to_all x2 -> x3, starting transfers between devices: 9.02 us -> 12.7 us  [exchange(): return lax.all_to_all(value, axis, split_axis=0, concat_axis=0, tiled=True)]
    ppermute x8, starting transfers between devices: 34.9 us -> 38.3 us  [passed_along(): return lax.ppermute(value, axis, pairs)]
    pallas_call x10 -> x11, Pallas kernels: 13.1 us -> 13.9 us  [kernel_call(): pl.pallas_call(body, out_shape=[jax.ShapeDtypeStruct(shape, dtype) for sh...]
    all_to_all x2 -> x3, waiting for transfers between devices: 14.7 us -> 14.7 us  [exchange(): return lax.all_to_all(value, axis, split_axis=0, concat_axis=0, tiled=True)]
  transfers between devices with their start and end apart: 10 -> 11, of which waited for: 7 -> 8; matrix products, arithmetic and copies ran while one was open for 0% -> 0% of each run, Pallas kernels for 0% -> 1%
where the time goes in v3:
time: 230 us; the launch traced here: 229 us
  blocking collectives  128 us (56%)
  starting transfers between devices  51 us (22%)
  waiting for transfers between devices  33.4 us (15%)
  Pallas kernels  13.9 us (6%)
    all_to_all x8, blocking collectives, exchange(): return lax.all_to_all(value, axis, split_axis=0, concat_axis=0, tiled=True)  128 us
    ppermute x8, starting transfers between devices, passed_along(): return lax.ppermute(value, axis, pairs)  38.3 us
    ppermute x8, waiting for transfers between devices, passed_along(): return lax.ppermute(value, axis, pairs)  18.6 us
    all_to_all x3, waiting for transfers between devices, exchange(): return lax.all_to_all(value, axis, split_axis=0, concat_axis=0, tiled=True)  14.7 us
    pallas_call x11, Pallas kernels, kernel_call(): pl.pallas_call(body, out_shape=[jax.ShapeDtypeStruct(shape, dtype) for sh...  13.9 us
    all_to_all x3, starting transfers between devices, exchange(): return lax.all_to_all(value, axis, split_axis=0, concat_axis=0, tiled=True)  12.7 us
  transfers between devices with their start and end apart: 11, of which 8 were waited for; matrix products, arithmetic and copies ran while one was open for 0% of the time, Pallas kernels for 1%

profile of v3, /device:TPU:1, one launch (start us, length us, event | category | flops | bytes accessed | tf_op | source)
XLA Modules:
  0.0 229.0 jit_solution(5300374899938527816)
XLA Ops:
  0.7 4.1 %collective-permute-start = (f32[400,128]{1,0:T(8,128)}, f32[400,128]{1,0:T(8,128)S(1)}, u32[]{:S(2)}, u32[]{:S(2)}) collective-permute-start(f32[400,128]{1,0:T(8,128)} %param.14), channel_id=1, source_target_pairs={{0,1},{1,2},{2,3},{3,0},{4,5},{5,6},{6,7},{7,4},{8,9},{9,10},{10,1... | collective-permute-start | bytes 614408 | tf_op jit(solution)/shard_map/ppermute | solution.py:34
  4.8 3.1 %collective-permute-start.1 = (f32[1,128]{1,0:T(1,128)}, f32[1,128]{1,0:T(1,128)S(1)}, u32[]{:S(2)}, u32[]{:S(2)}) collective-permute-start(f32[1,128]{1,0:T(1,128)} %bitcast.48), channel_id=1, source_target_pairs={{0,1},{1,2},{2,3},{3,0},{4,5},{5,6},{6,7},{7,4},{8,9},{9,10},{10,1... | collective-permute-start | bytes 1544 | tf_op jit(solution)/shard_map/ppermute | solution.py:34
  8.6 1.9 collective-permute-done.1.state_ref
  10.6 34.2 %all_to_all.55 = f32[128,4,128]{2,1,0:T(4,128)S(1)} all-to-all(f32[128,4,128]{2,1,0:T(4,128)S(1)} %bitcast.31), channel_id=1, replica_groups=mesh['z'=8,'y'=8,'core'=2,'x'=4] {'z','y','core'}, dimensions={0} | all-to-all | bytes 524288 | tf_op jit(solution)/shard_map/all_to_all | solution.py:38
  44.7 1.0 shard_map.164
  45.7 5.5 %all-to-all-start.1 = ((f32[128,4,128]{2,1,0:T(4,128)}), f32[128,4,128]{2,1,0:T(4,128)S(1)}, u32[]{:S(2)}, u32[]{:S(2)}) async-start(f32[128,4,128]{2,1,0:T(4,128)} %bitcast.4), calls=%async_computation.1 | async-start | bytes 524288 | tf_op jit(solution)/shard_map/all_to_all | solution.py:38
  51.9 14.7 %all-to-all-done.1 = f32[128,4,128]{2,1,0:T(4,128)S(1)} async-done(((f32[128,4,128]{2,1,0:T(4,128)}), f32[128,4,128]{2,1,0:T(4,128)S(1)}, u32[]{:S(2)}, u32[]{:S(2)}) %all-to-all-start.1) | async-done | bytes 262176 | tf_op jit(solution)/shard_map/all_to_all | solution.py:38
  66.7 3.2 %shard_map.165 = (f32[400,128]{1,0:T(8,128)S(1)}, f32[1,128]{1,0:T(1,128)S(1)}, f32[400,128]{1,0:T(8,128)S(1)}, f32[1,128]{1,0:T(1,128)S(1)}, f32[1280,128]{1,0:T(8,128)S(1)}, /*index=5*/f32[1280,128]{1,0:T(8,128)S(1)}) custom-call(s32[1,1]{1,0:T(1,128)} %bitcast.mine_ref, s32[1,1]{1,0:T(1,128)S(6)} %copy.19.live_ref, f32[512,128]{1,0:T(8,128)S(1)} %bitcast.33, ...), custom_call_target="tpu_custom_call" | custom-call | tf_op jit(solution)/shard_map/pallas_call | solution.py:60
  69.9 2.3 collective-permute-start.2
  72.2 1.7 collective-permute-done.2
  74.0 12.6 %all_to_all.56 = f32[4,320,128]{2,1,0:T(8,128)S(1)} all-to-all(f32[4,320,128]{2,1,0:T(8,128)S(1)} %bitcast.45), channel_id=1, replica_groups=mesh['z'=8,'y'=8,'core'=2,'x'=4] {'x'}, dimensions={0} | all-to-all | bytes 1310720 | tf_op jit(solution)/shard_map/all_to_all | solution.py:38
  86.6 11.0 %all_to_all.57 = f32[8,40,128]{2,1,0:T(8,128)S(1)} all-to-all(f32[8,40,128]{2,1,0:T(8,128)S(1)} %bitcast.46), channel_id=1, replica_groups=mesh['z'=8,'y'=8,'core'=2,'x'=4] {'y'}, dimensions={0} | all-to-all | bytes 327680 | tf_op jit(solution)/shard_map/all_to_all | solution.py:38
  97.6 10.7 %all_to_all.58 = f32[8,40,128]{2,1,0:T(8,128)S(1)} all-to-all(f32[8,40,128]{2,1,0:T(8,128)S(1)} %broadcast_in_dim.8), channel_id=1, replica_groups=mesh['z'=8,'y'=8,'core'=2,'x'=4] {'z'}, dimensions={0} | all-to-all | bytes 327680 | tf_op jit(solution)/shard_map/all_to_all | solution.py:38
  108.4 10.7 %all_to_all.59 = f32[8,40,128]{2,1,0:T(8,128)S(1)} all-to-all(f32[8,40,128]{2,1,0:T(8,128)S(1)} %broadcast_in_dim.9), channel_id=1, replica_groups=mesh['z'=8,'y'=8,'core'=2,'x'=4] {'y'}, dimensions={0} | all-to-all | bytes 327680 | tf_op jit(solution)/shard_map/all_to_all | solution.py:38
  119.1 10.0 %all_to_all.60 = f32[4,320,128]{2,1,0:T(8,128)S(1)} all-to-all(f32[4,320,128]{2,1,0:T(8,128)S(1)} %broadcast_in_dim.22), channel_id=1, replica_groups=mesh['z'=8,'y'=8,'core'=2,'x'=4] {'x'}, dimensions={0} | all-to-all | bytes 1310720 | tf_op jit(solution)/shard_map/all_to_all | solution.py:38
  129.1 8.5 %collective-permute-start.3 = (f32[1280,128]{1,0:T(8,128)S(1)}, f32[1280,128]{1,0:T(8,128)S(1)}, u32[]{:S(2)}, u32[]{:S(2)}) collective-permute-start(f32[1280,128]{1,0:T(8,128)S(1)} %bitcast.25), channel_id=1, source_target_pairs={{0,4},{4,0},{1,5},{5,1},{2,6},{6,2},{3,7},{7,3},{8,12},{12,8},{9,1... | collective-permute-start | bytes 1966088 | tf_op jit(solution)/shard_map/ppermute | solution.py:34
  138.3 1.0 collective-permute-done.3.other_ref
  139.3 3.7 %shard_map.167 = (f32[400,128]{1,0:T(8,128)}, f32[1,128]{1,0:T(1,128)}, f32[400,768]{1,0:T(8,128)S(1)}, f32[1,768]{1,0:T(1,128)S(1)}, f32[1536,128]{1,0:T(8,128)S(1)}, /*index=5*/f32[1536,128]{1,0:T(8,128)S(1)}) custom-call(s32[1,1]{1,0:T(1,128)} %bitcast.mine_ref, s32[1,1]{1,0:T(1,128)S(6)} %copy.19.live_ref, s32[1,1]{1,0:T(1,128)S(6)} %copy.18.partner_ref, ...), custom_call_target="tpu_custom_call" | custom-call | tf_op jit(solution)/shard_map/pallas_call | solution.py:60
  143.0 2.3 collective-permute-start.4
  145.3 1.9 collective-permute-done.4.got_ref
  148.2 3.5 %all-to-all-start.7 = ((f32[4,320,128]{2,1,0:T(8,128)}), f32[4,320,128]{2,1,0:T(8,128)S(1)}, u32[]{:S(2)}, u32[]{:S(2)}) async-start(f32[4,320,128]{2,1,0:T(8,128)} %bitcast.16), calls=%async_computation.7 | async-start | bytes 1310720 | tf_op jit(solution)/shard_map/all_to_all | solution.py:38
  151.6 4.5 %collective-permute-start.5 = (f32[448,128]{1,0:T(8,128)S(1)}, f32[448,128]{1,0:T(8,128)S(1)}, u32[]{:S(2)}, u32[]{:S(2)}) collective-permute-start(f32[448,128]{1,0:T(8,128)S(1)} %get-tuple-element.49), channel_id=1, source_target_pairs={{0,3},{1,0},{2,1},{3,2},{4,7},{5,4},{6,5},{7,6},{8,11},{9,8},{10,9... | collective-permute-start | bytes 688136 | tf_op jit(solution)/shard_map/ppermute | solution.py:34
  156.2 9.5 %collective-permute-done.5.block_ref = f32[448,128]{1,0:T(8,128)S(1)} collective-permute-done((f32[448,128]{1,0:T(8,128)S(1)}, f32[448,128]{1,0:T(8,128)S(1)}, u32[]{:S(2)}, u32[]{:S(2)}) %collective-permute-start.5) | collective-permute-done | bytes 229408 | tf_op jit(solution)/shard_map/ppermute | solution.py:34
  165.8 18.3 %all_to_all.61 = f32[64,3,4,128]{3,2,1,0:T(4,128)S(1)} all-to-all(f32[64,3,4,128]{3,2,1,0:T(4,128)S(1)} %bitcast.28), channel_id=1, replica_groups=mesh['z'=8,'y'=8,'core'=2,'x'=4] {'z','y'}, dimensions={0} | all-to-all | bytes 786432 | tf_op jit(solution)/shard_map/all_to_all | solution.py:38
  184.0 1.0 shard_map.170
  185.0 20.3 %all_to_all.62 = f32[64,3,4,128]{3,2,1,0:T(4,128)S(1)} all-to-all(f32[64,3,4,128]{3,2,1,0:T(4,128)S(1)} %bitcast.30), channel_id=1, replica_groups=mesh['z'=8,'y'=8,'core'=2,'x'=4] {'z','y'}, dimensions={0} | all-to-all | bytes 786432 | tf_op jit(solution)/shard_map/all_to_all | solution.py:38
  206.2 3.7 %all-to-all-start.10 = ((f32[4,320,128]{2,1,0:T(8,128)}), f32[4,320,128]{2,1,0:T(8,128)S(1)}, u32[]{:S(2)}, u32[]{:S(2)}) async-start(f32[4,320,128]{2,1,0:T(8,128)} %get-tuple-element.50), calls=%async_computation.10 | async-start | bytes 1310720 | tf_op jit(solution)/shard_map/all_to_all | solution.py:38
  209.9 6.6 %collective-permute-start.6 = (f32[256,128]{1,0:T(8,128)S(1)}, f32[256,128]{1,0:T(8,128)S(1)}, u32[]{:S(2)}, u32[]{:S(2)}) collective-permute-start(f32[256,128]{1,0:T(8,128)S(1)} %get-tuple-element.52), channel_id=1, source_target_pairs={{0,4},{4,0},{1,5},{5,1},{2,6},{6,2},{3,7},{7,3},{8,12},{12,8},{9,1... | collective-permute-start | bytes 393224 | tf_op jit(solution)/shard_map/ppermute | solution.py:34
  216.5 1.0 collective-permute-done.6.other_ref
  218.3 7.0 %collective-permute-start.7 = (f32[1280,128]{1,0:T(8,128)S(1)}, f32[1280,128]{1,0:T(8,128)S(1)}, u32[]{:S(2)}, u32[]{:S(2)}) collective-permute-start(f32[1280,128]{1,0:T(8,128)S(1)} %bitcast.23), channel_id=1, source_target_pairs={{0,4},{4,0},{1,5},{5,1},{2,6},{6,2},{3,7},{7,3},{8,12},{12,8},{9,1... | collective-permute-start | bytes 1966088 | tf_op jit(solution)/shard_map/ppermute | solution.py:34
  225.3 1.7 collective-permute-done.7.other_ref
  227.0 1.5 shard_map.173
  (34 shorter events, 4.4 us)
Async XLA Ops:
  0.6 66.0 %copy-start = (f32[400,768]{1,0:T(8,128)S(1)}, f32[400,768]{1,0:T(8,128)}, u32[]{:S(2)}) copy-start(f32[400,768]{1,0:T(8,128)} %relations_ref.3) | copy-start | bytes 3686404
  0.6 66.0 %copy-start.4 = (s32[1,1,2048]{2,1,0:T(1,128)S(1)}, s32[1,1,2048]{2,1,0:T(1,128)}, u32[]{:S(2)}) copy-start(s32[1,1,2048]{2,1,0:T(1,128)} %param.23) | copy-start | bytes 24580
  0.7 66.0 %copy-start.5 = (s32[1,1,1024]{2,1,0:T(1,128)S(1)}, s32[1,1,1024]{2,1,0:T(1,128)}, u32[]{:S(2)}) copy-start(s32[1,1,1024]{2,1,0:T(1,128)} %param.22) | copy-start | bytes 12292
  0.7 66.0 %copy-start.3 = (s32[1,1,1024]{2,1,0:T(1,128)S(1)}, s32[1,1,1024]{2,1,0:T(1,128)}, u32[]{:S(2)}) copy-start(s32[1,1,1024]{2,1,0:T(1,128)} %param.21) | copy-start | bytes 12292
  0.7 66.0 %copy-start.2 = (s32[1,1,1024]{2,1,0:T(1,128)S(1)}, s32[1,1,1024]{2,1,0:T(1,128)}, u32[]{:S(2)}) copy-start(s32[1,1,1024]{2,1,0:T(1,128)} %param.20) | copy-start | bytes 12292
  0.7 66.0 %copy-start.6 = (f32[128]{0:T(128)S(1)}, f32[128]{0:T(128)}, u32[]{:S(2)}) copy-start(f32[128]{0:T(128)} %param.13) | copy-start | bytes 1540
  0.7 66.0 %copy-start.1 = (f32[400,128]{1,0:T(8,128)S(1)}, f32[400,128]{1,0:T(8,128)}, u32[]{:S(2)}) copy-start(f32[400,128]{1,0:T(8,128)} %source_ref.1) | copy-start | bytes 614404
  0.7 9.7 %collective-permute-start = (f32[400,128]{1,0:T(8,128)}, f32[400,128]{1,0:T(8,128)S(1)}, u32[]{:S(2)}, u32[]{:S(2)}) collective-permute-start(f32[400,128]{1,0:T(8,128)} %param.14), channel_id=1, source_target_pairs={{0,1},{1,2},{2,3},{3,0},{4,5},{5,6},{6,7},{7,4},{8,9},{9,10},{10,1... | collective-permute-start | bytes 614408 | tf_op jit(solution)/shard_map/ppermute | solution.py:34
  4.8 5.6 %collective-permute-start.1 = (f32[1,128]{1,0:T(1,128)}, f32[1,128]{1,0:T(1,128)S(1)}, u32[]{:S(2)}, u32[]{:S(2)}) collective-permute-start(f32[1,128]{1,0:T(1,128)} %bitcast.48), channel_id=1, source_target_pairs={{0,1},{1,2},{2,3},{3,0},{4,5},{5,6},{6,7},{7,4},{8,9},{9,10},{10,1... | collective-permute-start | bytes 1544 | tf_op jit(solution)/shard_map/ppermute | solution.py:34
  45.7 20.9 %all-to-all-start.1 = ((f32[128,4,128]{2,1,0:T(4,128)}), f32[128,4,128]{2,1,0:T(4,128)S(1)}, u32[]{:S(2)}, u32[]{:S(2)}) async-start(f32[128,4,128]{2,1,0:T(4,128)} %bitcast.4), calls=%async_computation.1 | async-start | bytes 524288 | tf_op jit(solution)/shard_map/all_to_all | solution.py:38
  69.9 4.0 %collective-permute-start.2 = (f32[1280,128]{1,0:T(8,128)S(1)}, f32[1280,128]{1,0:T(8,128)S(1)}, u32[]{:S(2)}, u32[]{:S(2)}) collective-permute-start(f32[1280,128]{1,0:T(8,128)S(1)} %get-tuple-element.35), channel_id=1, source_target_pairs={{0,4},{4,0},{1,5},{5,1},{2,6},{6,2},{3,7},{7,3},{8,12},{12,8},{9,1... | collective-permute-start | bytes 1966088 | tf_op jit(solution)/shard_map/ppermute | solution.py:34
  108.4 29.2 %copy-start.7 = (f32[768]{0:T(1024)S(1)}, f32[768]{0:T(1024)}, u32[]{:S(2)}) copy-start(f32[768]{0:T(1024)} %param.17) | copy-start | bytes 9220
  129.1 10.2 %collective-permute-start.3 = (f32[1280,128]{1,0:T(8,128)S(1)}, f32[1280,128]{1,0:T(8,128)S(1)}, u32[]{:S(2)}, u32[]{:S(2)}) collective-permute-start(f32[1280,128]{1,0:T(8,128)S(1)} %bitcast.25), channel_id=1, source_target_pairs={{0,4},{4,0},{1,5},{5,1},{2,6},{6,2},{3,7},{7,3},{8,12},{12,8},{9,1... | collective-permute-start | bytes 1966088 | tf_op jit(solution)/shard_map/ppermute | solution.py:34
  143.0 4.2 %collective-permute-start.4 = (f32[1536,128]{1,0:T(8,128)S(1)}, f32[1536,128]{1,0:T(8,128)S(1)}, u32[]{:S(2)}, u32[]{:S(2)}) collective-permute-start(f32[1536,128]{1,0:T(8,128)S(1)} %get-tuple-element.47), channel_id=1, source_target_pairs={{0,4},{4,0},{1,5},{5,1},{2,6},{6,2},{3,7},{7,3},{8,12},{12,8},{9,1... | collective-permute-start | bytes 2359304 | tf_op jit(solution)/shard_map/ppermute | solution.py:34
  148.2 17.5 %all-to-all-start.7 = ((f32[4,320,128]{2,1,0:T(8,128)}), f32[4,320,128]{2,1,0:T(8,128)S(1)}, u32[]{:S(2)}, u32[]{:S(2)}) async-start(f32[4,320,128]{2,1,0:T(8,128)} %bitcast.16), calls=%async_computation.7 | async-start | bytes 1310720 | tf_op jit(solution)/shard_map/all_to_all | solution.py:38
  151.6 14.1 %collective-permute-start.5 = (f32[448,128]{1,0:T(8,128)S(1)}, f32[448,128]{1,0:T(8,128)S(1)}, u32[]{:S(2)}, u32[]{:S(2)}) collective-permute-start(f32[448,128]{1,0:T(8,128)S(1)} %get-tuple-element.49), channel_id=1, source_target_pairs={{0,3},{1,0},{2,1},{3,2},{4,7},{5,4},{6,5},{7,6},{8,11},{9,8},{10,9... | collective-permute-start | bytes 688136 | tf_op jit(solution)/shard_map/ppermute | solution.py:34
  206.2 12.1 %all-to-all-start.10 = ((f32[4,320,128]{2,1,0:T(8,128)}), f32[4,320,128]{2,1,0:T(8,128)S(1)}, u32[]{:S(2)}, u32[]{:S(2)}) async-start(f32[4,320,128]{2,1,0:T(8,128)} %get-tuple-element.50), calls=%async_computation.10 | async-start | bytes 1310720 | tf_op jit(solution)/shard_map/all_to_all | solution.py:38
  209.9 7.6 %collective-permute-start.6 = (f32[256,128]{1,0:T(8,128)S(1)}, f32[256,128]{1,0:T(8,128)S(1)}, u32[]{:S(2)}, u32[]{:S(2)}) collective-permute-start(f32[256,128]{1,0:T(8,128)S(1)} %get-tuple-element.52), channel_id=1, source_target_pairs={{0,4},{4,0},{1,5},{5,1},{2,6},{6,2},{3,7},{7,3},{8,12},{12,8},{9,1... | collective-permute-start | bytes 393224 | tf_op jit(solution)/shard_map/ppermute | solution.py:34
  218.3 8.7 %collective-permute-start.7 = (f32[1280,128]{1,0:T(8,128)S(1)}, f32[1280,128]{1,0:T(8,128)S(1)}, u32[]{:S(2)}, u32[]{:S(2)}) collective-permute-start(f32[1280,128]{1,0:T(8,128)S(1)} %bitcast.23), channel_id=1, source_target_pairs={{0,4},{4,0},{1,5},{5,1},{2,6},{6,2},{3,7},{7,3},{8,12},{12,8},{9,1... | collective-permute-start | bytes 1966088 | tf_op jit(solution)/shard_map/ppermute | solution.py:34

commit v4 on v3

--- a/solution.py
+++ b/solution.py
@@ -101,14 +101,37 @@
     return pl.ds(start, size, stride=stride)
 
 
-def pack_body(partner_ref, arriving_ref, state_ref, out_ref):
+def pack_body(partner_ref, dest_ref, state_ref, out_ref):
     for k in range(PIECE - 1):
-        out_ref[spaced(k, BLOCK, PIECE), :] = arriving_ref[LANES * k : LANES * (k + 1), :].T
-    tail = arriving_ref[LANES * (PIECE - 1) : DIM, :]
+        out_ref[spaced(k, BLOCK, PIECE), :] = dest_ref[LANES * k : LANES * (k + 1), :].T
+    tail = dest_ref[LANES * (PIECE - 1) : DIM, :]
     state = jnp.broadcast_to(state_ref[...], (8, LANES))
     own = jnp.full((8, LANES), partner_ref[0, 0].astype(f32))
     zero = jnp.zeros((LANES - tail.shape[0] - 16, LANES), f32)
     out_ref[spaced(PIECE - 1, BLOCK, PIECE), :] = jnp.concatenate([tail, state, own, zero], 0).T
+
+
+STATE_ROW = DIM
+LIVE_ROW = DIM + 1
+LIST_ROWS = (DIM + 8, DIM + 16, DIM + 24, DIM + 32)
+BUCKET_ROWS = DIM + 48
+
+
+def bucket_body(live_ref, source_ref, state_ref, list_s, list_t, list_r, list_n, out_ref):
+    out_ref[0:DIM, :] = source_ref[...]
+    live = jnp.full((7, LANES), live_ref[0, 0].astype(f32))
+    out_ref[DIM : DIM + 8, :] = jnp.concatenate([state_ref[...], live], 0)
+    for first, ref in zip(LIST_ROWS, (list_s, list_t, list_r, list_n)):
+        for k in range(ref.shape[1] // LANES):
+            row = ref[:, LANES * k : LANES * (k + 1)].astype(f32)
+            out_ref[first + k : first + k + 1, :] = row
+
+
+def listed(bucket_ref, which, span):
+    count = (NEG if which == 3 else SPAN) // LANES
+    first = LIST_ROWS[which] + count * span
+    rows = [bucket_ref[first + k : first + k + 1, :] for k in range(count)]
+    return jnp.concatenate(rows, 1).astype(jnp.int32)
 
 
 STATE_LANE = DIM - LANES * (PIECE - 1)
@@ -144,7 +167,7 @@
 
 def gradients(
     first,
-    live_count,
+    bucket_ref,
     target,
     pick_r,
     count_wide,
@@ -157,6 +180,8 @@
     grad_subject_ref,
 ):
     edge = lax.broadcasted_iota(jnp.int32, (1, SPAN), 1) + first
+    live_count = bucket_ref[LIVE_ROW : LIVE_ROW + 1, :]
+    live_count = jnp.concatenate([live_count] * (SPAN // LANES), 1).astype(jnp.int32)
     live = jnp.where(edge < live_count, 1.0, 0.0)
     target_bf = target.astype(bf16)
 
@@ -219,15 +244,9 @@
 
 def first_body(
     mine_ref,
-    live_ref,
     arrived_ref,
-    source_ref,
-    source_state_ref,
+    bucket_ref,
     relations_ref,
-    rows_s_ref,
-    rows_t_ref,
-    rows_r_ref,
-    rows_n_ref,
     source_out,
     source_state_out,
     target_out,
@@ -247,19 +266,19 @@
         + [last[:STATE_LANE, :]],
         0,
     )
-    source = source_ref[...]
-    pick_s = one_hot(BLOCK, rows_s_ref[:, 0:SPAN])
-    pick_t = one_hot(BLOCK, rows_t_ref[:, 0:SPAN])
-    pick_r = one_hot(NREL, rows_r_ref[:, 0:SPAN])
+    source = bucket_ref[0:DIM, :]
+    pick_s = one_hot(BLOCK, listed(bucket_ref, 0, 0))
+    pick_t = one_hot(BLOCK, listed(bucket_ref, 1, 0))
+    pick_r = one_hot(NREL, listed(bucket_ref, 2, 0))
     subject_ref[...] = dot(source.astype(bf16), pick_s)
     operator_ref[...] = dot(relations_ref[...].astype(bf16), pick_r)
     objects_ref[...] = dot(target.astype(bf16), pick_t)
     noise = gradients(
         0,
-        live_ref[0, 0],
+        bucket_ref,
         target,
         pick_r,
-        counted(rows_n_ref[:, 0:NEG]),
+        counted(listed(bucket_ref, 3, 0)),
         subject_ref,
         operator_ref,
         objects_ref,
@@ -270,7 +289,9 @@
     )
     halves(mine_ref[0, 0], flat_ref, keep_out, give_out)
     grad_source = dot_last(subject_ref[...].astype(bf16), pick_s)
-    source_out[...], source_state_out[...] = stepped(source, source_state_ref[...], grad_source)
+    source_out[...], source_state_out[...] = stepped(
+        source, bucket_ref[STATE_ROW : STATE_ROW + 1, :], grad_source
+    )
     grad_target = dot_last(query_ref[...].astype(bf16), pick_t) + noise
     target_out[...], target_state_out[...] = stepped(
         target, last[STATE_LANE : STATE_LANE + 1, :], grad_target
@@ -280,21 +301,18 @@
 def lookup_body(
     source_ref,
     target_ref,
-    rows_s_ref,
-    rows_t_ref,
-    rows_r_ref,
-    rows_n_ref,
+    bucket_ref,
     subject_ref,
     objects_ref,
     pick_r_ref,
     count_ref,
 ):
-    pick_s = one_hot(BLOCK, rows_s_ref[:, SPAN : 2 * SPAN])
-    pick_t = one_hot(BLOCK, rows_t_ref[:, SPAN : 2 * SPAN])
+    pick_s = one_hot(BLOCK, listed(bucket_ref, 0, 1))
+    pick_t = one_hot(BLOCK, listed(bucket_ref, 1, 1))
     subject_ref[...] = dot(source_ref[...].astype(bf16), pick_s)
     objects_ref[...] = dot(target_ref[...].astype(bf16), pick_t)
-    pick_r_ref[...] = one_hot(NREL, rows_r_ref[:, SPAN : 2 * SPAN])
-    count_ref[...] = counted(rows_n_ref[:, NEG : 2 * NEG])
+    pick_r_ref[...] = one_hot(NREL, listed(bucket_ref, 2, 1))
+    count_ref[...] = counted(listed(bucket_ref, 3, 1))
 
 
 def relation_update(mine, part_ref, other_ref, relations_ref, state_ref, out, state_out, flat_ref):
@@ -310,7 +328,6 @@
 
 def second_body(
     mine_ref,
-    live_ref,
     partner_ref,
     part_ref,
     other_ref,
@@ -324,10 +341,8 @@
     objects_ref,
     pick_r_ref,
     count_ref,
-    rows_s_ref,
-    rows_t_ref,
+    bucket_ref,
     source_out,
-    source_state_out,
     relations_out,
     relation_state_out,
     keep_out,
@@ -355,7 +370,7 @@
     target = target_ref[...]
     noise = gradients(
         SPAN,
-        live_ref[0, 0],
+        bucket_ref,
         target,
         pick_r,
         count_ref[...],
@@ -368,12 +383,12 @@
         subject_ref,
     )
     halves(mine, flat_ref, keep_out, give_out)
-    pick_s = one_hot(BLOCK, rows_s_ref[:, SPAN : 2 * SPAN])
-    pick_t = one_hot(BLOCK, rows_t_ref[:, SPAN : 2 * SPAN])
+    pick_s = one_hot(BLOCK, listed(bucket_ref, 0, 1))
+    pick_t = one_hot(BLOCK, listed(bucket_ref, 1, 1))
     grad_source = dot_last(subject_ref[...].astype(bf16), pick_s)
-    source_out[...], source_state_out[...] = stepped(
-        source_ref[...], source_state_ref[...], grad_source
-    )
+    source, source_state = stepped(source_ref[...], source_state_ref[...], grad_source)
+    source_out[0:DIM, :] = source
+    source_out[DIM : DIM + 8, :] = jnp.broadcast_to(source_state, (8, LANES))
     grad_target = dot_last(query_ref[...].astype(bf16), pick_t) + noise
     target, target_state = stepped(target, target_state_ref[...], grad_target)
     for k in range(PIECE):
@@ -405,19 +420,15 @@
     return pltpu.roll(value, LANES // 2, 1)
 
 
-def join_body(keep_ref, got_ref, sums_ref, block_ref):
-    sums_ref[...] = keep_ref[0:HALF_FLAT, :] + got_ref[0:HALF_FLAT, :]
-    full = 64 * FULL
-    block_ref[0:full, :] = keep_ref[HALF_FLAT : HALF_FLAT + full, :]
-    block_ref[full : 2 * full, :] = got_ref[HALF_FLAT : HALF_FLAT + full, :]
-    block_ref[2 * full :, :] = jnp.where(
-        low_lanes((64, LANES)), keep_ref[HALF_FLAT + full :, :], got_ref[HALF_FLAT + full :, :]
-    )
-
-
-def merge_body(received_ref, block_ref, out_ref):
-    for k in range(SUM_ROW):
-        out_ref[spaced(k, 64, ROWS), :] = block_ref[64 * k : 64 * (k + 1), :]
+def merge_body(received_ref, keep_ref, got_ref, out_ref):
+    for k in range(FULL):
+        rows = slice(HALF_FLAT + 64 * k, HALF_FLAT + 64 * (k + 1))
+        out_ref[spaced(k, 64, ROWS), :] = keep_ref[rows, :]
+        out_ref[spaced(FULL + k, 64, ROWS), :] = got_ref[rows, :]
+    rows = slice(HALF_FLAT + 64 * FULL, HALF_FLAT + 64 * PIECE)
+    out_ref[spaced(TAIL, 64, ROWS), :] = jnp.where(
+        low_lanes((64, LANES)), keep_ref[rows, :], got_ref[rows, :]
+    )
     for k in range(SUM_ROWS):
         rows = slice(64 * k, 64 * (k + 1))
         total = received_ref[0, rows, :] + received_ref[1, rows, :]
@@ -476,8 +487,20 @@
 
 
 def final_body(
-    mine_ref, part_ref, other_ref, relations_ref, state_ref, out_ref, state_out, flat_ref
+    mine_ref,
+    part_ref,
+    other_ref,
+    relations_ref,
+    state_ref,
+    source_ref,
+    out_ref,
+    state_out,
+    source_out,
+    source_state_out,
+    flat_ref,
 ):
+    source_out[...] = source_ref[0:DIM, :]
+    source_state_out[...] = source_ref[DIM : DIM + 1, :]
     relation_update(
         mine_ref[0, 0], part_ref, other_ref, relations_ref, state_ref, out_ref, state_out, flat_ref
     )
@@ -499,16 +522,24 @@
 ):
     mine = lax.axis_index("core").astype(jnp.int32).reshape(1, 1)
     turned = ((BLOCK, LANES), f32)
-    arriving = passed_along(dest_emb, "x", 1)
-    arriving_state = passed_along(dest_state.reshape(1, BLOCK), "x", 1)
+    partner = passed_along(partner, "x", -1)
     tile = ((BLOCK * PIECE, LANES), f32)
-    (cargo,) = kernel_call(pack_body, [tile], [partner, arriving, arriving_state], scalars=1)
+    (cargo,) = kernel_call(
+        pack_body, [tile], [partner, dest_emb, dest_state.reshape(1, -1)], scalars=1
+    )
+    lists = [
+        rows.reshape(1, -1) for rows in (source_rows, target_rows, relation_index, negative_rows)
+    ]
+    (bucket,) = kernel_call(
+        bucket_body,
+        [((BUCKET_ROWS, LANES), f32)],
+        [edge_count, source_emb, source_state.reshape(1, -1)] + lists,
+        scalars=1,
+    )
+    bucket = passed_along(bucket, "x", -1)
     spread = dealt(cargo, DOM, BLOCK)
     (spread,) = kernel_call(pick_body, [tile], [spread])
     arrived = dealt(spread, DOM, BLOCK)
-    lists = [
-        rows.reshape(1, -1) for rows in (source_rows, target_rows, relation_index, negative_rows)
-    ]
     block = ((DIM, BLOCK), f32)
     line = ((1, BLOCK), f32)
     half = ((HALF_FLAT, LANES), f32)
@@ -517,12 +548,12 @@
     source, source_acc, target, target_acc, keep, give = kernel_call(
         first_body,
         [block, line, block, line, half, half],
-        [mine, edge_count, arrived, source_emb, source_state.reshape(1, -1), relations] + lists,
+        [mine, arrived, bucket, relations],
         [WIDE] * 5 + [FLAT_TABLE],
-        scalars=2,
+        scalars=1,
     )
     subject, objects, pick_r, count = kernel_call(
-        lookup_body, [WIDE, WIDE, picks_r, square], [source, target] + lists
+        lookup_body, [WIDE, WIDE, picks_r, square], [source, target, bucket]
     )
     part = keep + passed_along(give, "core", 1)
     part = jnp.sum(exchange(part.reshape(4, 320, LANES), "x"), 0)
@@ -534,22 +565,22 @@
     table = ((DIM, NREL), f32)
     types = ((1, NREL), f32)
     longer = ((HALF_FLAT + 64 * PIECE, LANES), f32)
-    source, source_acc, relations, relation_acc, keep, give = kernel_call(
+    source, relations, relation_acc, keep, give = kernel_call(
         second_body,
-        [block, line, table, types, longer, longer],
-        [mine, edge_count, partner, part, other, source, source_acc, target, target_acc]
-        + [relations, relation_state.reshape(1, -1), subject, objects, pick_r, count]
-        + lists[:2],
+        [((DIM + 8, BLOCK), f32), table, types, longer, longer],
+        [mine, partner, part, other, source, source_acc, target, target_acc]
+        + [relations, relation_state.reshape(1, -1), subject, objects, pick_r, count, bucket],
         [WIDE] * 4 + [FLAT_TABLE, turned],
-        scalars=3,
+        scalars=2,
     )
     got = passed_along(give, "core", 1)
-    part, leaving = kernel_call(join_body, [half, ((64 * SUM_ROW, LANES), f32)], [keep, got])
-    leaving = passed_along(leaving, "x", -1)
+    source = passed_along(source, "x", 1)
+    part = keep[:HALF_FLAT] + got[:HALF_FLAT]
     received = exchange(part.reshape(4, 320, LANES), "x")
     packet = ((64 * ROWS, LANES), f32)
-    (packed,) = kernel_call(merge_body, [packet], [received, leaving])
+    (packed,) = kernel_call(merge_body, [packet], [received, keep, got])
     packed = packets(packed, ("z", "y"), 64)
+    packed, source = lax.optimization_barrier((packed, source))
     (packed,) = kernel_call(middle_body, [packet], [mine, packed], [turned], scalars=1)
     packed = packets(packed, ("z", "y"), 64)
     pieces = ((64 * PIECE, LANES), f32)
@@ -563,10 +594,10 @@
     )
     part, settled, settled_acc = lax.optimization_barrier((part, settled, settled_acc))
     other = passed_along(part, "core", 1)
-    relations, relation_acc = kernel_call(
+    relations, relation_acc, source, source_acc = kernel_call(
         final_body,
-        [table, types],
-        [mine, part, other, relations, relation_acc],
+        [table, types, block, line],
+        [mine, part, other, relations, relation_acc, source],
         [((FLAT, LANES), f32)],
         scalars=1,
     )

time: 230 us -> 230 us (level)
  waiting for transfers between devices: 33.4 us -> 29.8 us
    all_to_all x3, waiting for transfers between devices: 14.7 us -> 11.4 us  [exchange(): return lax.all_to_all(value, axis, split_axis=0, concat_axis=0, tiled=True)]
  transfers between devices with their start and end apart: 11 -> 11, of which waited for: 8 -> 10; matrix products, arithmetic and copies ran while one was open for 0% -> 0% of each run, Pallas kernels for 1% -> 1%
where the time goes in v4:
time: 230 us; the launch traced here: 229 us
  blocking collectives  128 us (56%)
  starting transfers between devices  52.9 us (23%)
  waiting for transfers between devices  29.8 us (13%)
  Pallas kernels  14.7 us (6%)
    all_to_all x8, blocking collectives, exchange(): return lax.all_to_all(value, axis, split_axis=0, concat_axis=0, tiled=True)  128 us
    ppermute x8, starting transfers between devices, passed_along(): return lax.ppermute(value, axis, pairs)  39.1 us
    ppermute x8, waiting for transfers between devices, passed_along(): return lax.ppermute(value, axis, pairs)  18.3 us
    pallas_call x11, Pallas kernels, kernel_call(): pl.pallas_call(body, out_shape=[jax.ShapeDtypeStruct(shape, dtype) for sh...  14.7 us
    all_to_all x3, starting transfers between devices, exchange(): return lax.all_to_all(value, axis, split_axis=0, concat_axis=0, tiled=True)  13.8 us
    all_to_all x3, waiting for transfers between devices, exchange(): return lax.all_to_all(value, axis, split_axis=0, concat_axis=0, tiled=True)  11.4 us
  transfers between devices with their start and end apart: 11, of which 10 were waited for; matrix products, arithmetic and copies ran while one was open for 0% of the time, Pallas kernels for 1%

profile of v4, /device:TPU:1, one launch (start us, length us, event | category | flops | bytes accessed | tf_op | source)
XLA Modules:
  0.0 229.0 jit_solution(15434771778843813868)
XLA Ops:
  0.6 5.2 %collective-permute-start = (s32[1,1]{1,0:T(1,128)}, s32[1,1]{1,0:T(1,128)}, u32[]{:S(2)}, u32[]{:S(2)}) collective-permute-start(s32[1,1]{1,0:T(1,128)} %param.18), channel_id=1, source_target_pairs={{0,3},{1,0},{2,1},{3,2},{4,7},{5,4},{6,5},{7,6},{8,11},{9,8},{10,9... | collective-permute-start | bytes 20 | tf_op jit(solution)/shard_map/ppermute | solution.py:34
  9.3 33.5 %all_to_all.55 = f32[128,4,128]{2,1,0:T(4,128)S(1)} all-to-all(f32[128,4,128]{2,1,0:T(4,128)S(1)} %bitcast.31), channel_id=1, replica_groups=mesh['z'=8,'y'=8,'core'=2,'x'=4] {'z','y','core'}, dimensions={0} | all-to-all | bytes 524288 | tf_op jit(solution)/shard_map/all_to_all | solution.py:38
  42.8 1.0 shard_map.164
  43.8 5.5 %all-to-all-start.1 = ((f32[128,4,128]{2,1,0:T(4,128)}), f32[128,4,128]{2,1,0:T(4,128)S(1)}, u32[]{:S(2)}, u32[]{:S(2)}) async-start(f32[128,4,128]{2,1,0:T(4,128)} %bitcast.4), calls=%async_computation.1 | async-start | bytes 524288 | tf_op jit(solution)/shard_map/all_to_all | solution.py:38
  50.1 5.0 %collective-permute-start.1 = (f32[448,128]{1,0:T(8,128)S(1)}, f32[448,128]{1,0:T(8,128)S(1)}, u32[]{:S(2)}, u32[]{:S(2)}) collective-permute-start(f32[448,128]{1,0:T(8,128)S(1)} %shard_map.165), channel_id=1, source_target_pairs={{0,3},{1,0},{2,1},{3,2},{4,7},{5,4},{6,5},{7,6},{8,11},{9,8},{10,9... | collective-permute-start | bytes 688136 | tf_op jit(solution)/shard_map/ppermute | solution.py:34
  55.1 3.9 %collective-permute-done.1.bucket_ref = f32[448,128]{1,0:T(8,128)S(1)} collective-permute-done((f32[448,128]{1,0:T(8,128)S(1)}, f32[448,128]{1,0:T(8,128)S(1)}, u32[]{:S(2)}, u32[]{:S(2)}) %collective-permute-start.1) | collective-permute-done | bytes 229408 | tf_op jit(solution)/shard_map/ppermute | solution.py:34
  59.0 5.7 %all-to-all-done.1 = f32[128,4,128]{2,1,0:T(4,128)S(1)} async-done(((f32[128,4,128]{2,1,0:T(4,128)}), f32[128,4,128]{2,1,0:T(4,128)S(1)}, u32[]{:S(2)}, u32[]{:S(2)}) %all-to-all-start.1) | async-done | bytes 262176 | tf_op jit(solution)/shard_map/all_to_all | solution.py:38
  64.7 3.2 %shard_map.166 = (f32[400,128]{1,0:T(8,128)S(1)}, f32[1,128]{1,0:T(1,128)S(1)}, f32[400,128]{1,0:T(8,128)S(1)}, f32[1,128]{1,0:T(1,128)S(1)}, f32[1280,128]{1,0:T(8,128)S(1)}, /*index=5*/f32[1280,128]{1,0:T(8,128)S(1)}) custom-call(s32[1,1]{1,0:T(1,128)} %bitcast.mine_ref, f32[512,128]{1,0:T(8,128)S(1)} %bitcast.30, ...), custom_call_target="tpu_custom_call" | custom-call | tf_op jit(solution)/shard_map/pallas_call | solution.py:60
  67.9 2.3 collective-permute-start.2
  70.2 1.7 collective-permute-done.2
  72.0 14.2 %all_to_all.56 = f32[4,320,128]{2,1,0:T(8,128)S(1)} all-to-all(f32[4,320,128]{2,1,0:T(8,128)S(1)} %bitcast.39), channel_id=1, replica_groups=mesh['z'=8,'y'=8,'core'=2,'x'=4] {'x'}, dimensions={0} | all-to-all | bytes 1310720 | tf_op jit(solution)/shard_map/all_to_all | solution.py:38
  86.2 11.0 %all_to_all.57 = f32[8,40,128]{2,1,0:T(8,128)S(1)} all-to-all(f32[8,40,128]{2,1,0:T(8,128)S(1)} %bitcast.41), channel_id=1, replica_groups=mesh['z'=8,'y'=8,'core'=2,'x'=4] {'y'}, dimensions={0} | all-to-all | bytes 327680 | tf_op jit(solution)/shard_map/all_to_all | solution.py:38
  97.3 14.9 %all_to_all.58 = f32[8,40,128]{2,1,0:T(8,128)S(1)} all-to-all(f32[8,40,128]{2,1,0:T(8,128)S(1)} %broadcast_in_dim.8), channel_id=1, replica_groups=mesh['z'=8,'y'=8,'core'=2,'x'=4] {'z'}, dimensions={0} | all-to-all | bytes 327680 | tf_op jit(solution)/shard_map/all_to_all | solution.py:38
  112.2 10.7 %all_to_all.59 = f32[8,40,128]{2,1,0:T(8,128)S(1)} all-to-all(f32[8,40,128]{2,1,0:T(8,128)S(1)} %broadcast_in_dim.9), channel_id=1, replica_groups=mesh['z'=8,'y'=8,'core'=2,'x'=4] {'y'}, dimensions={0} | all-to-all | bytes 327680 | tf_op jit(solution)/shard_map/all_to_all | solution.py:38
  122.9 10.0 %all_to_all.60 = f32[4,320,128]{2,1,0:T(8,128)S(1)} all-to-all(f32[4,320,128]{2,1,0:T(8,128)S(1)} %broadcast_in_dim.22), channel_id=1, replica_groups=mesh['z'=8,'y'=8,'core'=2,'x'=4] {'x'}, dimensions={0} | all-to-all | bytes 1310720 | tf_op jit(solution)/shard_map/all_to_all | solution.py:38
  133.0 8.7 %collective-permute-start.3 = (f32[1280,128]{1,0:T(8,128)S(1)}, f32[1280,128]{1,0:T(8,128)S(1)}, u32[]{:S(2)}, u32[]{:S(2)}) collective-permute-start(f32[1280,128]{1,0:T(8,128)S(1)} %bitcast.25), channel_id=1, source_target_pairs={{0,4},{4,0},{1,5},{5,1},{2,6},{6,2},{3,7},{7,3},{8,12},{12,8},{9,1... | collective-permute-start | bytes 1966088 | tf_op jit(solution)/shard_map/ppermute | solution.py:34
  142.3 1.0 collective-permute-done.3.other_ref
  143.4 3.9 %shard_map.168 = (f32[408,128]{1,0:T(8,128)S(1)}, f32[400,768]{1,0:T(8,128)S(1)}, f32[1,768]{1,0:T(1,128)S(1)}, f32[1536,128]{1,0:T(8,128)S(1)}, f32[1536,128]{1,0:T(8,128)S(1)}) custom-call(s32[1,1]{1,0:T(1,128)} %bitcast.mine_ref, s32[1,1]{1,0:T(1,128)} %collective-permute-done.partner_ref, f32[1280,128]{1,0:T(8,128)S(1)} %bitcast.26, ...), custom_call_target="tpu_custom_call" | custom-call | tf_op jit(solution)/shard_map/pallas_call | solution.py:60
  147.2 2.3 collective-permute-start.4
  149.5 1.9 collective-permute-done.4.got_ref
  151.5 13.0 %all_to_all.61.received_ref = f32[4,320,128]{2,1,0:T(8,128)S(1)} all-to-all(f32[4,320,128]{2,1,0:T(8,128)S(1)} %bitcast.40), channel_id=1, replica_groups=mesh['z'=8,'y'=8,'core'=2,'x'=4] {'x'}, dimensions={0} | all-to-all | bytes 1310720 | tf_op jit(solution)/shard_map/all_to_all | solution.py:38
  165.3 4.8 %all-to-all-start.8 = ((f32[64,3,4,128]{3,2,1,0:T(4,128)}), f32[64,3,4,128]{3,2,1,0:T(4,128)S(1)}, u32[]{:S(2)}, u32[]{:S(2)}) async-start(f32[64,3,4,128]{3,2,1,0:T(4,128)} %bitcast.16), calls=%async_computation.8 | async-start | bytes 786432 | tf_op jit(solution)/shard_map/all_to_all | solution.py:38
  170.1 2.2 collective-permute-start.5
  172.3 6.4 %collective-permute-done.5.source_ref = f32[408,128]{1,0:T(8,128)S(1)} collective-permute-done((f32[408,128]{1,0:T(8,128)S(1)}, f32[408,128]{1,0:T(8,128)S(1)}, u32[]{:S(2)}, u32[]{:S(2)}) %collective-permute-start.5) | collective-permute-done | bytes 208928 | tf_op jit(solution)/shard_map/ppermute | solution.py:34
  178.7 5.7 %all-to-all-done.8 = f32[64,3,4,128]{3,2,1,0:T(4,128)S(1)} async-done(((f32[64,3,4,128]{3,2,1,0:T(4,128)}), f32[64,3,4,128]{3,2,1,0:T(4,128)S(1)}, u32[]{:S(2)}, u32[]{:S(2)}) %all-to-all-start.8) | async-done | bytes 393248 | tf_op jit(solution)/shard_map/all_to_all | solution.py:38
  184.4 1.0 shard_map.170
  185.4 20.2 %all_to_all.62 = f32[64,3,4,128]{3,2,1,0:T(4,128)S(1)} all-to-all(f32[64,3,4,128]{3,2,1,0:T(4,128)S(1)} %bitcast.29), channel_id=1, replica_groups=mesh['z'=8,'y'=8,'core'=2,'x'=4] {'z','y'}, dimensions={0} | all-to-all | bytes 786432 | tf_op jit(solution)/shard_map/all_to_all | solution.py:38
  206.5 3.5 %all-to-all-start.10 = ((f32[4,320,128]{2,1,0:T(8,128)}), f32[4,320,128]{2,1,0:T(8,128)S(1)}, u32[]{:S(2)}, u32[]{:S(2)}) async-start(f32[4,320,128]{2,1,0:T(8,128)} %get-tuple-element.49), calls=%async_computation.10 | async-start | bytes 1310720 | tf_op jit(solution)/shard_map/all_to_all | solution.py:38
  210.0 6.5 %collective-permute-start.6 = (f32[256,128]{1,0:T(8,128)S(1)}, f32[256,128]{1,0:T(8,128)S(1)}, u32[]{:S(2)}, u32[]{:S(2)}) collective-permute-start(f32[256,128]{1,0:T(8,128)S(1)} %get-tuple-element.51), channel_id=1, source_target_pairs={{0,4},{4,0},{1,5},{5,1},{2,6},{6,2},{3,7},{7,3},{8,12},{12,8},{9,1... | collective-permute-start | bytes 393224 | tf_op jit(solution)/shard_map/ppermute | solution.py:34
  218.3 6.9 %collective-permute-start.7 = (f32[1280,128]{1,0:T(8,128)S(1)}, f32[1280,128]{1,0:T(8,128)S(1)}, u32[]{:S(2)}, u32[]{:S(2)}) collective-permute-start(f32[1280,128]{1,0:T(8,128)S(1)} %bitcast.23), channel_id=1, source_target_pairs={{0,4},{4,0},{1,5},{5,1},{2,6},{6,2},{3,7},{7,3},{8,12},{12,8},{9,1... | collective-permute-start | bytes 1966088 | tf_op jit(solution)/shard_map/ppermute | solution.py:34
  225.2 1.7 collective-permute-done.7.other_ref
  226.9 1.5 shard_map.173
  (39 shorter events, 8.5 us)
Async XLA Ops:
  0.6 49.3 %copy-start.8 = (f32[128]{0:T(128)S(1)}, f32[128]{0:T(128)}, u32[]{:S(2)}) copy-start(f32[128]{0:T(128)} %param.13) | copy-start | bytes 1540
  0.6 6.1 %collective-permute-start = (s32[1,1]{1,0:T(1,128)}, s32[1,1]{1,0:T(1,128)}, u32[]{:S(2)}, u32[]{:S(2)}) collective-permute-start(s32[1,1]{1,0:T(1,128)} %param.18), channel_id=1, source_target_pairs={{0,3},{1,0},{2,1},{3,2},{4,7},{5,4},{6,5},{7,6},{8,11},{9,8},{10,9... | collective-permute-start | bytes 20 | tf_op jit(solution)/shard_map/ppermute | solution.py:34
  6.7 0.9 copy-start.1
  7.6 0.7 copy-start.7
  8.3 41.7 %copy-start.2 = (f32[400,128]{1,0:T(8,128)S(1)}, f32[400,128]{1,0:T(8,128)}, u32[]{:S(2)}) copy-start(f32[400,128]{1,0:T(8,128)} %source_ref.1) | copy-start | bytes 614404
  8.3 41.7 %copy-start.3 = (s32[1,1,2048]{2,1,0:T(1,128)S(1)}, s32[1,1,2048]{2,1,0:T(1,128)}, u32[]{:S(2)}) copy-start(s32[1,1,2048]{2,1,0:T(1,128)} %param.23) | copy-start | bytes 24580
  8.3 41.7 %copy-start.4 = (s32[1,1,1024]{2,1,0:T(1,128)S(1)}, s32[1,1,1024]{2,1,0:T(1,128)}, u32[]{:S(2)}) copy-start(s32[1,1,1024]{2,1,0:T(1,128)} %param.20) | copy-start | bytes 12292
  8.3 41.7 %copy-start.5 = (s32[1,1,1024]{2,1,0:T(1,128)S(1)}, s32[1,1,1024]{2,1,0:T(1,128)}, u32[]{:S(2)}) copy-start(s32[1,1,1024]{2,1,0:T(1,128)} %param.21) | copy-start | bytes 12292
  8.3 41.7 %copy-start.6 = (s32[1,1,1024]{2,1,0:T(1,128)S(1)}, s32[1,1,1024]{2,1,0:T(1,128)}, u32[]{:S(2)}) copy-start(s32[1,1,1024]{2,1,0:T(1,128)} %param.22) | copy-start | bytes 12292
  8.3 56.4 %copy-start = (f32[400,768]{1,0:T(8,128)S(1)}, f32[400,768]{1,0:T(8,128)}, u32[]{:S(2)}) copy-start(f32[400,768]{1,0:T(8,128)} %relations_ref.3) | copy-start | bytes 3686404
  43.8 20.9 %all-to-all-start.1 = ((f32[128,4,128]{2,1,0:T(4,128)}), f32[128,4,128]{2,1,0:T(4,128)S(1)}, u32[]{:S(2)}, u32[]{:S(2)}) async-start(f32[128,4,128]{2,1,0:T(4,128)} %bitcast.4), calls=%async_computation.1 | async-start | bytes 524288 | tf_op jit(solution)/shard_map/all_to_all | solution.py:38
  50.1 8.9 %collective-permute-start.1 = (f32[448,128]{1,0:T(8,128)S(1)}, f32[448,128]{1,0:T(8,128)S(1)}, u32[]{:S(2)}, u32[]{:S(2)}) collective-permute-start(f32[448,128]{1,0:T(8,128)S(1)} %shard_map.165), channel_id=1, source_target_pairs={{0,3},{1,0},{2,1},{3,2},{4,7},{5,4},{6,5},{7,6},{8,11},{9,8},{10,9... | collective-permute-start | bytes 688136 | tf_op jit(solution)/shard_map/ppermute | solution.py:34
  67.9 4.0 %collective-permute-start.2 = (f32[1280,128]{1,0:T(8,128)S(1)}, f32[1280,128]{1,0:T(8,128)S(1)}, u32[]{:S(2)}, u32[]{:S(2)}) collective-permute-start(f32[1280,128]{1,0:T(8,128)S(1)} %get-tuple-element.36), channel_id=1, source_target_pairs={{0,4},{4,0},{1,5},{5,1},{2,6},{6,2},{3,7},{7,3},{8,12},{12,8},{9,1... | collective-permute-start | bytes 1966088 | tf_op jit(solution)/shard_map/ppermute | solution.py:34
  112.2 29.4 %copy-start.9 = (f32[768]{0:T(1024)S(1)}, f32[768]{0:T(1024)}, u32[]{:S(2)}) copy-start(f32[768]{0:T(1024)} %param.17) | copy-start | bytes 9220
  133.0 10.4 %collective-permute-start.3 = (f32[1280,128]{1,0:T(8,128)S(1)}, f32[1280,128]{1,0:T(8,128)S(1)}, u32[]{:S(2)}, u32[]{:S(2)}) collective-permute-start(f32[1280,128]{1,0:T(8,128)S(1)} %bitcast.25), channel_id=1, source_target_pairs={{0,4},{4,0},{1,5},{5,1},{2,6},{6,2},{3,7},{7,3},{8,12},{12,8},{9,1... | collective-permute-start | bytes 1966088 | tf_op jit(solution)/shard_map/ppermute | solution.py:34
  147.2 4.2 %collective-permute-start.4 = (f32[1536,128]{1,0:T(8,128)S(1)}, f32[1536,128]{1,0:T(8,128)S(1)}, u32[]{:S(2)}, u32[]{:S(2)}) collective-permute-start(f32[1536,128]{1,0:T(8,128)S(1)} %get-tuple-element.46), channel_id=1, source_target_pairs={{0,4},{4,0},{1,5},{5,1},{2,6},{6,2},{3,7},{7,3},{8,12},{12,8},{9,1... | collective-permute-start | bytes 2359304 | tf_op jit(solution)/shard_map/ppermute | solution.py:34
  165.3 19.1 %all-to-all-start.8 = ((f32[64,3,4,128]{3,2,1,0:T(4,128)}), f32[64,3,4,128]{3,2,1,0:T(4,128)S(1)}, u32[]{:S(2)}, u32[]{:S(2)}) async-start(f32[64,3,4,128]{3,2,1,0:T(4,128)} %bitcast.16), calls=%async_computation.8 | async-start | bytes 786432 | tf_op jit(solution)/shard_map/all_to_all | solution.py:38
  170.1 8.6 %collective-permute-start.5 = (f32[408,128]{1,0:T(8,128)S(1)}, f32[408,128]{1,0:T(8,128)S(1)}, u32[]{:S(2)}, u32[]{:S(2)}) collective-permute-start(f32[408,128]{1,0:T(8,128)S(1)} %get-tuple-element.47), channel_id=1, source_target_pairs={{0,1},{1,2},{2,3},{3,0},{4,5},{5,6},{6,7},{7,4},{8,9},{9,10},{10,1... | collective-permute-start | bytes 626696 | tf_op jit(solution)/shard_map/ppermute | solution.py:34
  206.5 11.8 %all-to-all-start.10 = ((f32[4,320,128]{2,1,0:T(8,128)}), f32[4,320,128]{2,1,0:T(8,128)S(1)}, u32[]{:S(2)}, u32[]{:S(2)}) async-start(f32[4,320,128]{2,1,0:T(8,128)} %get-tuple-element.49), calls=%async_computation.10 | async-start | bytes 1310720 | tf_op jit(solution)/shard_map/all_to_all | solution.py:38
  210.0 7.5 %collective-permute-start.6 = (f32[256,128]{1,0:T(8,128)S(1)}, f32[256,128]{1,0:T(8,128)S(1)}, u32[]{:S(2)}, u32[]{:S(2)}) collective-permute-start(f32[256,128]{1,0:T(8,128)S(1)} %get-tuple-element.51), channel_id=1, source_target_pairs={{0,4},{4,0},{1,5},{5,1},{2,6},{6,2},{3,7},{7,3},{8,12},{12,8},{9,1... | collective-permute-start | bytes 393224 | tf_op jit(solution)/shard_map/ppermute | solution.py:34
  218.3 8.6 %collective-permute-start.7 = (f32[1280,128]{1,0:T(8,128)S(1)}, f32[1280,128]{1,0:T(8,128)S(1)}, u32[]{:S(2)}, u32[]{:S(2)}) collective-permute-start(f32[1280,128]{1,0:T(8,128)S(1)} %bitcast.23), channel_id=1, source_target_pairs={{0,4},{4,0},{1,5},{5,1},{2,6},{6,2},{3,7},{7,3},{8,12},{12,8},{9,1... | collective-permute-start | bytes 1966088 | tf_op jit(solution)/shard_map/ppermute | solution.py:34

commit v5 on v4

--- a/solution.py
+++ b/solution.py
@@ -101,14 +101,21 @@
     return pl.ds(start, size, stride=stride)
 
 
-def pack_body(partner_ref, dest_ref, state_ref, out_ref):
+def pack_body(dest_ref, state_ref, out_ref):
     for k in range(PIECE - 1):
         out_ref[spaced(k, BLOCK, PIECE), :] = dest_ref[LANES * k : LANES * (k + 1), :].T
     tail = dest_ref[LANES * (PIECE - 1) : DIM, :]
     state = jnp.broadcast_to(state_ref[...], (8, LANES))
-    own = jnp.full((8, LANES), partner_ref[0, 0].astype(f32))
-    zero = jnp.zeros((LANES - tail.shape[0] - 16, LANES), f32)
-    out_ref[spaced(PIECE - 1, BLOCK, PIECE), :] = jnp.concatenate([tail, state, own, zero], 0).T
+    zero = jnp.zeros((LANES - tail.shape[0] - 8, LANES), f32)
+    out_ref[spaced(PIECE - 1, BLOCK, PIECE), :] = jnp.concatenate([tail, state, zero], 0).T
+
+
+def stamp_body(partner_ref, cargo_ref, out_ref):
+    rows = spaced(PIECE - 1, BLOCK, PIECE)
+    lane = lax.broadcasted_iota(jnp.int32, (BLOCK, LANES), 1)
+    own = partner_ref[0, 0].astype(f32)
+    out_ref[...] = cargo_ref[...]
+    out_ref[rows, :] = jnp.where(lane == OWN_LANE, own, cargo_ref[rows, :])
 
 
 STATE_ROW = DIM
@@ -163,6 +170,33 @@
     re = pl.ds(pl.multiple_of(8 * i, 8), 8)
     im = pl.ds(pl.multiple_of(HALF + 8 * i, 8), 8)
     return re, im
+
+
+HALF_CHUNKS = CHUNKS // 2
+HALF_REL = NREL // 2
+
+
+def flat_row(chunk):
+    return HALF_FLAT * (chunk // HALF_CHUNKS) + DIM * (chunk % HALF_CHUNKS)
+
+
+def half_update(grad_ref, param_of, state_of, out_ref, state_out):
+    for k in range(HALF_CHUNKS):
+        lanes = slice(LANES * k, LANES * (k + 1))
+        grad = grad_ref[DIM * k : DIM * (k + 1), :]
+        out_ref[:, lanes], state_out[:, lanes] = stepped(param_of(k), state_of(k), grad)
+
+
+def chunk_reader(ref, which):
+    def read(k):
+        first = pl.multiple_of(which * HALF_REL + LANES * k, LANES)
+        return ref[:, pl.ds(first, LANES)]
+
+    return read
+
+
+def static_reader(ref):
+    return lambda k: ref[:, LANES * k : LANES * (k + 1)]
 
 
 def gradients(
@@ -225,9 +259,12 @@
     grad_operator = operator_ref[...].astype(bf16)
     for k in range(0, CHUNKS, 2):
         pair = dot_last(grad_operator, pick_r[LANES * k : LANES * (k + 2), :])
-        flat_ref[DIM * k : DIM * (k + 1), :] = pair[:, :LANES]
-        flat_ref[DIM * (k + 1) : DIM * (k + 2), :] = pair[:, LANES:]
-    flat_ref[DIM * CHUNKS : FLAT, :] = jnp.zeros((FLAT - DIM * CHUNKS, LANES), f32)
+        for c in range(2):
+            first = flat_row(k + c)
+            flat_ref[first : first + DIM, :] = pair[:, LANES * c : LANES * (c + 1)]
+    rest = HALF_FLAT - DIM * HALF_CHUNKS
+    for h in range(1, 3):
+        flat_ref[HALF_FLAT * h - rest : HALF_FLAT * h, :] = jnp.zeros((rest, LANES), f32)
     return noise
 
 
@@ -247,16 +284,16 @@
     arrived_ref,
     bucket_ref,
     relations_ref,
-    source_out,
-    source_state_out,
+    grad_subject_ref,
+    query_ref,
     target_out,
     target_state_out,
+    noise_out,
     keep_out,
     give_out,
     subject_ref,
     operator_ref,
     objects_ref,
-    query_ref,
     slope_ref,
     flat_ref,
 ):
@@ -273,7 +310,7 @@
     subject_ref[...] = dot(source.astype(bf16), pick_s)
     operator_ref[...] = dot(relations_ref[...].astype(bf16), pick_r)
     objects_ref[...] = dot(target.astype(bf16), pick_t)
-    noise = gradients(
+    noise_out[...] = gradients(
         0,
         bucket_ref,
         target,
@@ -285,20 +322,50 @@
         query_ref,
         slope_ref,
         flat_ref,
-        subject_ref,
+        grad_subject_ref,
     )
     halves(mine_ref[0, 0], flat_ref, keep_out, give_out)
-    grad_source = dot_last(subject_ref[...].astype(bf16), pick_s)
+    target_out[...] = target
+    target_state_out[...] = last[STATE_LANE : STATE_LANE + 1, :]
+
+
+def update_body(
+    bucket_ref,
+    grad_subject_ref,
+    grad_objects_ref,
+    target_ref,
+    target_state_ref,
+    noise_ref,
+    source_out,
+    source_state_out,
+    target_out,
+    target_state_out,
+):
+    pick_s = one_hot(BLOCK, listed(bucket_ref, 0, 0))
+    pick_t = one_hot(BLOCK, listed(bucket_ref, 1, 0))
+    grad_source = dot_last(grad_subject_ref[...].astype(bf16), pick_s)
     source_out[...], source_state_out[...] = stepped(
-        source, bucket_ref[STATE_ROW : STATE_ROW + 1, :], grad_source
-    )
-    grad_target = dot_last(query_ref[...].astype(bf16), pick_t) + noise
+        bucket_ref[0:DIM, :], bucket_ref[STATE_ROW : STATE_ROW + 1, :], grad_source
+    )
+    grad_target = dot_last(grad_objects_ref[...].astype(bf16), pick_t) + noise_ref[...]
     target_out[...], target_state_out[...] = stepped(
-        target, last[STATE_LANE : STATE_LANE + 1, :], grad_target
-    )
+        target_ref[...], target_state_ref[...], grad_target
+    )
+
+
+def last_source_body(bucket_ref, grad_subject_ref, source_ref, source_state_ref, source_out):
+    pick_s = one_hot(BLOCK, listed(bucket_ref, 0, 1))
+    grad_source = dot_last(grad_subject_ref[...].astype(bf16), pick_s)
+    source, source_state = stepped(source_ref[...], source_state_ref[...], grad_source)
+    source_out[0:DIM, :] = source
+    source_out[DIM : DIM + 8, :] = jnp.broadcast_to(source_state, (8, LANES))
 
 
 def lookup_body(
+    mine_ref,
+    part_ref,
+    relations_ref,
+    relation_state_ref,
     source_ref,
     target_ref,
     bucket_ref,
@@ -306,7 +373,17 @@
     objects_ref,
     pick_r_ref,
     count_ref,
+    own_ref,
+    own_state_ref,
 ):
+    mine = mine_ref[0, 0]
+    half_update(
+        part_ref,
+        chunk_reader(relations_ref, mine),
+        chunk_reader(relation_state_ref, mine),
+        own_ref,
+        own_state_ref,
+    )
     pick_s = one_hot(BLOCK, listed(bucket_ref, 0, 1))
     pick_t = one_hot(BLOCK, listed(bucket_ref, 1, 1))
     subject_ref[...] = dot(source_ref[...].astype(bf16), pick_s)
@@ -315,24 +392,11 @@
     count_ref[...] = counted(listed(bucket_ref, 3, 1))
 
 
-def relation_update(mine, part_ref, other_ref, relations_ref, state_ref, out, state_out, flat_ref):
-    flat_ref[pl.ds(pl.multiple_of(mine * HALF_FLAT, 8), HALF_FLAT), :] = part_ref[...]
-    flat_ref[pl.ds(pl.multiple_of((1 - mine) * HALF_FLAT, 8), HALF_FLAT), :] = other_ref[...]
-    for k in range(CHUNKS):
-        lanes = slice(LANES * k, LANES * (k + 1))
-        grad = flat_ref[DIM * k : DIM * (k + 1), :]
-        new, new_state = stepped(relations_ref[:, lanes], state_ref[:, lanes], grad)
-        out[:, lanes] = new
-        state_out[:, lanes] = new_state
-
-
 def second_body(
     mine_ref,
     partner_ref,
-    part_ref,
+    own_ref,
     other_ref,
-    source_ref,
-    source_state_ref,
     target_ref,
     target_state_ref,
     relations_ref,
@@ -342,12 +406,11 @@
     pick_r_ref,
     count_ref,
     bucket_ref,
-    source_out,
-    relations_out,
-    relation_state_out,
+    subject_ref,
+    far_out,
+    far_state_out,
     keep_out,
     give_out,
-    subject_ref,
     operator_ref,
     query_ref,
     slope_ref,
@@ -355,24 +418,24 @@
     turned_ref,
 ):
     mine = mine_ref[0, 0]
-    relation_update(
-        mine,
-        part_ref,
+    half_update(
         other_ref,
-        relations_ref,
-        relation_state_ref,
-        relations_out,
-        relation_state_out,
-        flat_ref,
-    )
-    pick_r = pick_r_ref[...]
-    operator_ref[...] = dot(relations_out[...].astype(bf16), pick_r)
+        chunk_reader(relations_ref, 1 - mine),
+        chunk_reader(relation_state_ref, 1 - mine),
+        far_out,
+        far_state_out,
+    )
+    near_rows = pl.ds(pl.multiple_of(mine * HALF_REL, LANES), HALF_REL)
+    far_rows = pl.ds(pl.multiple_of((1 - mine) * HALF_REL, LANES), HALF_REL)
+    operator_ref[...] = dot(own_ref[...].astype(bf16), pick_r_ref[near_rows, :]) + dot(
+        far_out[...].astype(bf16), pick_r_ref[far_rows, :]
+    )
     target = target_ref[...]
     noise = gradients(
         SPAN,
         bucket_ref,
         target,
-        pick_r,
+        pick_r_ref[...],
         count_ref[...],
         first_subject_ref,
         operator_ref,
@@ -383,12 +446,7 @@
         subject_ref,
     )
     halves(mine, flat_ref, keep_out, give_out)
-    pick_s = one_hot(BLOCK, listed(bucket_ref, 0, 1))
     pick_t = one_hot(BLOCK, listed(bucket_ref, 1, 1))
-    grad_source = dot_last(subject_ref[...].astype(bf16), pick_s)
-    source, source_state = stepped(source_ref[...], source_state_ref[...], grad_source)
-    source_out[0:DIM, :] = source
-    source_out[DIM : DIM + 8, :] = jnp.broadcast_to(source_state, (8, LANES))
     grad_target = dot_last(query_ref[...].astype(bf16), pick_t) + noise
     target, target_state = stepped(target, target_state_ref[...], grad_target)
     for k in range(PIECE):
@@ -486,24 +544,38 @@
             state_out[...] = turned[STATE_LANE : STATE_LANE + 1, :]
 
 
+def near_body(part_ref, near_ref, near_state_ref, out_ref, state_out):
+    half_update(
+        part_ref, static_reader(near_ref), static_reader(near_state_ref), out_ref, state_out
+    )
+
+
 def final_body(
     mine_ref,
-    part_ref,
+    near_ref,
+    near_state_ref,
     other_ref,
-    relations_ref,
-    state_ref,
+    far_ref,
+    far_state_ref,
     source_ref,
     out_ref,
     state_out,
     source_out,
     source_state_out,
-    flat_ref,
 ):
     source_out[...] = source_ref[0:DIM, :]
     source_state_out[...] = source_ref[DIM : DIM + 1, :]
-    relation_update(
-        mine_ref[0, 0], part_ref, other_ref, relations_ref, state_ref, out_ref, state_out, flat_ref
-    )
+    mine = mine_ref[0, 0]
+    for k in range(HALF_CHUNKS):
+        lanes = slice(LANES * k, LANES * (k + 1))
+        near = pl.ds(pl.multiple_of(mine * HALF_REL + LANES * k, LANES), LANES)
+        far = pl.ds(pl.multiple_of((1 - mine) * HALF_REL + LANES * k, LANES), LANES)
+        out_ref[:, near] = near_ref[:, lanes]
+        state_out[:, near] = near_state_ref[:, lanes]
+        grad = other_ref[DIM * k : DIM * (k + 1), :]
+        out_ref[:, far], state_out[:, far] = stepped(
+            far_ref[:, lanes], far_state_ref[:, lanes], grad
+        )
 
 
 def local(
@@ -524,9 +596,8 @@
     turned = ((BLOCK, LANES), f32)
     partner = passed_along(partner, "x", -1)
     tile = ((BLOCK * PIECE, LANES), f32)
-    (cargo,) = kernel_call(
-        pack_body, [tile], [partner, dest_emb, dest_state.reshape(1, -1)], scalars=1
-    )
+    (cargo,) = kernel_call(pack_body, [tile], [dest_emb, dest_state.reshape(1, -1)])
+    (cargo,) = kernel_call(stamp_body, [tile], [partner, cargo], scalars=1)
     lists = [
         rows.reshape(1, -1) for rows in (source_rows, target_rows, relation_index, negative_rows)
     ]
@@ -545,35 +616,54 @@
     half = ((HALF_FLAT, LANES), f32)
     picks_r = ((NREL, SPAN), bf16)
     square = ((BLOCK, BLOCK), f32)
-    source, source_acc, target, target_acc, keep, give = kernel_call(
+    half_table = ((DIM, HALF_REL), f32)
+    half_types = ((1, HALF_REL), f32)
+    relation_acc = relation_state.reshape(1, -1)
+    grad_subject, grad_objects, target, target_acc, noise, keep, give = kernel_call(
         first_body,
-        [block, line, block, line, half, half],
+        [WIDE, WIDE, block, line, block, half, half],
         [mine, arrived, bucket, relations],
-        [WIDE] * 5 + [FLAT_TABLE],
+        [WIDE] * 4 + [FLAT_TABLE],
         scalars=1,
     )
-    subject, objects, pick_r, count = kernel_call(
-        lookup_body, [WIDE, WIDE, picks_r, square], [source, target, bucket]
-    )
-    part = keep + passed_along(give, "core", 1)
+    source, source_acc, target, target_acc = kernel_call(
+        update_body,
+        [block, line, block, line],
+        [bucket, grad_subject, grad_objects, target, target_acc, noise],
+    )
+    got, source, source_acc, target, target_acc = lax.optimization_barrier(
+        (passed_along(give, "core", 1), source, source_acc, target, target_acc)
+    )
+    part = keep + got
     part = jnp.sum(exchange(part.reshape(4, 320, LANES), "x"), 0)
     part = jnp.sum(exchange(part.reshape(8, 40, LANES), "y"), 0)
     part = jnp.sum(gathered(part, "z"), 0)
     part = gathered(part, "y").reshape(320, LANES)
     part = gathered(part, "x").reshape(HALF_FLAT, LANES)
     other = passed_along(part, "core", 1)
+    subject, objects, pick_r, count, near, near_acc = kernel_call(
+        lookup_body,
+        [WIDE, WIDE, picks_r, square, half_table, half_types],
+        [mine, part, relations, relation_acc, source, target, bucket],
+        scalars=1,
+    )
     table = ((DIM, NREL), f32)
     types = ((1, NREL), f32)
     longer = ((HALF_FLAT + 64 * PIECE, LANES), f32)
-    source, relations, relation_acc, keep, give = kernel_call(
+    grad_subject, far, far_acc, keep, give = kernel_call(
         second_body,
-        [((DIM + 8, BLOCK), f32), table, types, longer, longer],
-        [mine, partner, part, other, source, source_acc, target, target_acc]
-        + [relations, relation_state.reshape(1, -1), subject, objects, pick_r, count, bucket],
-        [WIDE] * 4 + [FLAT_TABLE, turned],
+        [WIDE, half_table, half_types, longer, longer],
+        [mine, partner, near, other, target, target_acc, relations, relation_acc]
+        + [subject, objects, pick_r, count, bucket],
+        [WIDE] * 3 + [FLAT_TABLE, turned],
         scalars=2,
     )
-    got = passed_along(give, "core", 1)
+    (source,) = kernel_call(
+        last_source_body,
+        [((DIM + 8, BLOCK), f32)],
+        [bucket, grad_subject, source, source_acc],
+    )
+    got, source = lax.optimization_barrier((passed_along(give, "core", 1), source))
     source = passed_along(source, "x", 1)
     part = keep[:HALF_FLAT] + got[:HALF_FLAT]
     received = exchange(part.reshape(4, 320, LANES), "x")
@@ -594,11 +684,11 @@
     )
     part, settled, settled_acc = lax.optimization_barrier((part, settled, settled_acc))
     other = passed_along(part, "core", 1)
+    near, near_acc = kernel_call(near_body, [half_table, half_types], [part, near, near_acc])
     relations, relation_acc, source, source_acc = kernel_call(
         final_body,
         [table, types, block, line],
-        [mine, part, other, relations, relation_acc, source],
-        [((FLAT, LANES), f32)],
+        [mine, near, near_acc, other, far, far_acc, source],
         scalars=1,
     )
     return (

time: 230 us -> 227 us (0.987)
    pallas_call x11 -> x15, Pallas kernels: 14.7 us -> 15.1 us  [kernel_call(): pl.pallas_call(body, out_shape=[jax.ShapeDtypeStruct(shape, dtype) for sh...]
  transfers between devices with their start and end apart: 11 -> 11, of which waited for: 10 -> 9; matrix products, arithmetic and copies ran while one was open for 0% -> 0% of each run, Pallas kernels for 1% -> 1%
where the time goes in v5:
time: 227 us
  blocking collectives  127 us (56%)
  starting transfers between devices  52.6 us (23%)
  waiting for transfers between devices  28.1 us (12%)
  Pallas kernels  15.1 us (7%)
    all_to_all x8, blocking collectives, exchange(): return lax.all_to_all(value, axis, split_axis=0, concat_axis=0, tiled=True)  127 us
    ppermute x8, starting transfers between devices, passed_along(): return lax.ppermute(value, axis, pairs)  38.8 us
    ppermute x8, waiting for transfers between devices, passed_along(): return lax.ppermute(value, axis, pairs)  16.3 us
    pallas_call x15, Pallas kernels, kernel_call(): pl.pallas_call(body, out_shape=[jax.ShapeDtypeStruct(shape, dtype) for sh...  15.1 us
    all_to_all x3, starting transfers between devices, exchange(): return lax.all_to_all(value, axis, split_axis=0, concat_axis=0, tiled=True)  13.8 us
    all_to_all x3, waiting for transfers between devices, exchange(): return lax.all_to_all(value, axis, split_axis=0, concat_axis=0, tiled=True)  11.8 us
  transfers between devices with their start and end apart: 11, of which 9 were waited for; matrix products, arithmetic and copies ran while one was open for 0% of the time, Pallas kernels for 1%

profile of v5, /device:TPU:1, one launch (start us, length us, event | category | flops | bytes accessed | tf_op | source)
XLA Modules:
  0.0 226.6 jit_solution(8986402950265434318)
XLA Ops:
  0.6 5.2 %collective-permute-start = (s32[1,1]{1,0:T(1,128)}, s32[1,1]{1,0:T(1,128)}, u32[]{:S(2)}, u32[]{:S(2)}) collective-permute-start(s32[1,1]{1,0:T(1,128)} %param.18), channel_id=1, source_target_pairs={{0,3},{1,0},{2,1},{3,2},{4,7},{5,4},{6,5},{7,6},{8,11},{9,8},{10,9... | collective-permute-start | bytes 20 | tf_op jit(solution)/shard_map/ppermute | solution.py:34
  8.3 32.9 %all_to_all.55 = f32[128,4,128]{2,1,0:T(4,128)S(1)} all-to-all(f32[128,4,128]{2,1,0:T(4,128)S(1)} %bitcast.31), channel_id=1, replica_groups=mesh['z'=8,'y'=8,'core'=2,'x'=4] {'z','y','core'}, dimensions={0} | all-to-all | bytes 524288 | tf_op jit(solution)/shard_map/all_to_all | solution.py:38
  41.3 1.0 shard_map.165
  42.3 5.5 %all-to-all-start.1 = ((f32[128,4,128]{2,1,0:T(4,128)}), f32[128,4,128]{2,1,0:T(4,128)S(1)}, u32[]{:S(2)}, u32[]{:S(2)}) async-start(f32[128,4,128]{2,1,0:T(4,128)} %bitcast.4), calls=%async_computation.1 | async-start | bytes 524288 | tf_op jit(solution)/shard_map/all_to_all | solution.py:38
  48.6 4.7 %collective-permute-start.1 = (f32[448,128]{1,0:T(8,128)S(1)}, f32[448,128]{1,0:T(8,128)S(1)}, u32[]{:S(2)}, u32[]{:S(2)}) collective-permute-start(f32[448,128]{1,0:T(8,128)S(1)} %shard_map.166), channel_id=1, source_target_pairs={{0,3},{1,0},{2,1},{3,2},{4,7},{5,4},{6,5},{7,6},{8,11},{9,8},{10,9... | collective-permute-start | bytes 688136 | tf_op jit(solution)/shard_map/ppermute | solution.py:34
  53.3 3.9 %collective-permute-done.1.bucket_ref = f32[448,128]{1,0:T(8,128)S(1)} collective-permute-done((f32[448,128]{1,0:T(8,128)S(1)}, f32[448,128]{1,0:T(8,128)S(1)}, u32[]{:S(2)}, u32[]{:S(2)}) %collective-permute-start.1) | collective-permute-done | bytes 229408 | tf_op jit(solution)/shard_map/ppermute | solution.py:34
  57.2 6.0 %all-to-all-done.1 = f32[128,4,128]{2,1,0:T(4,128)S(1)} async-done(((f32[128,4,128]{2,1,0:T(4,128)}), f32[128,4,128]{2,1,0:T(4,128)S(1)}, u32[]{:S(2)}, u32[]{:S(2)}) %all-to-all-start.1) | async-done | bytes 262176 | tf_op jit(solution)/shard_map/all_to_all | solution.py:38
  63.2 2.9 %shard_map.167 = (f32[400,512]{1,0:T(8,128)S(1)}, f32[400,512]{1,0:T(8,128)S(1)}, f32[400,128]{1,0:T(8,128)S(1)}, f32[1,128]{1,0:T(1,128)S(1)}, f32[400,128]{1,0...) custom-call(s32[1,1]{1,0:T(1,128)} %bitcast.mine_ref, f32[512,128]{1,0:T(8,128)S(1)} %bitcast.30, ...), custom_call_target="tpu_custom_call" | custom-call | tf_op jit(solution)/shard_map/pallas_call | solution.py:60
  66.1 2.3 %collective-permute-start.2 = (f32[1280,128]{1,0:T(8,128)S(1)}, f32[1280,128]{1,0:T(8,128)S(1)}, u32[]{:S(2)}, u32[]{:S(2)}) collective-permute-start(f32[1280,128]{1,0:T(8,128)S(1)} %get-tuple-element.52), channel_id=1, source_target_pairs={{0,4},{4,0},{1,5},{5,1},{2,6},{6,2},{3,7},{7,3},{8,12},{12,8},{9,1... | collective-permute-start | bytes 1966088 | tf_op jit(solution)/shard_map/ppermute | solution.py:34
  68.9 1.2 collective-permute-done.2
  70.2 13.9 %all_to_all.56 = f32[4,320,128]{2,1,0:T(8,128)S(1)} all-to-all(f32[4,320,128]{2,1,0:T(8,128)S(1)} %bitcast.39), channel_id=1, replica_groups=mesh['z'=8,'y'=8,'core'=2,'x'=4] {'x'}, dimensions={0} | all-to-all | bytes 1310720 | tf_op jit(solution)/shard_map/all_to_all | solution.py:38
  84.2 11.0 %all_to_all.57 = f32[8,40,128]{2,1,0:T(8,128)S(1)} all-to-all(f32[8,40,128]{2,1,0:T(8,128)S(1)} %bitcast.41), channel_id=1, replica_groups=mesh['z'=8,'y'=8,'core'=2,'x'=4] {'y'}, dimensions={0} | all-to-all | bytes 327680 | tf_op jit(solution)/shard_map/all_to_all | solution.py:38
  95.2 14.9 %all_to_all.58 = f32[8,40,128]{2,1,0:T(8,128)S(1)} all-to-all(f32[8,40,128]{2,1,0:T(8,128)S(1)} %broadcast_in_dim.8), channel_id=1, replica_groups=mesh['z'=8,'y'=8,'core'=2,'x'=4] {'z'}, dimensions={0} | all-to-all | bytes 327680 | tf_op jit(solution)/shard_map/all_to_all | solution.py:38
  110.2 10.7 %all_to_all.59 = f32[8,40,128]{2,1,0:T(8,128)S(1)} all-to-all(f32[8,40,128]{2,1,0:T(8,128)S(1)} %broadcast_in_dim.9), channel_id=1, replica_groups=mesh['z'=8,'y'=8,'core'=2,'x'=4] {'y'}, dimensions={0} | all-to-all | bytes 327680 | tf_op jit(solution)/shard_map/all_to_all | solution.py:38
  120.9 10.0 %all_to_all.60 = f32[4,320,128]{2,1,0:T(8,128)S(1)} all-to-all(f32[4,320,128]{2,1,0:T(8,128)S(1)} %broadcast_in_dim.22), channel_id=1, replica_groups=mesh['z'=8,'y'=8,'core'=2,'x'=4] {'x'}, dimensions={0} | all-to-all | bytes 1310720 | tf_op jit(solution)/shard_map/all_to_all | solution.py:38
  130.9 8.7 %collective-permute-start.3 = (f32[1280,128]{1,0:T(8,128)S(1)}, f32[1280,128]{1,0:T(8,128)S(1)}, u32[]{:S(2)}, u32[]{:S(2)}) collective-permute-start(f32[1280,128]{1,0:T(8,128)S(1)} %bitcast.25), channel_id=1, source_target_pairs={{0,4},{4,0},{1,5},{5,1},{2,6},{6,2},{3,7},{7,3},{8,12},{12,8},{9,1... | collective-permute-start | bytes 1966088 | tf_op jit(solution)/shard_map/ppermute | solution.py:34
  141.3 3.7 %shard_map.170 = (f32[400,512]{1,0:T(8,128)S(1)}, f32[400,384]{1,0:T(8,128)S(1)}, f32[1,384]{1,0:T(1,128)S(1)}, f32[1536,128]{1,0:T(8,128)S(1)}, f32[1536,128]{1,0:T(8,128)S(1)}) custom-call(s32[1,1]{1,0:T(1,128)} %bitcast.mine_ref, s32[1,1]{1,0:T(1,128)} %collective-permute-done.partner_ref, f32[400,384]{1,0:T(8,128)S(1)} %get-tuple-element.65.own_ref.near_ref, ...), custom_call_target="tpu_custom_call" | custom-call | tf_op jit(solution)/shard_map/pallas_call | solution.py:60
  145.0 2.3 %collective-permute-start.4 = (f32[1536,128]{1,0:T(8,128)S(1)}, f32[1536,128]{1,0:T(8,128)S(1)}, u32[]{:S(2)}, u32[]{:S(2)}) collective-permute-start(f32[1536,128]{1,0:T(8,128)S(1)} %get-tuple-element.72), channel_id=1, source_target_pairs={{0,4},{4,0},{1,5},{5,1},{2,6},{6,2},{3,7},{7,3},{8,12},{12,8},{9,1... | collective-permute-start | bytes 2359304 | tf_op jit(solution)/shard_map/ppermute | solution.py:34
  147.7 1.6 collective-permute-done.4.got_ref
  149.3 13.0 %all_to_all.61.received_ref = f32[4,320,128]{2,1,0:T(8,128)S(1)} all-to-all(f32[4,320,128]{2,1,0:T(8,128)S(1)} %bitcast.40), channel_id=1, replica_groups=mesh['z'=8,'y'=8,'core'=2,'x'=4] {'x'}, dimensions={0} | all-to-all | bytes 1310720 | tf_op jit(solution)/shard_map/all_to_all | solution.py:38
  163.1 4.8 %all-to-all-start.8 = ((f32[64,3,4,128]{3,2,1,0:T(4,128)}), f32[64,3,4,128]{3,2,1,0:T(4,128)S(1)}, u32[]{:S(2)}, u32[]{:S(2)}) async-start(f32[64,3,4,128]{3,2,1,0:T(4,128)} %bitcast.16), calls=%async_computation.8 | async-start | bytes 786432 | tf_op jit(solution)/shard_map/all_to_all | solution.py:38
  167.9 2.2 collective-permute-start.5
  170.1 6.4 %collective-permute-done.5.source_ref = f32[408,128]{1,0:T(8,128)S(1)} collective-permute-done((f32[408,128]{1,0:T(8,128)S(1)}, f32[408,128]{1,0:T(8,128)S(1)}, u32[]{:S(2)}, u32[]{:S(2)}) %collective-permute-start.5) | collective-permute-done | bytes 208928 | tf_op jit(solution)/shard_map/ppermute | solution.py:34
  176.5 5.7 %all-to-all-done.8 = f32[64,3,4,128]{3,2,1,0:T(4,128)S(1)} async-done(((f32[64,3,4,128]{3,2,1,0:T(4,128)}), f32[64,3,4,128]{3,2,1,0:T(4,128)S(1)}, u32[]{:S(2)}, u32[]{:S(2)}) %all-to-all-start.8) | async-done | bytes 393248 | tf_op jit(solution)/shard_map/all_to_all | solution.py:38
  182.2 1.0 shard_map.173
  183.3 20.2 %all_to_all.62 = f32[64,3,4,128]{3,2,1,0:T(4,128)S(1)} all-to-all(f32[64,3,4,128]{3,2,1,0:T(4,128)S(1)} %bitcast.29), channel_id=1, replica_groups=mesh['z'=8,'y'=8,'core'=2,'x'=4] {'z','y'}, dimensions={0} | all-to-all | bytes 786432 | tf_op jit(solution)/shard_map/all_to_all | solution.py:38
  204.3 3.5 %all-to-all-start.10 = ((f32[4,320,128]{2,1,0:T(8,128)}), f32[4,320,128]{2,1,0:T(8,128)S(1)}, u32[]{:S(2)}, u32[]{:S(2)}) async-start(f32[4,320,128]{2,1,0:T(8,128)} %get-tuple-element.78), calls=%async_computation.10 | async-start | bytes 1310720 | tf_op jit(solution)/shard_map/all_to_all | solution.py:38
  207.8 6.5 %collective-permute-start.6 = (f32[256,128]{1,0:T(8,128)S(1)}, f32[256,128]{1,0:T(8,128)S(1)}, u32[]{:S(2)}, u32[]{:S(2)}) collective-permute-start(f32[256,128]{1,0:T(8,128)S(1)} %get-tuple-element.80), channel_id=1, source_target_pairs={{0,4},{4,0},{1,5},{5,1},{2,6},{6,2},{3,7},{7,3},{8,12},{12,8},{9,1... | collective-permute-start | bytes 393224 | tf_op jit(solution)/shard_map/ppermute | solution.py:34
  214.3 1.0 collective-permute-done.6.other_ref
  216.1 6.9 %collective-permute-start.7 = (f32[1280,128]{1,0:T(8,128)S(1)}, f32[1280,128]{1,0:T(8,128)S(1)}, u32[]{:S(2)}, u32[]{:S(2)}) collective-permute-start(f32[1280,128]{1,0:T(8,128)S(1)} %bitcast.23), channel_id=1, source_target_pairs={{0,4},{4,0},{1,5},{5,1},{2,6},{6,2},{3,7},{7,3},{8,12},{12,8},{9,1... | collective-permute-start | bytes 1966088 | tf_op jit(solution)/shard_map/ppermute | solution.py:34
  223.2 1.5 collective-permute-done.7.other_ref
  224.7 1.3 shard_map.177
  (43 shorter events, 8.5 us)
Async XLA Ops:
  0.6 7.0 %collective-permute-start = (s32[1,1]{1,0:T(1,128)}, s32[1,1]{1,0:T(1,128)}, u32[]{:S(2)}, u32[]{:S(2)}) collective-permute-start(s32[1,1]{1,0:T(1,128)} %param.18), channel_id=1, source_target_pairs={{0,3},{1,0},{2,1},{3,2},{4,7},{5,4},{6,5},{7,6},{8,11},{9,8},{10,9... | collective-permute-start | bytes 20 | tf_op jit(solution)/shard_map/ppermute | solution.py:34
  5.9 0.9 copy-start.2
  6.8 0.7 copy-start.8
  7.4 41.0 %copy-start.1 = (f32[400,128]{1,0:T(8,128)S(1)}, f32[400,128]{1,0:T(8,128)}, u32[]{:S(2)}) copy-start(f32[400,128]{1,0:T(8,128)} %source_ref.1) | copy-start | bytes 614404
  7.4 41.0 %copy-start.3 = (s32[1,1,2048]{2,1,0:T(1,128)S(1)}, s32[1,1,2048]{2,1,0:T(1,128)}, u32[]{:S(2)}) copy-start(s32[1,1,2048]{2,1,0:T(1,128)} %param.23) | copy-start | bytes 24580
  7.5 41.0 %copy-start.4 = (s32[1,1,1024]{2,1,0:T(1,128)S(1)}, s32[1,1,1024]{2,1,0:T(1,128)}, u32[]{:S(2)}) copy-start(s32[1,1,1024]{2,1,0:T(1,128)} %param.20) | copy-start | bytes 12292
  7.5 41.1 %copy-start.5 = (s32[1,1,1024]{2,1,0:T(1,128)S(1)}, s32[1,1,1024]{2,1,0:T(1,128)}, u32[]{:S(2)}) copy-start(s32[1,1,1024]{2,1,0:T(1,128)} %param.21) | copy-start | bytes 12292
  7.5 41.1 %copy-start.6 = (s32[1,1,1024]{2,1,0:T(1,128)S(1)}, s32[1,1,1024]{2,1,0:T(1,128)}, u32[]{:S(2)}) copy-start(s32[1,1,1024]{2,1,0:T(1,128)} %param.22) | copy-start | bytes 12292
  7.5 41.1 %copy-start.7 = (f32[128]{0:T(128)S(1)}, f32[128]{0:T(128)}, u32[]{:S(2)}) copy-start(f32[128]{0:T(128)} %param.13) | copy-start | bytes 1540
  7.6 55.6 %copy-start = (f32[400,768]{1,0:T(8,128)S(1)}, f32[400,768]{1,0:T(8,128)}, u32[]{:S(2)}) copy-start(f32[400,768]{1,0:T(8,128)} %relations_ref.5) | copy-start | bytes 3686404
  42.3 20.9 %all-to-all-start.1 = ((f32[128,4,128]{2,1,0:T(4,128)}), f32[128,4,128]{2,1,0:T(4,128)S(1)}, u32[]{:S(2)}, u32[]{:S(2)}) async-start(f32[128,4,128]{2,1,0:T(4,128)} %bitcast.4), calls=%async_computation.1 | async-start | bytes 524288 | tf_op jit(solution)/shard_map/all_to_all | solution.py:38
  48.6 8.6 %collective-permute-start.1 = (f32[448,128]{1,0:T(8,128)S(1)}, f32[448,128]{1,0:T(8,128)S(1)}, u32[]{:S(2)}, u32[]{:S(2)}) collective-permute-start(f32[448,128]{1,0:T(8,128)S(1)} %shard_map.166), channel_id=1, source_target_pairs={{0,3},{1,0},{2,1},{3,2},{4,7},{5,4},{6,5},{7,6},{8,11},{9,8},{10,9... | collective-permute-start | bytes 688136 | tf_op jit(solution)/shard_map/ppermute | solution.py:34
  66.1 4.0 %collective-permute-start.2 = (f32[1280,128]{1,0:T(8,128)S(1)}, f32[1280,128]{1,0:T(8,128)S(1)}, u32[]{:S(2)}, u32[]{:S(2)}) collective-permute-start(f32[1280,128]{1,0:T(8,128)S(1)} %get-tuple-element.52), channel_id=1, source_target_pairs={{0,4},{4,0},{1,5},{5,1},{2,6},{6,2},{3,7},{7,3},{8,12},{12,8},{9,1... | collective-permute-start | bytes 1966088 | tf_op jit(solution)/shard_map/ppermute | solution.py:34
  110.2 29.4 %copy-start.9 = (f32[768]{0:T(1024)S(1)}, f32[768]{0:T(1024)}, u32[]{:S(2)}) copy-start(f32[768]{0:T(1024)} %param.17) | copy-start | bytes 9220
  130.9 10.4 %collective-permute-start.3 = (f32[1280,128]{1,0:T(8,128)S(1)}, f32[1280,128]{1,0:T(8,128)S(1)}, u32[]{:S(2)}, u32[]{:S(2)}) collective-permute-start(f32[1280,128]{1,0:T(8,128)S(1)} %bitcast.25), channel_id=1, source_target_pairs={{0,4},{4,0},{1,5},{5,1},{2,6},{6,2},{3,7},{7,3},{8,12},{12,8},{9,1... | collective-permute-start | bytes 1966088 | tf_op jit(solution)/shard_map/ppermute | solution.py:34
  145.0 4.2 %collective-permute-start.4 = (f32[1536,128]{1,0:T(8,128)S(1)}, f32[1536,128]{1,0:T(8,128)S(1)}, u32[]{:S(2)}, u32[]{:S(2)}) collective-permute-start(f32[1536,128]{1,0:T(8,128)S(1)} %get-tuple-element.72), channel_id=1, source_target_pairs={{0,4},{4,0},{1,5},{5,1},{2,6},{6,2},{3,7},{7,3},{8,12},{12,8},{9,1... | collective-permute-start | bytes 2359304 | tf_op jit(solution)/shard_map/ppermute | solution.py:34
  163.1 19.1 %all-to-all-start.8 = ((f32[64,3,4,128]{3,2,1,0:T(4,128)}), f32[64,3,4,128]{3,2,1,0:T(4,128)S(1)}, u32[]{:S(2)}, u32[]{:S(2)}) async-start(f32[64,3,4,128]{3,2,1,0:T(4,128)} %bitcast.16), calls=%async_computation.8 | async-start | bytes 786432 | tf_op jit(solution)/shard_map/all_to_all | solution.py:38
  167.9 8.6 %collective-permute-start.5 = (f32[408,128]{1,0:T(8,128)S(1)}, f32[408,128]{1,0:T(8,128)S(1)}, u32[]{:S(2)}, u32[]{:S(2)}) collective-permute-start(f32[408,128]{1,0:T(8,128)S(1)} %shard_map.171), channel_id=1, source_target_pairs={{0,1},{1,2},{2,3},{3,0},{4,5},{5,6},{6,7},{7,4},{8,9},{9,10},{10,1... | collective-permute-start | bytes 626696 | tf_op jit(solution)/shard_map/ppermute | solution.py:34
  204.3 11.8 %all-to-all-start.10 = ((f32[4,320,128]{2,1,0:T(8,128)}), f32[4,320,128]{2,1,0:T(8,128)S(1)}, u32[]{:S(2)}, u32[]{:S(2)}) async-start(f32[4,320,128]{2,1,0:T(8,128)} %get-tuple-element.78), calls=%async_computation.10 | async-start | bytes 1310720 | tf_op jit(solution)/shard_map/all_to_all | solution.py:38
  207.8 7.5 %collective-permute-start.6 = (f32[256,128]{1,0:T(8,128)S(1)}, f32[256,128]{1,0:T(8,128)S(1)}, u32[]{:S(2)}, u32[]{:S(2)}) collective-permute-start(f32[256,128]{1,0:T(8,128)S(1)} %get-tuple-element.80), channel_id=1, source_target_pairs={{0,4},{4,0},{1,5},{5,1},{2,6},{6,2},{3,7},{7,3},{8,12},{12,8},{9,1... | collective-permute-start | bytes 393224 | tf_op jit(solution)/shard_map/ppermute | solution.py:34
  216.1 8.6 %collective-permute-start.7 = (f32[1280,128]{1,0:T(8,128)S(1)}, f32[1280,128]{1,0:T(8,128)S(1)}, u32[]{:S(2)}, u32[]{:S(2)}) collective-permute-start(f32[1280,128]{1,0:T(8,128)S(1)} %bitcast.23), channel_id=1, source_target_pairs={{0,4},{4,0},{1,5},{5,1},{2,6},{6,2},{3,7},{7,3},{8,12},{12,8},{9,1... | collective-permute-start | bytes 1966088 | tf_op jit(solution)/shard_map/ppermute | solution.py:34

commit v6 on v5

--- a/solution.py
+++ b/solution.py
@@ -608,7 +608,7 @@
         scalars=1,
     )
     bucket = passed_along(bucket, "x", -1)
-    spread = dealt(cargo, DOM, BLOCK)
+    spread, bucket = lax.optimization_barrier((dealt(cargo, DOM, BLOCK), bucket))
     (spread,) = kernel_call(pick_body, [tile], [spread])
     arrived = dealt(spread, DOM, BLOCK)
     block = ((DIM, BLOCK), f32)

time: 227 us -> 228 us (level)
  blocking collectives: 127 us -> 90.1 us
  starting transfers between devices: 52.6 us -> 74 us
  waiting for transfers between devices: 28.1 us -> 43.4 us
    all_to_all x8 -> x7, blocking collectives: 127 us -> 90.1 us  [exchange(): return lax.all_to_all(value, axis, split_axis=0, concat_axis=0, tiled=True)]
    all_to_all x3 -> x4, starting transfers between devices: 13.8 us -> 35.4 us  [exchange(): return lax.all_to_all(value, axis, split_axis=0, concat_axis=0, tiled=True)]
    all_to_all x3 -> x4, waiting for transfers between devices: 11.8 us -> 26.9 us  [exchange(): return lax.all_to_all(value, axis, split_axis=0, concat_axis=0, tiled=True)]
  transfers between devices with their start and end apart: 11 -> 12, of which waited for: 9 -> 10; matrix products, arithmetic and copies ran while one was open for 0% -> 0% of each run, Pallas kernels for 1% -> 1%
where the time goes in v6:
time: 228 us
  blocking collectives  90.1 us (40%)
  starting transfers between devices  74 us (32%)
  waiting for transfers between devices  43.4 us (19%)
  Pallas kernels  16 us (7%)
    all_to_all x7, blocking collectives, exchange(): return lax.all_to_all(value, axis, split_axis=0, concat_axis=0, tiled=True)  90.1 us
    ppermute x8, starting transfers between devices, passed_along(): return lax.ppermute(value, axis, pairs)  38.6 us
    all_to_all x4, starting transfers between devices, exchange(): return lax.all_to_all(value, axis, split_axis=0, concat_axis=0, tiled=True)  35.4 us
    all_to_all x4, waiting for transfers between devices, exchange(): return lax.all_to_all(value, axis, split_axis=0, concat_axis=0, tiled=True)  26.9 us
    ppermute x8, waiting for transfers between devices, passed_along(): return lax.ppermute(value, axis, pairs)  16.4 us
    pallas_call x15, Pallas kernels, kernel_call(): pl.pallas_call(body, out_shape=[jax.ShapeDtypeStruct(shape, dtype) for sh...  16 us
  transfers between devices with their start and end apart: 12, of which 10 were waited for; matrix products, arithmetic and copies ran while one was open for 0% of the time, Pallas kernels for 1%

profile of v6, /device:TPU:1, one launch (start us, length us, event | category | flops | bytes accessed | tf_op | source)
XLA Modules:
  0.0 227.5 jit_solution(9398027838938791204)
XLA Ops:
  0.6 5.3 %collective-permute-start = (s32[1,1]{1,0:T(1,128)}, s32[1,1]{1,0:T(1,128)}, u32[]{:S(2)}, u32[]{:S(2)}) collective-permute-start(s32[1,1]{1,0:T(1,128)} %param.18), channel_id=1, source_target_pairs={{0,3},{1,0},{2,1},{3,2},{4,7},{5,4},{6,5},{7,6},{8,11},{9,8},{10,9... | collective-permute-start | bytes 20 | tf_op jit(solution)/shard_map/ppermute | solution.py:34
  7.8 1.5 shard_map.164
  9.2 17.9 %all-to-all-start = ((f32[128,4,128]{2,1,0:T(4,128)}), f32[128,4,128]{2,1,0:T(4,128)S(1)}, u32[]{:S(2)}, u32[]{:S(2)}) async-start(f32[128,4,128]{2,1,0:T(4,128)} %bitcast.2), calls=%async_computation | async-start | bytes 524288 | tf_op jit(solution)/shard_map/all_to_all | solution.py:38
  27.8 4.6 %collective-permute-start.1 = (f32[448,128]{1,0:T(8,128)S(1)}, f32[448,128]{1,0:T(8,128)S(1)}, u32[]{:S(2)}, u32[]{:S(2)}) collective-permute-start(f32[448,128]{1,0:T(8,128)S(1)} %shard_map.165), channel_id=1, source_target_pairs={{0,3},{1,0},{2,1},{3,2},{4,7},{5,4},{6,5},{7,6},{8,11},{9,8},{10,9... | collective-permute-start | bytes 688136 | tf_op jit(solution)/shard_map/ppermute | solution.py:34
  32.4 4.0 %collective-permute-done.1.bucket_ref = f32[448,128]{1,0:T(8,128)S(1)} collective-permute-done((f32[448,128]{1,0:T(8,128)S(1)}, f32[448,128]{1,0:T(8,128)S(1)}, u32[]{:S(2)}, u32[]{:S(2)}) %collective-permute-start.1) | collective-permute-done | bytes 229408 | tf_op jit(solution)/shard_map/ppermute | solution.py:34
  36.4 5.9 %all-to-all-done = f32[128,4,128]{2,1,0:T(4,128)S(1)} async-done(((f32[128,4,128]{2,1,0:T(4,128)}), f32[128,4,128]{2,1,0:T(4,128)S(1)}, u32[]{:S(2)}, u32[]{:S(2)}) %all-to-all-start) | async-done | bytes 262176 | tf_op jit(solution)/shard_map/all_to_all | solution.py:38
  42.4 1.0 shard_map.166
  43.4 9.2 %all-to-all-start.1 = ((f32[128,4,128]{2,1,0:T(4,128)}), f32[128,4,128]{2,1,0:T(4,128)S(1)}, u32[]{:S(2)}, u32[]{:S(2)}) async-start(f32[128,4,128]{2,1,0:T(4,128)} %bitcast.9), calls=%async_computation.1 | async-start | bytes 524288 | tf_op jit(solution)/shard_map/all_to_all | solution.py:38
  52.6 15.3 %all-to-all-done.1 = f32[128,4,128]{2,1,0:T(4,128)S(1)} async-done(((f32[128,4,128]{2,1,0:T(4,128)}), f32[128,4,128]{2,1,0:T(4,128)S(1)}, u32[]{:S(2)}, u32[]{:S(2)}) %all-to-all-start.1) | async-done | bytes 262176 | tf_op jit(solution)/shard_map/all_to_all | solution.py:38
  67.9 2.9 %shard_map.167 = (f32[400,512]{1,0:T(8,128)S(1)}, f32[400,512]{1,0:T(8,128)S(1)}, f32[400,128]{1,0:T(8,128)S(1)}, f32[1,128]{1,0:T(1,128)S(1)}, f32[400,128]{1,0...) custom-call(s32[1,1]{1,0:T(1,128)} %bitcast.mine_ref, f32[512,128]{1,0:T(8,128)S(1)} %bitcast.30, ...), custom_call_target="tpu_custom_call" | custom-call | tf_op jit(solution)/shard_map/pallas_call | solution.py:60
  70.8 2.3 %collective-permute-start.2 = (f32[1280,128]{1,0:T(8,128)S(1)}, f32[1280,128]{1,0:T(8,128)S(1)}, u32[]{:S(2)}, u32[]{:S(2)}) collective-permute-start(f32[1280,128]{1,0:T(8,128)S(1)} %get-tuple-element.56), channel_id=1, source_target_pairs={{0,4},{4,0},{1,5},{5,1},{2,6},{6,2},{3,7},{7,3},{8,12},{12,8},{9,1... | collective-permute-start | bytes 1966088 | tf_op jit(solution)/shard_map/ppermute | solution.py:34
  73.6 1.2 collective-permute-done.2
  74.9 14.5 %all_to_all.55 = f32[4,320,128]{2,1,0:T(8,128)S(1)} all-to-all(f32[4,320,128]{2,1,0:T(8,128)S(1)} %bitcast.38), channel_id=1, replica_groups=mesh['z'=8,'y'=8,'core'=2,'x'=4] {'x'}, dimensions={0} | all-to-all | bytes 1310720 | tf_op jit(solution)/shard_map/all_to_all | solution.py:38
  89.4 11.0 %all_to_all.56 = f32[8,40,128]{2,1,0:T(8,128)S(1)} all-to-all(f32[8,40,128]{2,1,0:T(8,128)S(1)} %bitcast.40), channel_id=1, replica_groups=mesh['z'=8,'y'=8,'core'=2,'x'=4] {'y'}, dimensions={0} | all-to-all | bytes 327680 | tf_op jit(solution)/shard_map/all_to_all | solution.py:38
  100.5 10.7 %all_to_all.57 = f32[8,40,128]{2,1,0:T(8,128)S(1)} all-to-all(f32[8,40,128]{2,1,0:T(8,128)S(1)} %broadcast_in_dim.8), channel_id=1, replica_groups=mesh['z'=8,'y'=8,'core'=2,'x'=4] {'z'}, dimensions={0} | all-to-all | bytes 327680 | tf_op jit(solution)/shard_map/all_to_all | solution.py:38
  111.2 10.7 %all_to_all.58 = f32[8,40,128]{2,1,0:T(8,128)S(1)} all-to-all(f32[8,40,128]{2,1,0:T(8,128)S(1)} %broadcast_in_dim.9), channel_id=1, replica_groups=mesh['z'=8,'y'=8,'core'=2,'x'=4] {'y'}, dimensions={0} | all-to-all | bytes 327680 | tf_op jit(solution)/shard_map/all_to_all | solution.py:38
  122.0 10.0 %all_to_all.59 = f32[4,320,128]{2,1,0:T(8,128)S(1)} all-to-all(f32[4,320,128]{2,1,0:T(8,128)S(1)} %broadcast_in_dim.22), channel_id=1, replica_groups=mesh['z'=8,'y'=8,'core'=2,'x'=4] {'x'}, dimensions={0} | all-to-all | bytes 1310720 | tf_op jit(solution)/shard_map/all_to_all | solution.py:38
  132.0 8.5 %collective-permute-start.3 = (f32[1280,128]{1,0:T(8,128)S(1)}, f32[1280,128]{1,0:T(8,128)S(1)}, u32[]{:S(2)}, u32[]{:S(2)}) collective-permute-start(f32[1280,128]{1,0:T(8,128)S(1)} %bitcast.25), channel_id=1, source_target_pairs={{0,4},{4,0},{1,5},{5,1},{2,6},{6,2},{3,7},{7,3},{8,12},{12,8},{9,1... | collective-permute-start | bytes 1966088 | tf_op jit(solution)/shard_map/ppermute | solution.py:34
  142.2 3.8 %shard_map.170 = (f32[400,512]{1,0:T(8,128)S(1)}, f32[400,384]{1,0:T(8,128)S(1)}, f32[1,384]{1,0:T(1,128)S(1)}, f32[1536,128]{1,0:T(8,128)S(1)}, f32[1536,128]{1,0:T(8,128)S(1)}) custom-call(s32[1,1]{1,0:T(1,128)} %bitcast.mine_ref, s32[1,1]{1,0:T(1,128)} %collective-permute-done.partner_ref, f32[400,384]{1,0:T(8,128)S(1)} %get-tuple-element.69.own_ref.near_ref, ...), custom_call_target="tpu_custom_call" | custom-call | tf_op jit(solution)/shard_map/pallas_call | solution.py:60
  146.0 2.3 %collective-permute-start.4 = (f32[1536,128]{1,0:T(8,128)S(1)}, f32[1536,128]{1,0:T(8,128)S(1)}, u32[]{:S(2)}, u32[]{:S(2)}) collective-permute-start(f32[1536,128]{1,0:T(8,128)S(1)} %get-tuple-element.76), channel_id=1, source_target_pairs={{0,4},{4,0},{1,5},{5,1},{2,6},{6,2},{3,7},{7,3},{8,12},{12,8},{9,1... | collective-permute-start | bytes 2359304 | tf_op jit(solution)/shard_map/ppermute | solution.py:34
  148.6 1.6 collective-permute-done.4.got_ref
  150.2 13.0 %all_to_all.60.received_ref = f32[4,320,128]{2,1,0:T(8,128)S(1)} all-to-all(f32[4,320,128]{2,1,0:T(8,128)S(1)} %bitcast.39), channel_id=1, replica_groups=mesh['z'=8,'y'=8,'core'=2,'x'=4] {'x'}, dimensions={0} | all-to-all | bytes 1310720 | tf_op jit(solution)/shard_map/all_to_all | solution.py:38
  164.1 4.8 %all-to-all-start.8 = ((f32[64,3,4,128]{3,2,1,0:T(4,128)}), f32[64,3,4,128]{3,2,1,0:T(4,128)S(1)}, u32[]{:S(2)}, u32[]{:S(2)}) async-start(f32[64,3,4,128]{3,2,1,0:T(4,128)} %bitcast.16), calls=%async_computation.8 | async-start | bytes 786432 | tf_op jit(solution)/shard_map/all_to_all | solution.py:38
  168.9 2.2 collective-permute-start.5
  171.1 6.4 %collective-permute-done.5.source_ref = f32[408,128]{1,0:T(8,128)S(1)} collective-permute-done((f32[408,128]{1,0:T(8,128)S(1)}, f32[408,128]{1,0:T(8,128)S(1)}, u32[]{:S(2)}, u32[]{:S(2)}) %collective-permute-start.5) | collective-permute-done | bytes 208928 | tf_op jit(solution)/shard_map/ppermute | solution.py:34
  177.4 5.7 %all-to-all-done.8 = f32[64,3,4,128]{3,2,1,0:T(4,128)S(1)} async-done(((f32[64,3,4,128]{3,2,1,0:T(4,128)}), f32[64,3,4,128]{3,2,1,0:T(4,128)S(1)}, u32[]{:S(2)}, u32[]{:S(2)}) %all-to-all-start.8) | async-done | bytes 393248 | tf_op jit(solution)/shard_map/all_to_all | solution.py:38
  184.2 20.2 %all_to_all.61 = f32[64,3,4,128]{3,2,1,0:T(4,128)S(1)} all-to-all(f32[64,3,4,128]{3,2,1,0:T(4,128)S(1)} %bitcast.29), channel_id=1, replica_groups=mesh['z'=8,'y'=8,'core'=2,'x'=4] {'z','y'}, dimensions={0} | all-to-all | bytes 786432 | tf_op jit(solution)/shard_map/all_to_all | solution.py:38
  205.3 3.5 %all-to-all-start.10 = ((f32[4,320,128]{2,1,0:T(8,128)}), f32[4,320,128]{2,1,0:T(8,128)S(1)}, u32[]{:S(2)}, u32[]{:S(2)}) async-start(f32[4,320,128]{2,1,0:T(8,128)} %get-tuple-element.82), calls=%async_computation.10 | async-start | bytes 1310720 | tf_op jit(solution)/shard_map/all_to_all | solution.py:38
  208.7 6.5 %collective-permute-start.6 = (f32[256,128]{1,0:T(8,128)S(1)}, f32[256,128]{1,0:T(8,128)S(1)}, u32[]{:S(2)}, u32[]{:S(2)}) collective-permute-start(f32[256,128]{1,0:T(8,128)S(1)} %get-tuple-element.84), channel_id=1, source_target_pairs={{0,4},{4,0},{1,5},{5,1},{2,6},{6,2},{3,7},{7,3},{8,12},{12,8},{9,1... | collective-permute-start | bytes 393224 | tf_op jit(solution)/shard_map/ppermute | solution.py:34
  217.0 6.9 %collective-permute-start.7 = (f32[1280,128]{1,0:T(8,128)S(1)}, f32[1280,128]{1,0:T(8,128)S(1)}, u32[]{:S(2)}, u32[]{:S(2)}) collective-permute-start(f32[1280,128]{1,0:T(8,128)S(1)} %bitcast.23), channel_id=1, source_target_pairs={{0,4},{4,0},{1,5},{5,1},{2,6},{6,2},{3,7},{7,3},{8,12},{12,8},{9,1... | collective-permute-start | bytes 1966088 | tf_op jit(solution)/shard_map/ppermute | solution.py:34
  224.2 1.5 collective-permute-done.7.other_ref
  225.7 1.3 shard_map.177
  (44 shorter events, 9.8 us)
Async XLA Ops:
  0.6 27.1 %copy-start.1 = (f32[400,128]{1,0:T(8,128)S(1)}, f32[400,128]{1,0:T(8,128)}, u32[]{:S(2)}) copy-start(f32[400,128]{1,0:T(8,128)} %source_ref.1) | copy-start | bytes 614404
  0.6 7.1 %collective-permute-start = (s32[1,1]{1,0:T(1,128)}, s32[1,1]{1,0:T(1,128)}, u32[]{:S(2)}, u32[]{:S(2)}) collective-permute-start(s32[1,1]{1,0:T(1,128)} %param.18), channel_id=1, source_target_pairs={{0,3},{1,0},{2,1},{3,2},{4,7},{5,4},{6,5},{7,6},{8,11},{9,8},{10,9... | collective-permute-start | bytes 20 | tf_op jit(solution)/shard_map/ppermute | solution.py:34
  6.0 0.9 copy-start.2
  6.9 0.7 copy-start.8
  7.6 20.2 %copy-start.3 = (s32[1,1,2048]{2,1,0:T(1,128)S(1)}, s32[1,1,2048]{2,1,0:T(1,128)}, u32[]{:S(2)}) copy-start(s32[1,1,2048]{2,1,0:T(1,128)} %param.23) | copy-start | bytes 24580
  7.6 20.2 %copy-start.4 = (s32[1,1,1024]{2,1,0:T(1,128)S(1)}, s32[1,1,1024]{2,1,0:T(1,128)}, u32[]{:S(2)}) copy-start(s32[1,1,1024]{2,1,0:T(1,128)} %param.20) | copy-start | bytes 12292
  7.6 20.2 %copy-start.5 = (s32[1,1,1024]{2,1,0:T(1,128)S(1)}, s32[1,1,1024]{2,1,0:T(1,128)}, u32[]{:S(2)}) copy-start(s32[1,1,1024]{2,1,0:T(1,128)} %param.21) | copy-start | bytes 12292
  7.6 20.2 %copy-start.6 = (s32[1,1,1024]{2,1,0:T(1,128)S(1)}, s32[1,1,1024]{2,1,0:T(1,128)}, u32[]{:S(2)}) copy-start(s32[1,1,1024]{2,1,0:T(1,128)} %param.22) | copy-start | bytes 12292
  7.6 20.2 %copy-start.7 = (f32[128]{0:T(128)S(1)}, f32[128]{0:T(128)}, u32[]{:S(2)}) copy-start(f32[128]{0:T(128)} %param.13) | copy-start | bytes 1540
  7.7 60.1 %copy-start = (f32[400,768]{1,0:T(8,128)S(1)}, f32[400,768]{1,0:T(8,128)}, u32[]{:S(2)}) copy-start(f32[400,768]{1,0:T(8,128)} %relations_ref.5) | copy-start | bytes 3686404
  9.2 33.1 %all-to-all-start = ((f32[128,4,128]{2,1,0:T(4,128)}), f32[128,4,128]{2,1,0:T(4,128)S(1)}, u32[]{:S(2)}, u32[]{:S(2)}) async-start(f32[128,4,128]{2,1,0:T(4,128)} %bitcast.2), calls=%async_computation | async-start | bytes 524288 | tf_op jit(solution)/shard_map/all_to_all | solution.py:38
  27.8 8.6 %collective-permute-start.1 = (f32[448,128]{1,0:T(8,128)S(1)}, f32[448,128]{1,0:T(8,128)S(1)}, u32[]{:S(2)}, u32[]{:S(2)}) collective-permute-start(f32[448,128]{1,0:T(8,128)S(1)} %shard_map.165), channel_id=1, source_target_pairs={{0,3},{1,0},{2,1},{3,2},{4,7},{5,4},{6,5},{7,6},{8,11},{9,8},{10,9... | collective-permute-start | bytes 688136 | tf_op jit(solution)/shard_map/ppermute | solution.py:34
  43.4 24.5 %all-to-all-start.1 = ((f32[128,4,128]{2,1,0:T(4,128)}), f32[128,4,128]{2,1,0:T(4,128)S(1)}, u32[]{:S(2)}, u32[]{:S(2)}) async-start(f32[128,4,128]{2,1,0:T(4,128)} %bitcast.9), calls=%async_computation.1 | async-start | bytes 524288 | tf_op jit(solution)/shard_map/all_to_all | solution.py:38
  70.8 4.0 %collective-permute-start.2 = (f32[1280,128]{1,0:T(8,128)S(1)}, f32[1280,128]{1,0:T(8,128)S(1)}, u32[]{:S(2)}, u32[]{:S(2)}) collective-permute-start(f32[1280,128]{1,0:T(8,128)S(1)} %get-tuple-element.56), channel_id=1, source_target_pairs={{0,4},{4,0},{1,5},{5,1},{2,6},{6,2},{3,7},{7,3},{8,12},{12,8},{9,1... | collective-permute-start | bytes 1966088 | tf_op jit(solution)/shard_map/ppermute | solution.py:34
  111.2 29.2 %copy-start.9 = (f32[768]{0:T(1024)S(1)}, f32[768]{0:T(1024)}, u32[]{:S(2)}) copy-start(f32[768]{0:T(1024)} %param.17) | copy-start | bytes 9220
  132.0 10.2 %collective-permute-start.3 = (f32[1280,128]{1,0:T(8,128)S(1)}, f32[1280,128]{1,0:T(8,128)S(1)}, u32[]{:S(2)}, u32[]{:S(2)}) collective-permute-start(f32[1280,128]{1,0:T(8,128)S(1)} %bitcast.25), channel_id=1, source_target_pairs={{0,4},{4,0},{1,5},{5,1},{2,6},{6,2},{3,7},{7,3},{8,12},{12,8},{9,1... | collective-permute-start | bytes 1966088 | tf_op jit(solution)/shard_map/ppermute | solution.py:34
  146.0 4.2 %collective-permute-start.4 = (f32[1536,128]{1,0:T(8,128)S(1)}, f32[1536,128]{1,0:T(8,128)S(1)}, u32[]{:S(2)}, u32[]{:S(2)}) collective-permute-start(f32[1536,128]{1,0:T(8,128)S(1)} %get-tuple-element.76), channel_id=1, source_target_pairs={{0,4},{4,0},{1,5},{5,1},{2,6},{6,2},{3,7},{7,3},{8,12},{12,8},{9,1... | collective-permute-start | bytes 2359304 | tf_op jit(solution)/shard_map/ppermute | solution.py:34
  164.1 19.1 %all-to-all-start.8 = ((f32[64,3,4,128]{3,2,1,0:T(4,128)}), f32[64,3,4,128]{3,2,1,0:T(4,128)S(1)}, u32[]{:S(2)}, u32[]{:S(2)}) async-start(f32[64,3,4,128]{3,2,1,0:T(4,128)} %bitcast.16), calls=%async_computation.8 | async-start | bytes 786432 | tf_op jit(solution)/shard_map/all_to_all | solution.py:38
  168.9 8.6 %collective-permute-start.5 = (f32[408,128]{1,0:T(8,128)S(1)}, f32[408,128]{1,0:T(8,128)S(1)}, u32[]{:S(2)}, u32[]{:S(2)}) collective-permute-start(f32[408,128]{1,0:T(8,128)S(1)} %shard_map.171), channel_id=1, source_target_pairs={{0,1},{1,2},{2,3},{3,0},{4,5},{5,6},{6,7},{7,4},{8,9},{9,10},{10,1... | collective-permute-start | bytes 626696 | tf_op jit(solution)/shard_map/ppermute | solution.py:34
  205.3 11.8 %all-to-all-start.10 = ((f32[4,320,128]{2,1,0:T(8,128)}), f32[4,320,128]{2,1,0:T(8,128)S(1)}, u32[]{:S(2)}, u32[]{:S(2)}) async-start(f32[4,320,128]{2,1,0:T(8,128)} %get-tuple-element.82), calls=%async_computation.10 | async-start | bytes 1310720 | tf_op jit(solution)/shard_map/all_to_all | solution.py:38
  208.7 7.5 %collective-permute-start.6 = (f32[256,128]{1,0:T(8,128)S(1)}, f32[256,128]{1,0:T(8,128)S(1)}, u32[]{:S(2)}, u32[]{:S(2)}) collective-permute-start(f32[256,128]{1,0:T(8,128)S(1)} %get-tuple-element.84), channel_id=1, source_target_pairs={{0,4},{4,0},{1,5},{5,1},{2,6},{6,2},{3,7},{7,3},{8,12},{12,8},{9,1... | collective-permute-start | bytes 393224 | tf_op jit(solution)/shard_map/ppermute | solution.py:34
  217.0 8.6 %collective-permute-start.7 = (f32[1280,128]{1,0:T(8,128)S(1)}, f32[1280,128]{1,0:T(8,128)S(1)}, u32[]{:S(2)}, u32[]{:S(2)}) collective-permute-start(f32[1280,128]{1,0:T(8,128)S(1)} %bitcast.23), channel_id=1, source_target_pairs={{0,4},{4,0},{1,5},{5,1},{2,6},{6,2},{3,7},{7,3},{8,12},{12,8},{9,1... | collective-permute-start | bytes 1966088 | tf_op jit(solution)/shard_map/ppermute | solution.py:34

commit v7 on v5

--- a/solution.py
+++ b/solution.py
@@ -101,21 +101,22 @@
     return pl.ds(start, size, stride=stride)
 
 
-def pack_body(dest_ref, state_ref, out_ref):
+def pack_body(dest_ref, out_ref):
     for k in range(PIECE - 1):
         out_ref[spaced(k, BLOCK, PIECE), :] = dest_ref[LANES * k : LANES * (k + 1), :].T
     tail = dest_ref[LANES * (PIECE - 1) : DIM, :]
-    state = jnp.broadcast_to(state_ref[...], (8, LANES))
-    zero = jnp.zeros((LANES - tail.shape[0] - 8, LANES), f32)
-    out_ref[spaced(PIECE - 1, BLOCK, PIECE), :] = jnp.concatenate([tail, state, zero], 0).T
-
-
-def stamp_body(partner_ref, cargo_ref, out_ref):
+    zero = jnp.zeros((LANES - tail.shape[0], LANES), f32)
+    out_ref[spaced(PIECE - 1, BLOCK, PIECE), :] = jnp.concatenate([tail, zero], 0).T
+
+
+def stamp_body(partner_ref, state_ref, cargo_ref, out_ref):
     rows = spaced(PIECE - 1, BLOCK, PIECE)
     lane = lax.broadcasted_iota(jnp.int32, (BLOCK, LANES), 1)
     own = partner_ref[0, 0].astype(f32)
     out_ref[...] = cargo_ref[...]
-    out_ref[rows, :] = jnp.where(lane == OWN_LANE, own, cargo_ref[rows, :])
+    state = jnp.broadcast_to(state_ref[...], (BLOCK, LANES)).T
+    last = jnp.where(lane == OWN_LANE, own, cargo_ref[rows, :])
+    out_ref[rows, :] = jnp.where(lane == STATE_LANE, state, last)
 
 
 STATE_ROW = DIM
@@ -176,10 +177,6 @@
 HALF_REL = NREL // 2
 
 
-def flat_row(chunk):
-    return HALF_FLAT * (chunk // HALF_CHUNKS) + DIM * (chunk % HALF_CHUNKS)
-
-
 def half_update(grad_ref, param_of, state_of, out_ref, state_out):
     for k in range(HALF_CHUNKS):
         lanes = slice(LANES * k, LANES * (k + 1))
@@ -200,17 +197,19 @@
 
 
 def gradients(
+    mine,
     first,
     bucket_ref,
     target,
-    pick_r,
+    pick_r_ref,
     count_wide,
     subject_ref,
     operator_ref,
     objects_ref,
     query_ref,
     slope_ref,
-    flat_ref,
+    keep_ref,
+    give_ref,
     grad_subject_ref,
 ):
     edge = lax.broadcasted_iota(jnp.int32, (1, SPAN), 1) + first
@@ -257,26 +256,17 @@
 
     lax.fori_loop(0, HALF // 8, push, 0, unroll=5)
     grad_operator = operator_ref[...].astype(bf16)
-    for k in range(0, CHUNKS, 2):
-        pair = dot_last(grad_operator, pick_r[LANES * k : LANES * (k + 2), :])
-        for c in range(2):
-            first = flat_row(k + c)
-            flat_ref[first : first + DIM, :] = pair[:, LANES * c : LANES * (c + 1)]
     rest = HALF_FLAT - DIM * HALF_CHUNKS
-    for h in range(1, 3):
-        flat_ref[HALF_FLAT * h - rest : HALF_FLAT * h, :] = jnp.zeros((rest, LANES), f32)
+    for which, out_ref in ((mine, keep_ref), (1 - mine, give_ref)):
+        rows = pl.ds(pl.multiple_of(which * HALF_REL, LANES), HALF_REL)
+        some = dot_last(grad_operator, pick_r_ref[rows, :])
+        for k in range(HALF_CHUNKS):
+            out_ref[DIM * k : DIM * (k + 1), :] = some[:, LANES * k : LANES * (k + 1)]
+        out_ref[HALF_FLAT - rest : HALF_FLAT, :] = jnp.zeros((rest, LANES), f32)
     return noise
 
 
 WIDE = ((DIM, SPAN), f32)
-FLAT_TABLE = ((FLAT, LANES), f32)
-
-
-def halves(mine, flat_ref, keep_ref, give_ref):
-    keep_ref[0:HALF_FLAT, :] = flat_ref[pl.ds(pl.multiple_of(mine * HALF_FLAT, 8), HALF_FLAT), :]
-    give_ref[0:HALF_FLAT, :] = flat_ref[
-        pl.ds(pl.multiple_of((1 - mine) * HALF_FLAT, 8), HALF_FLAT), :
-    ]
 
 
 def first_body(
@@ -295,7 +285,7 @@
     operator_ref,
     objects_ref,
     slope_ref,
-    flat_ref,
+    pick_r_ref,
 ):
     last = arrived_ref[spaced(PIECE - 1, BLOCK, PIECE), :].T
     target = jnp.concatenate(
@@ -306,25 +296,26 @@
     source = bucket_ref[0:DIM, :]
     pick_s = one_hot(BLOCK, listed(bucket_ref, 0, 0))
     pick_t = one_hot(BLOCK, listed(bucket_ref, 1, 0))
-    pick_r = one_hot(NREL, listed(bucket_ref, 2, 0))
+    pick_r_ref[...] = one_hot(NREL, listed(bucket_ref, 2, 0))
     subject_ref[...] = dot(source.astype(bf16), pick_s)
-    operator_ref[...] = dot(relations_ref[...].astype(bf16), pick_r)
+    operator_ref[...] = dot(relations_ref[...].astype(bf16), pick_r_ref[...])
     objects_ref[...] = dot(target.astype(bf16), pick_t)
     noise_out[...] = gradients(
+        mine_ref[0, 0],
         0,
         bucket_ref,
         target,
-        pick_r,
+        pick_r_ref,
         counted(listed(bucket_ref, 3, 0)),
         subject_ref,
         operator_ref,
         objects_ref,
         query_ref,
         slope_ref,
-        flat_ref,
+        keep_out,
+        give_out,
         grad_subject_ref,
     )
-    halves(mine_ref[0, 0], flat_ref, keep_out, give_out)
     target_out[...] = target
     target_state_out[...] = last[STATE_LANE : STATE_LANE + 1, :]
 
@@ -414,7 +405,6 @@
     operator_ref,
     query_ref,
     slope_ref,
-    flat_ref,
     turned_ref,
 ):
     mine = mine_ref[0, 0]
@@ -432,20 +422,21 @@
     )
     target = target_ref[...]
     noise = gradients(
+        mine,
         SPAN,
         bucket_ref,
         target,
-        pick_r_ref[...],
+        pick_r_ref,
         count_ref[...],
         first_subject_ref,
         operator_ref,
         objects_ref,
         query_ref,
         slope_ref,
-        flat_ref,
+        keep_out,
+        give_out,
         subject_ref,
     )
-    halves(mine, flat_ref, keep_out, give_out)
     pick_t = one_hot(BLOCK, listed(bucket_ref, 1, 1))
     grad_target = dot_last(query_ref[...].astype(bf16), pick_t) + noise
     target, target_state = stepped(target, target_state_ref[...], grad_target)
@@ -596,8 +587,10 @@
     turned = ((BLOCK, LANES), f32)
     partner = passed_along(partner, "x", -1)
     tile = ((BLOCK * PIECE, LANES), f32)
-    (cargo,) = kernel_call(pack_body, [tile], [dest_emb, dest_state.reshape(1, -1)])
-    (cargo,) = kernel_call(stamp_body, [tile], [partner, cargo], scalars=1)
+    (cargo,) = kernel_call(pack_body, [tile], [dest_emb])
+    (cargo,) = kernel_call(
+        stamp_body, [tile], [partner, dest_state.reshape(1, -1), cargo], scalars=1
+    )
     lists = [
         rows.reshape(1, -1) for rows in (source_rows, target_rows, relation_index, negative_rows)
     ]
@@ -623,7 +616,7 @@
         first_body,
         [WIDE, WIDE, block, line, block, half, half],
         [mine, arrived, bucket, relations],
-        [WIDE] * 4 + [FLAT_TABLE],
+        [WIDE] * 4 + [picks_r],
         scalars=1,
     )
     source, source_acc, target, target_acc = kernel_call(
@@ -655,7 +648,7 @@
         [WIDE, half_table, half_types, longer, longer],
         [mine, partner, near, other, target, target_acc, relations, relation_acc]
         + [subject, objects, pick_r, count, bucket],
-        [WIDE] * 3 + [FLAT_TABLE, turned],
+        [WIDE] * 3 + [turned],
         scalars=2,
     )
     (source,) = kernel_call(

time: 227 us -> 228 us (level)
  no operation moved by 1% of the time
where the time goes in v7:
time: 228 us; the launch traced here: 227 us
  blocking collectives  127 us (56%)
  starting transfers between devices  53.1 us (23%)
  waiting for transfers between devices  27.6 us (12%)
  Pallas kernels  15.2 us (7%)
    all_to_all x8, blocking collectives, exchange(): return lax.all_to_all(value, axis, split_axis=0, concat_axis=0, tiled=True)  127 us
    ppermute x8, starting transfers between devices, passed_along(): return lax.ppermute(value, axis, pairs)  39.3 us
    ppermute x8, waiting for transfers between devices, passed_along(): return lax.ppermute(value, axis, pairs)  16.3 us
    pallas_call x15, Pallas kernels, kernel_call(): pl.pallas_call(body, out_shape=[jax.ShapeDtypeStruct(shape, dtype) for sh...  15.2 us
    all_to_all x3, starting transfers between devices, exchange(): return lax.all_to_all(value, axis, split_axis=0, concat_axis=0, tiled=True)  13.8 us
    all_to_all x3, waiting for transfers between devices, exchange(): return lax.all_to_all(value, axis, split_axis=0, concat_axis=0, tiled=True)  11.3 us
  transfers between devices with their start and end apart: 11, of which 9 were waited for; matrix products, arithmetic and copies ran while one was open for 0% of the time, Pallas kernels for 1%

profile of v7, /device:TPU:1, one launch (start us, length us, event | category | flops | bytes accessed | tf_op | source)
XLA Modules:
  0.0 227.4 jit_solution(17981832343903738226)
XLA Ops:
  0.6 5.2 %collective-permute-start = (s32[1,1]{1,0:T(1,128)}, s32[1,1]{1,0:T(1,128)}, u32[]{:S(2)}, u32[]{:S(2)}) collective-permute-start(s32[1,1]{1,0:T(1,128)} %param.18), channel_id=1, source_target_pairs={{0,3},{1,0},{2,1},{3,2},{4,7},{5,4},{6,5},{7,6},{8,11},{9,8},{10,9... | collective-permute-start | bytes 20 | tf_op jit(solution)/shard_map/ppermute | solution.py:34
  8.4 33.2 %all_to_all.55 = f32[128,4,128]{2,1,0:T(4,128)S(1)} all-to-all(f32[128,4,128]{2,1,0:T(4,128)S(1)} %bitcast.31), channel_id=1, replica_groups=mesh['z'=8,'y'=8,'core'=2,'x'=4] {'z','y','core'}, dimensions={0} | all-to-all | bytes 524288 | tf_op jit(solution)/shard_map/all_to_all | solution.py:38
  41.6 1.0 shard_map.165
  42.6 5.5 %all-to-all-start.1 = ((f32[128,4,128]{2,1,0:T(4,128)}), f32[128,4,128]{2,1,0:T(4,128)S(1)}, u32[]{:S(2)}, u32[]{:S(2)}) async-start(f32[128,4,128]{2,1,0:T(4,128)} %bitcast.4), calls=%async_computation.1 | async-start | bytes 524288 | tf_op jit(solution)/shard_map/all_to_all | solution.py:38
  48.9 5.2 %collective-permute-start.1 = (f32[448,128]{1,0:T(8,128)S(1)}, f32[448,128]{1,0:T(8,128)S(1)}, u32[]{:S(2)}, u32[]{:S(2)}) collective-permute-start(f32[448,128]{1,0:T(8,128)S(1)} %shard_map.166), channel_id=1, source_target_pairs={{0,3},{1,0},{2,1},{3,2},{4,7},{5,4},{6,5},{7,6},{8,11},{9,8},{10,9... | collective-permute-start | bytes 688136 | tf_op jit(solution)/shard_map/ppermute | solution.py:34
  54.1 3.9 %collective-permute-done.1.bucket_ref = f32[448,128]{1,0:T(8,128)S(1)} collective-permute-done((f32[448,128]{1,0:T(8,128)S(1)}, f32[448,128]{1,0:T(8,128)S(1)}, u32[]{:S(2)}, u32[]{:S(2)}) %collective-permute-start.1) | collective-permute-done | bytes 229408 | tf_op jit(solution)/shard_map/ppermute | solution.py:34
  58.0 5.6 %all-to-all-done.1 = f32[128,4,128]{2,1,0:T(4,128)S(1)} async-done(((f32[128,4,128]{2,1,0:T(4,128)}), f32[128,4,128]{2,1,0:T(4,128)S(1)}, u32[]{:S(2)}, u32[]{:S(2)}) %all-to-all-start.1) | async-done | bytes 262176 | tf_op jit(solution)/shard_map/all_to_all | solution.py:38
  63.6 2.9 %shard_map.167 = (f32[400,512]{1,0:T(8,128)S(1)}, f32[400,512]{1,0:T(8,128)S(1)}, f32[400,128]{1,0:T(8,128)S(1)}, f32[1,128]{1,0:T(1,128)S(1)}, f32[400,128]{1,0...) custom-call(s32[1,1]{1,0:T(1,128)} %bitcast.mine_ref, f32[512,128]{1,0:T(8,128)S(1)} %bitcast.30, ...), custom_call_target="tpu_custom_call" | custom-call | tf_op jit(solution)/shard_map/pallas_call | solution.py:60
  66.4 2.3 %collective-permute-start.2 = (f32[1280,128]{1,0:T(8,128)S(1)}, f32[1280,128]{1,0:T(8,128)S(1)}, u32[]{:S(2)}, u32[]{:S(2)}) collective-permute-start(f32[1280,128]{1,0:T(8,128)S(1)} %get-tuple-element.52), channel_id=1, source_target_pairs={{0,4},{4,0},{1,5},{5,1},{2,6},{6,2},{3,7},{7,3},{8,12},{12,8},{9,1... | collective-permute-start | bytes 1966088 | tf_op jit(solution)/shard_map/ppermute | solution.py:34
  69.2 1.2 collective-permute-done.2
  70.5 14.4 %all_to_all.56 = f32[4,320,128]{2,1,0:T(8,128)S(1)} all-to-all(f32[4,320,128]{2,1,0:T(8,128)S(1)} %bitcast.39), channel_id=1, replica_groups=mesh['z'=8,'y'=8,'core'=2,'x'=4] {'x'}, dimensions={0} | all-to-all | bytes 1310720 | tf_op jit(solution)/shard_map/all_to_all | solution.py:38
  84.9 11.0 %all_to_all.57 = f32[8,40,128]{2,1,0:T(8,128)S(1)} all-to-all(f32[8,40,128]{2,1,0:T(8,128)S(1)} %bitcast.41), channel_id=1, replica_groups=mesh['z'=8,'y'=8,'core'=2,'x'=4] {'y'}, dimensions={0} | all-to-all | bytes 327680 | tf_op jit(solution)/shard_map/all_to_all | solution.py:38
  96.0 14.9 %all_to_all.58 = f32[8,40,128]{2,1,0:T(8,128)S(1)} all-to-all(f32[8,40,128]{2,1,0:T(8,128)S(1)} %broadcast_in_dim.8), channel_id=1, replica_groups=mesh['z'=8,'y'=8,'core'=2,'x'=4] {'z'}, dimensions={0} | all-to-all | bytes 327680 | tf_op jit(solution)/shard_map/all_to_all | solution.py:38
  111.0 10.7 %all_to_all.59 = f32[8,40,128]{2,1,0:T(8,128)S(1)} all-to-all(f32[8,40,128]{2,1,0:T(8,128)S(1)} %broadcast_in_dim.9), channel_id=1, replica_groups=mesh['z'=8,'y'=8,'core'=2,'x'=4] {'y'}, dimensions={0} | all-to-all | bytes 327680 | tf_op jit(solution)/shard_map/all_to_all | solution.py:38
  121.7 10.0 %all_to_all.60 = f32[4,320,128]{2,1,0:T(8,128)S(1)} all-to-all(f32[4,320,128]{2,1,0:T(8,128)S(1)} %broadcast_in_dim.22), channel_id=1, replica_groups=mesh['z'=8,'y'=8,'core'=2,'x'=4] {'x'}, dimensions={0} | all-to-all | bytes 1310720 | tf_op jit(solution)/shard_map/all_to_all | solution.py:38
  131.7 8.7 %collective-permute-start.3 = (f32[1280,128]{1,0:T(8,128)S(1)}, f32[1280,128]{1,0:T(8,128)S(1)}, u32[]{:S(2)}, u32[]{:S(2)}) collective-permute-start(f32[1280,128]{1,0:T(8,128)S(1)} %bitcast.25), channel_id=1, source_target_pairs={{0,4},{4,0},{1,5},{5,1},{2,6},{6,2},{3,7},{7,3},{8,12},{12,8},{9,1... | collective-permute-start | bytes 1966088 | tf_op jit(solution)/shard_map/ppermute | solution.py:34
  142.1 3.7 %shard_map.170 = (f32[400,512]{1,0:T(8,128)S(1)}, f32[400,384]{1,0:T(8,128)S(1)}, f32[1,384]{1,0:T(1,128)S(1)}, f32[1536,128]{1,0:T(8,128)S(1)}, f32[1536,128]{1,0:T(8,128)S(1)}) custom-call(s32[1,1]{1,0:T(1,128)} %bitcast.mine_ref, s32[1,1]{1,0:T(1,128)} %collective-permute-done.partner_ref, f32[400,384]{1,0:T(8,128)S(1)} %get-tuple-element.65.own_ref.near_ref, ...), custom_call_target="tpu_custom_call" | custom-call | tf_op jit(solution)/shard_map/pallas_call | solution.py:60
  145.8 2.3 %collective-permute-start.4 = (f32[1536,128]{1,0:T(8,128)S(1)}, f32[1536,128]{1,0:T(8,128)S(1)}, u32[]{:S(2)}, u32[]{:S(2)}) collective-permute-start(f32[1536,128]{1,0:T(8,128)S(1)} %get-tuple-element.72), channel_id=1, source_target_pairs={{0,4},{4,0},{1,5},{5,1},{2,6},{6,2},{3,7},{7,3},{8,12},{12,8},{9,1... | collective-permute-start | bytes 2359304 | tf_op jit(solution)/shard_map/ppermute | solution.py:34
  148.4 1.6 collective-permute-done.4.got_ref
  150.1 13.0 %all_to_all.61.received_ref = f32[4,320,128]{2,1,0:T(8,128)S(1)} all-to-all(f32[4,320,128]{2,1,0:T(8,128)S(1)} %bitcast.40), channel_id=1, replica_groups=mesh['z'=8,'y'=8,'core'=2,'x'=4] {'x'}, dimensions={0} | all-to-all | bytes 1310720 | tf_op jit(solution)/shard_map/all_to_all | solution.py:38
  163.9 4.8 %all-to-all-start.8 = ((f32[64,3,4,128]{3,2,1,0:T(4,128)}), f32[64,3,4,128]{3,2,1,0:T(4,128)S(1)}, u32[]{:S(2)}, u32[]{:S(2)}) async-start(f32[64,3,4,128]{3,2,1,0:T(4,128)} %bitcast.16), calls=%async_computation.8 | async-start | bytes 786432 | tf_op jit(solution)/shard_map/all_to_all | solution.py:38
  168.7 2.2 collective-permute-start.5
  170.9 6.4 %collective-permute-done.5.source_ref = f32[408,128]{1,0:T(8,128)S(1)} collective-permute-done((f32[408,128]{1,0:T(8,128)S(1)}, f32[408,128]{1,0:T(8,128)S(1)}, u32[]{:S(2)}, u32[]{:S(2)}) %collective-permute-start.5) | collective-permute-done | bytes 208928 | tf_op jit(solution)/shard_map/ppermute | solution.py:34
  177.3 5.7 %all-to-all-done.8 = f32[64,3,4,128]{3,2,1,0:T(4,128)S(1)} async-done(((f32[64,3,4,128]{3,2,1,0:T(4,128)}), f32[64,3,4,128]{3,2,1,0:T(4,128)S(1)}, u32[]{:S(2)}, u32[]{:S(2)}) %all-to-all-start.8) | async-done | bytes 393248 | tf_op jit(solution)/shard_map/all_to_all | solution.py:38
  183.0 1.0 shard_map.173
  184.0 20.2 %all_to_all.62 = f32[64,3,4,128]{3,2,1,0:T(4,128)S(1)} all-to-all(f32[64,3,4,128]{3,2,1,0:T(4,128)S(1)} %bitcast.29), channel_id=1, replica_groups=mesh['z'=8,'y'=8,'core'=2,'x'=4] {'z','y'}, dimensions={0} | all-to-all | bytes 786432 | tf_op jit(solution)/shard_map/all_to_all | solution.py:38
  205.1 3.5 %all-to-all-start.10 = ((f32[4,320,128]{2,1,0:T(8,128)}), f32[4,320,128]{2,1,0:T(8,128)S(1)}, u32[]{:S(2)}, u32[]{:S(2)}) async-start(f32[4,320,128]{2,1,0:T(8,128)} %get-tuple-element.78), calls=%async_computation.10 | async-start | bytes 1310720 | tf_op jit(solution)/shard_map/all_to_all | solution.py:38
  208.6 6.5 %collective-permute-start.6 = (f32[256,128]{1,0:T(8,128)S(1)}, f32[256,128]{1,0:T(8,128)S(1)}, u32[]{:S(2)}, u32[]{:S(2)}) collective-permute-start(f32[256,128]{1,0:T(8,128)S(1)} %get-tuple-element.80), channel_id=1, source_target_pairs={{0,4},{4,0},{1,5},{5,1},{2,6},{6,2},{3,7},{7,3},{8,12},{12,8},{9,1... | collective-permute-start | bytes 393224 | tf_op jit(solution)/shard_map/ppermute | solution.py:34
  215.1 1.0 collective-permute-done.6.other_ref
  216.9 6.9 %collective-permute-start.7 = (f32[1280,128]{1,0:T(8,128)S(1)}, f32[1280,128]{1,0:T(8,128)S(1)}, u32[]{:S(2)}, u32[]{:S(2)}) collective-permute-start(f32[1280,128]{1,0:T(8,128)S(1)} %bitcast.23), channel_id=1, source_target_pairs={{0,4},{4,0},{1,5},{5,1},{2,6},{6,2},{3,7},{7,3},{8,12},{12,8},{9,1... | collective-permute-start | bytes 1966088 | tf_op jit(solution)/shard_map/ppermute | solution.py:34
  224.0 1.5 collective-permute-done.7.other_ref
  225.5 1.3 shard_map.177
  (43 shorter events, 8.6 us)
Async XLA Ops:
  0.6 6.3 %collective-permute-start = (s32[1,1]{1,0:T(1,128)}, s32[1,1]{1,0:T(1,128)}, u32[]{:S(2)}, u32[]{:S(2)}) collective-permute-start(s32[1,1]{1,0:T(1,128)} %param.18), channel_id=1, source_target_pairs={{0,3},{1,0},{2,1},{3,2},{4,7},{5,4},{6,5},{7,6},{8,11},{9,8},{10,9... | collective-permute-start | bytes 20 | tf_op jit(solution)/shard_map/ppermute | solution.py:34
  5.9 0.9 copy-start.1
  6.8 42.0 %copy-start.2 = (f32[400,128]{1,0:T(8,128)S(1)}, f32[400,128]{1,0:T(8,128)}, u32[]{:S(2)}) copy-start(f32[400,128]{1,0:T(8,128)} %source_ref.1) | copy-start | bytes 614404
  6.8 42.0 %copy-start.3 = (s32[1,1,2048]{2,1,0:T(1,128)S(1)}, s32[1,1,2048]{2,1,0:T(1,128)}, u32[]{:S(2)}) copy-start(s32[1,1,2048]{2,1,0:T(1,128)} %param.23) | copy-start | bytes 24580
  6.8 42.1 %copy-start.4 = (s32[1,1,1024]{2,1,0:T(1,128)S(1)}, s32[1,1,1024]{2,1,0:T(1,128)}, u32[]{:S(2)}) copy-start(s32[1,1,1024]{2,1,0:T(1,128)} %param.20) | copy-start | bytes 12292
  6.8 42.1 %copy-start.5 = (s32[1,1,1024]{2,1,0:T(1,128)S(1)}, s32[1,1,1024]{2,1,0:T(1,128)}, u32[]{:S(2)}) copy-start(s32[1,1,1024]{2,1,0:T(1,128)} %param.21) | copy-start | bytes 12292
  6.8 42.1 %copy-start.6 = (s32[1,1,1024]{2,1,0:T(1,128)S(1)}, s32[1,1,1024]{2,1,0:T(1,128)}, u32[]{:S(2)}) copy-start(s32[1,1,1024]{2,1,0:T(1,128)} %param.22) | copy-start | bytes 12292
  6.8 42.1 %copy-start.7 = (f32[128]{0:T(128)S(1)}, f32[128]{0:T(128)}, u32[]{:S(2)}) copy-start(f32[128]{0:T(128)} %param.13) | copy-start | bytes 1540
  7.0 0.7 copy-start.8
  7.6 55.9 %copy-start = (f32[400,768]{1,0:T(8,128)S(1)}, f32[400,768]{1,0:T(8,128)}, u32[]{:S(2)}) copy-start(f32[400,768]{1,0:T(8,128)} %relations_ref.5) | copy-start | bytes 3686404
  42.6 20.9 %all-to-all-start.1 = ((f32[128,4,128]{2,1,0:T(4,128)}), f32[128,4,128]{2,1,0:T(4,128)S(1)}, u32[]{:S(2)}, u32[]{:S(2)}) async-start(f32[128,4,128]{2,1,0:T(4,128)} %bitcast.4), calls=%async_computation.1 | async-start | bytes 524288 | tf_op jit(solution)/shard_map/all_to_all | solution.py:38
  48.9 9.1 %collective-permute-start.1 = (f32[448,128]{1,0:T(8,128)S(1)}, f32[448,128]{1,0:T(8,128)S(1)}, u32[]{:S(2)}, u32[]{:S(2)}) collective-permute-start(f32[448,128]{1,0:T(8,128)S(1)} %shard_map.166), channel_id=1, source_target_pairs={{0,3},{1,0},{2,1},{3,2},{4,7},{5,4},{6,5},{7,6},{8,11},{9,8},{10,9... | collective-permute-start | bytes 688136 | tf_op jit(solution)/shard_map/ppermute | solution.py:34
  66.4 4.0 %collective-permute-start.2 = (f32[1280,128]{1,0:T(8,128)S(1)}, f32[1280,128]{1,0:T(8,128)S(1)}, u32[]{:S(2)}, u32[]{:S(2)}) collective-permute-start(f32[1280,128]{1,0:T(8,128)S(1)} %get-tuple-element.52), channel_id=1, source_target_pairs={{0,4},{4,0},{1,5},{5,1},{2,6},{6,2},{3,7},{7,3},{8,12},{12,8},{9,1... | collective-permute-start | bytes 1966088 | tf_op jit(solution)/shard_map/ppermute | solution.py:34
  111.0 29.4 %copy-start.9 = (f32[768]{0:T(1024)S(1)}, f32[768]{0:T(1024)}, u32[]{:S(2)}) copy-start(f32[768]{0:T(1024)} %param.17) | copy-start | bytes 9220
  131.7 10.4 %collective-permute-start.3 = (f32[1280,128]{1,0:T(8,128)S(1)}, f32[1280,128]{1,0:T(8,128)S(1)}, u32[]{:S(2)}, u32[]{:S(2)}) collective-permute-start(f32[1280,128]{1,0:T(8,128)S(1)} %bitcast.25), channel_id=1, source_target_pairs={{0,4},{4,0},{1,5},{5,1},{2,6},{6,2},{3,7},{7,3},{8,12},{12,8},{9,1... | collective-permute-start | bytes 1966088 | tf_op jit(solution)/shard_map/ppermute | solution.py:34
  145.8 4.2 %collective-permute-start.4 = (f32[1536,128]{1,0:T(8,128)S(1)}, f32[1536,128]{1,0:T(8,128)S(1)}, u32[]{:S(2)}, u32[]{:S(2)}) collective-permute-start(f32[1536,128]{1,0:T(8,128)S(1)} %get-tuple-element.72), channel_id=1, source_target_pairs={{0,4},{4,0},{1,5},{5,1},{2,6},{6,2},{3,7},{7,3},{8,12},{12,8},{9,1... | collective-permute-start | bytes 2359304 | tf_op jit(solution)/shard_map/ppermute | solution.py:34
  163.9 19.1 %all-to-all-start.8 = ((f32[64,3,4,128]{3,2,1,0:T(4,128)}), f32[64,3,4,128]{3,2,1,0:T(4,128)S(1)}, u32[]{:S(2)}, u32[]{:S(2)}) async-start(f32[64,3,4,128]{3,2,1,0:T(4,128)} %bitcast.16), calls=%async_computation.8 | async-start | bytes 786432 | tf_op jit(solution)/shard_map/all_to_all | solution.py:38
  168.7 8.6 %collective-permute-start.5 = (f32[408,128]{1,0:T(8,128)S(1)}, f32[408,128]{1,0:T(8,128)S(1)}, u32[]{:S(2)}, u32[]{:S(2)}) collective-permute-start(f32[408,128]{1,0:T(8,128)S(1)} %shard_map.171), channel_id=1, source_target_pairs={{0,1},{1,2},{2,3},{3,0},{4,5},{5,6},{6,7},{7,4},{8,9},{9,10},{10,1... | collective-permute-start | bytes 626696 | tf_op jit(solution)/shard_map/ppermute | solution.py:34
  205.1 11.8 %all-to-all-start.10 = ((f32[4,320,128]{2,1,0:T(8,128)}), f32[4,320,128]{2,1,0:T(8,128)S(1)}, u32[]{:S(2)}, u32[]{:S(2)}) async-start(f32[4,320,128]{2,1,0:T(8,128)} %get-tuple-element.78), calls=%async_computation.10 | async-start | bytes 1310720 | tf_op jit(solution)/shard_map/all_to_all | solution.py:38
  208.6 7.5 %collective-permute-start.6 = (f32[256,128]{1,0:T(8,128)S(1)}, f32[256,128]{1,0:T(8,128)S(1)}, u32[]{:S(2)}, u32[]{:S(2)}) collective-permute-start(f32[256,128]{1,0:T(8,128)S(1)} %get-tuple-element.80), channel_id=1, source_target_pairs={{0,4},{4,0},{1,5},{5,1},{2,6},{6,2},{3,7},{7,3},{8,12},{12,8},{9,1... | collective-permute-start | bytes 393224 | tf_op jit(solution)/shard_map/ppermute | solution.py:34
  216.9 8.6 %collective-permute-start.7 = (f32[1280,128]{1,0:T(8,128)S(1)}, f32[1280,128]{1,0:T(8,128)S(1)}, u32[]{:S(2)}, u32[]{:S(2)}) collective-permute-start(f32[1280,128]{1,0:T(8,128)S(1)} %bitcast.23), channel_id=1, source_target_pairs={{0,4},{4,0},{1,5},{5,1},{2,6},{6,2},{3,7},{7,3},{8,12},{12,8},{9,1... | collective-permute-start | bytes 1966088 | tf_op jit(solution)/shard_map/ppermute | solution.py:34

commit v8 on v7

--- a/solution.py
+++ b/solution.py
@@ -601,7 +601,7 @@
         scalars=1,
     )
     bucket = passed_along(bucket, "x", -1)
-    spread = dealt(cargo, DOM, BLOCK)
+    spread, bucket = lax.optimization_barrier((dealt(cargo, DOM, BLOCK), bucket))
     (spread,) = kernel_call(pick_body, [tile], [spread])
     arrived = dealt(spread, DOM, BLOCK)
     block = ((DIM, BLOCK), f32)

time: 228 us -> 229 us (level)
  blocking collectives: 127 us -> 90.1 us
  starting transfers between devices: 53.1 us -> 75 us
  waiting for transfers between devices: 27.6 us -> 42.9 us
    all_to_all x8 -> x7, blocking collectives: 127 us -> 90.1 us  [exchange(): return lax.all_to_all(value, axis, split_axis=0, concat_axis=0, tiled=True)]
    all_to_all x3 -> x4, starting transfers between devices: 13.8 us -> 36.2 us  [exchange(): return lax.all_to_all(value, axis, split_axis=0, concat_axis=0, tiled=True)]
    all_to_all x3 -> x4, waiting for transfers between devices: 11.3 us -> 26.5 us  [exchange(): return lax.all_to_all(value, axis, split_axis=0, concat_axis=0, tiled=True)]
  transfers between devices with their start and end apart: 11 -> 12, of which waited for: 9 -> 10; matrix products, arithmetic and copies ran while one was open for 0% -> 0% of each run, Pallas kernels for 1% -> 1%
where the time goes in v8:
time: 229 us; the launch traced here: 228 us
  blocking collectives  90.1 us (39%)
  starting transfers between devices  75 us (33%)
  waiting for transfers between devices  42.9 us (19%)
  Pallas kernels  16 us (7%)
    all_to_all x7, blocking collectives, exchange(): return lax.all_to_all(value, axis, split_axis=0, concat_axis=0, tiled=True)  90.1 us
    ppermute x8, starting transfers between devices, passed_along(): return lax.ppermute(value, axis, pairs)  38.9 us
    all_to_all x4, starting transfers between devices, exchange(): return lax.all_to_all(value, axis, split_axis=0, concat_axis=0, tiled=True)  36.2 us
    all_to_all x4, waiting for transfers between devices, exchange(): return lax.all_to_all(value, axis, split_axis=0, concat_axis=0, tiled=True)  26.5 us
    ppermute x8, waiting for transfers between devices, passed_along(): return lax.ppermute(value, axis, pairs)  16.4 us
    pallas_call x15, Pallas kernels, kernel_call(): pl.pallas_call(body, out_shape=[jax.ShapeDtypeStruct(shape, dtype) for sh...  16 us
  transfers between devices with their start and end apart: 12, of which 10 were waited for; matrix products, arithmetic and copies ran while one was open for 0% of the time, Pallas kernels for 1%

profile of v8, /device:TPU:1, one launch (start us, length us, event | category | flops | bytes accessed | tf_op | source)
XLA Modules:
  0.0 228.2 jit_solution(2336348214912814201)
XLA Ops:
  0.6 5.2 %collective-permute-start = (s32[1,1]{1,0:T(1,128)}, s32[1,1]{1,0:T(1,128)}, u32[]{:S(2)}, u32[]{:S(2)}) collective-permute-start(s32[1,1]{1,0:T(1,128)} %param.18), channel_id=1, source_target_pairs={{0,3},{1,0},{2,1},{3,2},{4,7},{5,4},{6,5},{7,6},{8,11},{9,8},{10,9... | collective-permute-start | bytes 20 | tf_op jit(solution)/shard_map/ppermute | solution.py:34
  7.6 1.5 shard_map.164
  9.2 18.2 %all-to-all-start = ((f32[128,4,128]{2,1,0:T(4,128)}), f32[128,4,128]{2,1,0:T(4,128)S(1)}, u32[]{:S(2)}, u32[]{:S(2)}) async-start(f32[128,4,128]{2,1,0:T(4,128)} %bitcast.2), calls=%async_computation | async-start | bytes 524288 | tf_op jit(solution)/shard_map/all_to_all | solution.py:38
  28.1 5.0 %collective-permute-start.1 = (f32[448,128]{1,0:T(8,128)S(1)}, f32[448,128]{1,0:T(8,128)S(1)}, u32[]{:S(2)}, u32[]{:S(2)}) collective-permute-start(f32[448,128]{1,0:T(8,128)S(1)} %shard_map.165), channel_id=1, source_target_pairs={{0,3},{1,0},{2,1},{3,2},{4,7},{5,4},{6,5},{7,6},{8,11},{9,8},{10,9... | collective-permute-start | bytes 688136 | tf_op jit(solution)/shard_map/ppermute | solution.py:34
  33.1 4.0 %collective-permute-done.1.bucket_ref = f32[448,128]{1,0:T(8,128)S(1)} collective-permute-done((f32[448,128]{1,0:T(8,128)S(1)}, f32[448,128]{1,0:T(8,128)S(1)}, u32[]{:S(2)}, u32[]{:S(2)}) %collective-permute-start.1) | collective-permute-done | bytes 229408 | tf_op jit(solution)/shard_map/ppermute | solution.py:34
  37.1 5.5 %all-to-all-done = f32[128,4,128]{2,1,0:T(4,128)S(1)} async-done(((f32[128,4,128]{2,1,0:T(4,128)}), f32[128,4,128]{2,1,0:T(4,128)S(1)}, u32[]{:S(2)}, u32[]{:S(2)}) %all-to-all-start) | async-done | bytes 262176 | tf_op jit(solution)/shard_map/all_to_all | solution.py:38
  42.6 1.0 shard_map.166
  43.6 9.7 %all-to-all-start.1 = ((f32[128,4,128]{2,1,0:T(4,128)}), f32[128,4,128]{2,1,0:T(4,128)S(1)}, u32[]{:S(2)}, u32[]{:S(2)}) async-start(f32[128,4,128]{2,1,0:T(4,128)} %bitcast.9), calls=%async_computation.1 | async-start | bytes 524288 | tf_op jit(solution)/shard_map/all_to_all | solution.py:38
  53.3 15.3 %all-to-all-done.1 = f32[128,4,128]{2,1,0:T(4,128)S(1)} async-done(((f32[128,4,128]{2,1,0:T(4,128)}), f32[128,4,128]{2,1,0:T(4,128)S(1)}, u32[]{:S(2)}, u32[]{:S(2)}) %all-to-all-start.1) | async-done | bytes 262176 | tf_op jit(solution)/shard_map/all_to_all | solution.py:38
  68.6 2.9 %shard_map.167 = (f32[400,512]{1,0:T(8,128)S(1)}, f32[400,512]{1,0:T(8,128)S(1)}, f32[400,128]{1,0:T(8,128)S(1)}, f32[1,128]{1,0:T(1,128)S(1)}, f32[400,128]{1,0...) custom-call(s32[1,1]{1,0:T(1,128)} %bitcast.mine_ref, f32[512,128]{1,0:T(8,128)S(1)} %bitcast.30, ...), custom_call_target="tpu_custom_call" | custom-call | tf_op jit(solution)/shard_map/pallas_call | solution.py:60
  71.5 2.3 collective-permute-start.2
  74.3 1.2 collective-permute-done.2
  75.6 14.5 %all_to_all.55 = f32[4,320,128]{2,1,0:T(8,128)S(1)} all-to-all(f32[4,320,128]{2,1,0:T(8,128)S(1)} %bitcast.38), channel_id=1, replica_groups=mesh['z'=8,'y'=8,'core'=2,'x'=4] {'x'}, dimensions={0} | all-to-all | bytes 1310720 | tf_op jit(solution)/shard_map/all_to_all | solution.py:38
  90.1 11.0 %all_to_all.56 = f32[8,40,128]{2,1,0:T(8,128)S(1)} all-to-all(f32[8,40,128]{2,1,0:T(8,128)S(1)} %bitcast.40), channel_id=1, replica_groups=mesh['z'=8,'y'=8,'core'=2,'x'=4] {'y'}, dimensions={0} | all-to-all | bytes 327680 | tf_op jit(solution)/shard_map/all_to_all | solution.py:38
  101.1 10.7 %all_to_all.57 = f32[8,40,128]{2,1,0:T(8,128)S(1)} all-to-all(f32[8,40,128]{2,1,0:T(8,128)S(1)} %broadcast_in_dim.8), channel_id=1, replica_groups=mesh['z'=8,'y'=8,'core'=2,'x'=4] {'z'}, dimensions={0} | all-to-all | bytes 327680 | tf_op jit(solution)/shard_map/all_to_all | solution.py:38
  111.9 10.7 %all_to_all.58 = f32[8,40,128]{2,1,0:T(8,128)S(1)} all-to-all(f32[8,40,128]{2,1,0:T(8,128)S(1)} %broadcast_in_dim.9), channel_id=1, replica_groups=mesh['z'=8,'y'=8,'core'=2,'x'=4] {'y'}, dimensions={0} | all-to-all | bytes 327680 | tf_op jit(solution)/shard_map/all_to_all | solution.py:38
  122.6 10.0 %all_to_all.59 = f32[4,320,128]{2,1,0:T(8,128)S(1)} all-to-all(f32[4,320,128]{2,1,0:T(8,128)S(1)} %broadcast_in_dim.22), channel_id=1, replica_groups=mesh['z'=8,'y'=8,'core'=2,'x'=4] {'x'}, dimensions={0} | all-to-all | bytes 1310720 | tf_op jit(solution)/shard_map/all_to_all | solution.py:38
  132.7 8.5 %collective-permute-start.3 = (f32[1280,128]{1,0:T(8,128)S(1)}, f32[1280,128]{1,0:T(8,128)S(1)}, u32[]{:S(2)}, u32[]{:S(2)}) collective-permute-start(f32[1280,128]{1,0:T(8,128)S(1)} %bitcast.25), channel_id=1, source_target_pairs={{0,4},{4,0},{1,5},{5,1},{2,6},{6,2},{3,7},{7,3},{8,12},{12,8},{9,1... | collective-permute-start | bytes 1966088 | tf_op jit(solution)/shard_map/ppermute | solution.py:34
  142.8 3.8 %shard_map.170 = (f32[400,512]{1,0:T(8,128)S(1)}, f32[400,384]{1,0:T(8,128)S(1)}, f32[1,384]{1,0:T(1,128)S(1)}, f32[1536,128]{1,0:T(8,128)S(1)}, f32[1536,128]{1,0:T(8,128)S(1)}) custom-call(s32[1,1]{1,0:T(1,128)} %bitcast.mine_ref, s32[1,1]{1,0:T(1,128)} %collective-permute-done.partner_ref, f32[400,384]{1,0:T(8,128)S(1)} %get-tuple-element.69.own_ref.near_ref, ...), custom_call_target="tpu_custom_call" | custom-call | tf_op jit(solution)/shard_map/pallas_call | solution.py:60
  146.6 2.3 collective-permute-start.4
  149.2 1.6 collective-permute-done.4.got_ref
  150.9 13.0 %all_to_all.60.received_ref = f32[4,320,128]{2,1,0:T(8,128)S(1)} all-to-all(f32[4,320,128]{2,1,0:T(8,128)S(1)} %bitcast.39), channel_id=1, replica_groups=mesh['z'=8,'y'=8,'core'=2,'x'=4] {'x'}, dimensions={0} | all-to-all | bytes 1310720 | tf_op jit(solution)/shard_map/all_to_all | solution.py:38
  164.7 4.8 %all-to-all-start.8 = ((f32[64,3,4,128]{3,2,1,0:T(4,128)}), f32[64,3,4,128]{3,2,1,0:T(4,128)S(1)}, u32[]{:S(2)}, u32[]{:S(2)}) async-start(f32[64,3,4,128]{3,2,1,0:T(4,128)} %bitcast.16), calls=%async_computation.8 | async-start | bytes 786432 | tf_op jit(solution)/shard_map/all_to_all | solution.py:38
  169.5 2.2 collective-permute-start.5
  171.7 6.4 %collective-permute-done.5.source_ref = f32[408,128]{1,0:T(8,128)S(1)} collective-permute-done((f32[408,128]{1,0:T(8,128)S(1)}, f32[408,128]{1,0:T(8,128)S(1)}, u32[]{:S(2)}, u32[]{:S(2)}) %collective-permute-start.5) | collective-permute-done | bytes 208928 | tf_op jit(solution)/shard_map/ppermute | solution.py:34
  178.1 5.7 %all-to-all-done.8 = f32[64,3,4,128]{3,2,1,0:T(4,128)S(1)} async-done(((f32[64,3,4,128]{3,2,1,0:T(4,128)}), f32[64,3,4,128]{3,2,1,0:T(4,128)S(1)}, u32[]{:S(2)}, u32[]{:S(2)}) %all-to-all-start.8) | async-done | bytes 393248 | tf_op jit(solution)/shard_map/all_to_all | solution.py:38
  184.8 20.2 %all_to_all.61 = f32[64,3,4,128]{3,2,1,0:T(4,128)S(1)} all-to-all(f32[64,3,4,128]{3,2,1,0:T(4,128)S(1)} %bitcast.29), channel_id=1, replica_groups=mesh['z'=8,'y'=8,'core'=2,'x'=4] {'z','y'}, dimensions={0} | all-to-all | bytes 786432 | tf_op jit(solution)/shard_map/all_to_all | solution.py:38
  205.9 3.5 %all-to-all-start.10 = ((f32[4,320,128]{2,1,0:T(8,128)}), f32[4,320,128]{2,1,0:T(8,128)S(1)}, u32[]{:S(2)}, u32[]{:S(2)}) async-start(f32[4,320,128]{2,1,0:T(8,128)} %get-tuple-element.82), calls=%async_computation.10 | async-start | bytes 1310720 | tf_op jit(solution)/shard_map/all_to_all | solution.py:38
  209.4 6.5 %collective-permute-start.6 = (f32[256,128]{1,0:T(8,128)S(1)}, f32[256,128]{1,0:T(8,128)S(1)}, u32[]{:S(2)}, u32[]{:S(2)}) collective-permute-start(f32[256,128]{1,0:T(8,128)S(1)} %get-tuple-element.84), channel_id=1, source_target_pairs={{0,4},{4,0},{1,5},{5,1},{2,6},{6,2},{3,7},{7,3},{8,12},{12,8},{9,1... | collective-permute-start | bytes 393224 | tf_op jit(solution)/shard_map/ppermute | solution.py:34
  217.7 6.9 %collective-permute-start.7 = (f32[1280,128]{1,0:T(8,128)S(1)}, f32[1280,128]{1,0:T(8,128)S(1)}, u32[]{:S(2)}, u32[]{:S(2)}) collective-permute-start(f32[1280,128]{1,0:T(8,128)S(1)} %bitcast.23), channel_id=1, source_target_pairs={{0,4},{4,0},{1,5},{5,1},{2,6},{6,2},{3,7},{7,3},{8,12},{12,8},{9,1... | collective-permute-start | bytes 1966088 | tf_op jit(solution)/shard_map/ppermute | solution.py:34
  224.8 1.5 collective-permute-done.7.other_ref
  226.3 1.3 shard_map.177
  (44 shorter events, 9.8 us)
Async XLA Ops:
  0.6 6.3 %collective-permute-start = (s32[1,1]{1,0:T(1,128)}, s32[1,1]{1,0:T(1,128)}, u32[]{:S(2)}, u32[]{:S(2)}) collective-permute-start(s32[1,1]{1,0:T(1,128)} %param.18), channel_id=1, source_target_pairs={{0,3},{1,0},{2,1},{3,2},{4,7},{5,4},{6,5},{7,6},{8,11},{9,8},{10,9... | collective-permute-start | bytes 20 | tf_op jit(solution)/shard_map/ppermute | solution.py:34
  5.9 0.9 copy-start.1
  6.8 21.2 %copy-start.2 = (f32[400,128]{1,0:T(8,128)S(1)}, f32[400,128]{1,0:T(8,128)}, u32[]{:S(2)}) copy-start(f32[400,128]{1,0:T(8,128)} %source_ref.1) | copy-start | bytes 614404
  6.8 21.2 %copy-start.3 = (s32[1,1,2048]{2,1,0:T(1,128)S(1)}, s32[1,1,2048]{2,1,0:T(1,128)}, u32[]{:S(2)}) copy-start(s32[1,1,2048]{2,1,0:T(1,128)} %param.23) | copy-start | bytes 24580
  6.8 21.2 %copy-start.4 = (s32[1,1,1024]{2,1,0:T(1,128)S(1)}, s32[1,1,1024]{2,1,0:T(1,128)}, u32[]{:S(2)}) copy-start(s32[1,1,1024]{2,1,0:T(1,128)} %param.20) | copy-start | bytes 12292
  6.8 21.2 %copy-start.5 = (s32[1,1,1024]{2,1,0:T(1,128)S(1)}, s32[1,1,1024]{2,1,0:T(1,128)}, u32[]{:S(2)}) copy-start(s32[1,1,1024]{2,1,0:T(1,128)} %param.21) | copy-start | bytes 12292
  6.8 21.2 %copy-start.6 = (s32[1,1,1024]{2,1,0:T(1,128)S(1)}, s32[1,1,1024]{2,1,0:T(1,128)}, u32[]{:S(2)}) copy-start(s32[1,1,1024]{2,1,0:T(1,128)} %param.22) | copy-start | bytes 12292
  6.8 21.2 %copy-start.7 = (f32[128]{0:T(128)S(1)}, f32[128]{0:T(128)}, u32[]{:S(2)}) copy-start(f32[128]{0:T(128)} %param.13) | copy-start | bytes 1540
  7.0 0.7 copy-start.8
  7.6 60.9 %copy-start = (f32[400,768]{1,0:T(8,128)S(1)}, f32[400,768]{1,0:T(8,128)}, u32[]{:S(2)}) copy-start(f32[400,768]{1,0:T(8,128)} %relations_ref.5) | copy-start | bytes 3686404
  9.2 33.4 %all-to-all-start = ((f32[128,4,128]{2,1,0:T(4,128)}), f32[128,4,128]{2,1,0:T(4,128)S(1)}, u32[]{:S(2)}, u32[]{:S(2)}) async-start(f32[128,4,128]{2,1,0:T(4,128)} %bitcast.2), calls=%async_computation | async-start | bytes 524288 | tf_op jit(solution)/shard_map/all_to_all | solution.py:38
  28.1 9.0 %collective-permute-start.1 = (f32[448,128]{1,0:T(8,128)S(1)}, f32[448,128]{1,0:T(8,128)S(1)}, u32[]{:S(2)}, u32[]{:S(2)}) collective-permute-start(f32[448,128]{1,0:T(8,128)S(1)} %shard_map.165), channel_id=1, source_target_pairs={{0,3},{1,0},{2,1},{3,2},{4,7},{5,4},{6,5},{7,6},{8,11},{9,8},{10,9... | collective-permute-start | bytes 688136 | tf_op jit(solution)/shard_map/ppermute | solution.py:34
  43.6 25.0 %all-to-all-start.1 = ((f32[128,4,128]{2,1,0:T(4,128)}), f32[128,4,128]{2,1,0:T(4,128)S(1)}, u32[]{:S(2)}, u32[]{:S(2)}) async-start(f32[128,4,128]{2,1,0:T(4,128)} %bitcast.9), calls=%async_computation.1 | async-start | bytes 524288 | tf_op jit(solution)/shard_map/all_to_all | solution.py:38
  71.5 4.0 %collective-permute-start.2 = (f32[1280,128]{1,0:T(8,128)S(1)}, f32[1280,128]{1,0:T(8,128)S(1)}, u32[]{:S(2)}, u32[]{:S(2)}) collective-permute-start(f32[1280,128]{1,0:T(8,128)S(1)} %get-tuple-element.56), channel_id=1, source_target_pairs={{0,4},{4,0},{1,5},{5,1},{2,6},{6,2},{3,7},{7,3},{8,12},{12,8},{9,1... | collective-permute-start | bytes 1966088 | tf_op jit(solution)/shard_map/ppermute | solution.py:34
  111.9 29.2 %copy-start.9 = (f32[768]{0:T(1024)S(1)}, f32[768]{0:T(1024)}, u32[]{:S(2)}) copy-start(f32[768]{0:T(1024)} %param.17) | copy-start | bytes 9220
  132.7 10.2 %collective-permute-start.3 = (f32[1280,128]{1,0:T(8,128)S(1)}, f32[1280,128]{1,0:T(8,128)S(1)}, u32[]{:S(2)}, u32[]{:S(2)}) collective-permute-start(f32[1280,128]{1,0:T(8,128)S(1)} %bitcast.25), channel_id=1, source_target_pairs={{0,4},{4,0},{1,5},{5,1},{2,6},{6,2},{3,7},{7,3},{8,12},{12,8},{9,1... | collective-permute-start | bytes 1966088 | tf_op jit(solution)/shard_map/ppermute | solution.py:34
  146.6 4.2 %collective-permute-start.4 = (f32[1536,128]{1,0:T(8,128)S(1)}, f32[1536,128]{1,0:T(8,128)S(1)}, u32[]{:S(2)}, u32[]{:S(2)}) collective-permute-start(f32[1536,128]{1,0:T(8,128)S(1)} %get-tuple-element.76), channel_id=1, source_target_pairs={{0,4},{4,0},{1,5},{5,1},{2,6},{6,2},{3,7},{7,3},{8,12},{12,8},{9,1... | collective-permute-start | bytes 2359304 | tf_op jit(solution)/shard_map/ppermute | solution.py:34
  164.7 19.1 %all-to-all-start.8 = ((f32[64,3,4,128]{3,2,1,0:T(4,128)}), f32[64,3,4,128]{3,2,1,0:T(4,128)S(1)}, u32[]{:S(2)}, u32[]{:S(2)}) async-start(f32[64,3,4,128]{3,2,1,0:T(4,128)} %bitcast.16), calls=%async_computation.8 | async-start | bytes 786432 | tf_op jit(solution)/shard_map/all_to_all | solution.py:38
  169.5 8.6 %collective-permute-start.5 = (f32[408,128]{1,0:T(8,128)S(1)}, f32[408,128]{1,0:T(8,128)S(1)}, u32[]{:S(2)}, u32[]{:S(2)}) collective-permute-start(f32[408,128]{1,0:T(8,128)S(1)} %shard_map.171), channel_id=1, source_target_pairs={{0,1},{1,2},{2,3},{3,0},{4,5},{5,6},{6,7},{7,4},{8,9},{9,10},{10,1... | collective-permute-start | bytes 626696 | tf_op jit(solution)/shard_map/ppermute | solution.py:34
  205.9 11.8 %all-to-all-start.10 = ((f32[4,320,128]{2,1,0:T(8,128)}), f32[4,320,128]{2,1,0:T(8,128)S(1)}, u32[]{:S(2)}, u32[]{:S(2)}) async-start(f32[4,320,128]{2,1,0:T(8,128)} %get-tuple-element.82), calls=%async_computation.10 | async-start | bytes 1310720 | tf_op jit(solution)/shard_map/all_to_all | solution.py:38
  209.4 7.5 %collective-permute-start.6 = (f32[256,128]{1,0:T(8,128)S(1)}, f32[256,128]{1,0:T(8,128)S(1)}, u32[]{:S(2)}, u32[]{:S(2)}) collective-permute-start(f32[256,128]{1,0:T(8,128)S(1)} %get-tuple-element.84), channel_id=1, source_target_pairs={{0,4},{4,0},{1,5},{5,1},{2,6},{6,2},{3,7},{7,3},{8,12},{12,8},{9,1... | collective-permute-start | bytes 393224 | tf_op jit(solution)/shard_map/ppermute | solution.py:34
  217.7 8.6 %collective-permute-start.7 = (f32[1280,128]{1,0:T(8,128)S(1)}, f32[1280,128]{1,0:T(8,128)S(1)}, u32[]{:S(2)}, u32[]{:S(2)}) collective-permute-start(f32[1280,128]{1,0:T(8,128)S(1)} %bitcast.23), channel_id=1, source_target_pairs={{0,4},{4,0},{1,5},{5,1},{2,6},{6,2},{3,7},{7,3},{8,12},{12,8},{9,1... | collective-permute-start | bytes 1966088 | tf_op jit(solution)/shard_map/ppermute | solution.py:34

commit v9 on v5

--- a/solution.py
+++ b/solution.py
@@ -670,10 +670,10 @@
     packet = ((64 * ROWS, LANES), f32)
     (packed,) = kernel_call(merge_body, [packet], [received, keep, got])
     packed = packets(packed, ("z", "y"), 64)
-    packed, source = lax.optimization_barrier((packed, source))
     (packed,) = kernel_call(middle_body, [packet], [mine, packed], [turned], scalars=1)
     packed = packets(packed, ("z", "y"), 64)
     pieces = ((64 * PIECE, LANES), f32)
+    packed, source = lax.optimization_barrier((packed, source))
     sums, returned, sibling = kernel_call(
         parting_body, [((4, 320, LANES), f32), pieces, pieces], [packed]
     )

time: 227 us -> 227 us (level)
  no operation moved by 1% of the time
where the time goes in v9:
time: 227 us; the launch traced here: 226 us
  blocking collectives  125 us (55%)
  starting transfers between devices  54.3 us (24%)
  waiting for transfers between devices  27.6 us (12%)
  Pallas kernels  15.1 us (7%)
    all_to_all x8, blocking collectives, exchange(): return lax.all_to_all(value, axis, split_axis=0, concat_axis=0, tiled=True)  125 us
    ppermute x8, starting transfers between devices, passed_along(): return lax.ppermute(value, axis, pairs)  38.6 us
    ppermute x8, waiting for transfers between devices, passed_along(): return lax.ppermute(value, axis, pairs)  15.8 us
    all_to_all x3, starting transfers between devices, exchange(): return lax.all_to_all(value, axis, split_axis=0, concat_axis=0, tiled=True)  15.7 us
    pallas_call x15, Pallas kernels, kernel_call(): pl.pallas_call(body, out_shape=[jax.ShapeDtypeStruct(shape, dtype) for sh...  15.1 us
    all_to_all x3, waiting for transfers between devices, exchange(): return lax.all_to_all(value, axis, split_axis=0, concat_axis=0, tiled=True)  11.8 us
  transfers between devices with their start and end apart: 11, of which 9 were waited for; matrix products, arithmetic and copies ran while one was open for 0% of the time, Pallas kernels for 1%

profile of v9, /device:TPU:1, one launch (start us, length us, event | category | flops | bytes accessed | tf_op | source)
XLA Modules:
  0.0 225.9 jit_solution(3415537793990396981)
XLA Ops:
  0.6 5.2 %collective-permute-start = (s32[1,1]{1,0:T(1,128)}, s32[1,1]{1,0:T(1,128)}, u32[]{:S(2)}, u32[]{:S(2)}) collective-permute-start(s32[1,1]{1,0:T(1,128)} %param.18), channel_id=1, source_target_pairs={{0,3},{1,0},{2,1},{3,2},{4,7},{5,4},{6,5},{7,6},{8,11},{9,8},{10,9... | collective-permute-start | bytes 20 | tf_op jit(solution)/shard_map/ppermute | solution.py:34
  8.3 32.9 %all_to_all.55 = f32[128,4,128]{2,1,0:T(4,128)S(1)} all-to-all(f32[128,4,128]{2,1,0:T(4,128)S(1)} %bitcast.31), channel_id=1, replica_groups=mesh['z'=8,'y'=8,'core'=2,'x'=4] {'z','y','core'}, dimensions={0} | all-to-all | bytes 524288 | tf_op jit(solution)/shard_map/all_to_all | solution.py:38
  41.3 1.0 shard_map.165
  42.3 5.5 %all-to-all-start.1 = ((f32[128,4,128]{2,1,0:T(4,128)}), f32[128,4,128]{2,1,0:T(4,128)S(1)}, u32[]{:S(2)}, u32[]{:S(2)}) async-start(f32[128,4,128]{2,1,0:T(4,128)} %bitcast.4), calls=%async_computation.1 | async-start | bytes 524288 | tf_op jit(solution)/shard_map/all_to_all | solution.py:38
  48.6 4.7 %collective-permute-start.1 = (f32[448,128]{1,0:T(8,128)S(1)}, f32[448,128]{1,0:T(8,128)S(1)}, u32[]{:S(2)}, u32[]{:S(2)}) collective-permute-start(f32[448,128]{1,0:T(8,128)S(1)} %shard_map.166), channel_id=1, source_target_pairs={{0,3},{1,0},{2,1},{3,2},{4,7},{5,4},{6,5},{7,6},{8,11},{9,8},{10,9... | collective-permute-start | bytes 688136 | tf_op jit(solution)/shard_map/ppermute | solution.py:34
  53.3 3.9 %collective-permute-done.1.bucket_ref = f32[448,128]{1,0:T(8,128)S(1)} collective-permute-done((f32[448,128]{1,0:T(8,128)S(1)}, f32[448,128]{1,0:T(8,128)S(1)}, u32[]{:S(2)}, u32[]{:S(2)}) %collective-permute-start.1) | collective-permute-done | bytes 229408 | tf_op jit(solution)/shard_map/ppermute | solution.py:34
  57.2 6.0 %all-to-all-done.1 = f32[128,4,128]{2,1,0:T(4,128)S(1)} async-done(((f32[128,4,128]{2,1,0:T(4,128)}), f32[128,4,128]{2,1,0:T(4,128)S(1)}, u32[]{:S(2)}, u32[]{:S(2)}) %all-to-all-start.1) | async-done | bytes 262176 | tf_op jit(solution)/shard_map/all_to_all | solution.py:38
  63.2 2.9 %shard_map.167 = (f32[400,512]{1,0:T(8,128)S(1)}, f32[400,512]{1,0:T(8,128)S(1)}, f32[400,128]{1,0:T(8,128)S(1)}, f32[1,128]{1,0:T(1,128)S(1)}, f32[400,128]{1,0...) custom-call(s32[1,1]{1,0:T(1,128)} %bitcast.mine_ref, f32[512,128]{1,0:T(8,128)S(1)} %bitcast.30, ...), custom_call_target="tpu_custom_call" | custom-call | tf_op jit(solution)/shard_map/pallas_call | solution.py:60
  66.1 2.3 %collective-permute-start.2 = (f32[1280,128]{1,0:T(8,128)S(1)}, f32[1280,128]{1,0:T(8,128)S(1)}, u32[]{:S(2)}, u32[]{:S(2)}) collective-permute-start(f32[1280,128]{1,0:T(8,128)S(1)} %get-tuple-element.52), channel_id=1, source_target_pairs={{0,4},{4,0},{1,5},{5,1},{2,6},{6,2},{3,7},{7,3},{8,12},{12,8},{9,1... | collective-permute-start | bytes 1966088 | tf_op jit(solution)/shard_map/ppermute | solution.py:34
  68.9 1.2 collective-permute-done.2
  70.2 13.9 %all_to_all.56 = f32[4,320,128]{2,1,0:T(8,128)S(1)} all-to-all(f32[4,320,128]{2,1,0:T(8,128)S(1)} %bitcast.39), channel_id=1, replica_groups=mesh['z'=8,'y'=8,'core'=2,'x'=4] {'x'}, dimensions={0} | all-to-all | bytes 1310720 | tf_op jit(solution)/shard_map/all_to_all | solution.py:38
  84.2 11.0 %all_to_all.57 = f32[8,40,128]{2,1,0:T(8,128)S(1)} all-to-all(f32[8,40,128]{2,1,0:T(8,128)S(1)} %bitcast.41), channel_id=1, replica_groups=mesh['z'=8,'y'=8,'core'=2,'x'=4] {'y'}, dimensions={0} | all-to-all | bytes 327680 | tf_op jit(solution)/shard_map/all_to_all | solution.py:38
  95.2 14.9 %all_to_all.58 = f32[8,40,128]{2,1,0:T(8,128)S(1)} all-to-all(f32[8,40,128]{2,1,0:T(8,128)S(1)} %broadcast_in_dim.8), channel_id=1, replica_groups=mesh['z'=8,'y'=8,'core'=2,'x'=4] {'z'}, dimensions={0} | all-to-all | bytes 327680 | tf_op jit(solution)/shard_map/all_to_all | solution.py:38
  110.2 10.7 %all_to_all.59 = f32[8,40,128]{2,1,0:T(8,128)S(1)} all-to-all(f32[8,40,128]{2,1,0:T(8,128)S(1)} %broadcast_in_dim.9), channel_id=1, replica_groups=mesh['z'=8,'y'=8,'core'=2,'x'=4] {'y'}, dimensions={0} | all-to-all | bytes 327680 | tf_op jit(solution)/shard_map/all_to_all | solution.py:38
  120.9 10.0 %all_to_all.60 = f32[4,320,128]{2,1,0:T(8,128)S(1)} all-to-all(f32[4,320,128]{2,1,0:T(8,128)S(1)} %broadcast_in_dim.22), channel_id=1, replica_groups=mesh['z'=8,'y'=8,'core'=2,'x'=4] {'x'}, dimensions={0} | all-to-all | bytes 1310720 | tf_op jit(solution)/shard_map/all_to_all | solution.py:38
  130.9 8.7 %collective-permute-start.3 = (f32[1280,128]{1,0:T(8,128)S(1)}, f32[1280,128]{1,0:T(8,128)S(1)}, u32[]{:S(2)}, u32[]{:S(2)}) collective-permute-start(f32[1280,128]{1,0:T(8,128)S(1)} %bitcast.25), channel_id=1, source_target_pairs={{0,4},{4,0},{1,5},{5,1},{2,6},{6,2},{3,7},{7,3},{8,12},{12,8},{9,1... | collective-permute-start | bytes 1966088 | tf_op jit(solution)/shard_map/ppermute | solution.py:34
  141.3 3.7 %shard_map.170 = (f32[400,512]{1,0:T(8,128)S(1)}, f32[400,384]{1,0:T(8,128)S(1)}, f32[1,384]{1,0:T(1,128)S(1)}, f32[1536,128]{1,0:T(8,128)S(1)}, f32[1536,128]{1,0:T(8,128)S(1)}) custom-call(s32[1,1]{1,0:T(1,128)} %bitcast.mine_ref, s32[1,1]{1,0:T(1,128)} %collective-permute-done.partner_ref, f32[400,384]{1,0:T(8,128)S(1)} %get-tuple-element.65.own_ref.near_ref, ...), custom_call_target="tpu_custom_call" | custom-call | tf_op jit(solution)/shard_map/pallas_call | solution.py:60
  145.0 2.3 %collective-permute-start.4 = (f32[1536,128]{1,0:T(8,128)S(1)}, f32[1536,128]{1,0:T(8,128)S(1)}, u32[]{:S(2)}, u32[]{:S(2)}) collective-permute-start(f32[1536,128]{1,0:T(8,128)S(1)} %get-tuple-element.72), channel_id=1, source_target_pairs={{0,4},{4,0},{1,5},{5,1},{2,6},{6,2},{3,7},{7,3},{8,12},{12,8},{9,1... | collective-permute-start | bytes 2359304 | tf_op jit(solution)/shard_map/ppermute | solution.py:34
  147.7 1.6 collective-permute-done.4.got_ref
  149.3 13.0 %all_to_all.61.received_ref = f32[4,320,128]{2,1,0:T(8,128)S(1)} all-to-all(f32[4,320,128]{2,1,0:T(8,128)S(1)} %bitcast.40), channel_id=1, replica_groups=mesh['z'=8,'y'=8,'core'=2,'x'=4] {'x'}, dimensions={0} | all-to-all | bytes 1310720 | tf_op jit(solution)/shard_map/all_to_all | solution.py:38
  162.4 18.3 %all_to_all.62 = f32[64,3,4,128]{3,2,1,0:T(4,128)S(1)} all-to-all(f32[64,3,4,128]{3,2,1,0:T(4,128)S(1)} %bitcast.28), channel_id=1, replica_groups=mesh['z'=8,'y'=8,'core'=2,'x'=4] {'z','y'}, dimensions={0} | all-to-all | bytes 786432 | tf_op jit(solution)/shard_map/all_to_all | solution.py:38
  180.7 1.8 shard_map.173
  182.4 6.6 %all-to-all-start.9 = ((f32[64,3,4,128]{3,2,1,0:T(4,128)}), f32[64,3,4,128]{3,2,1,0:T(4,128)S(1)}, u32[]{:S(2)}, u32[]{:S(2)}) async-start(f32[64,3,4,128]{3,2,1,0:T(4,128)} %bitcast.18), calls=%async_computation.9 | async-start | bytes 786432 | tf_op jit(solution)/shard_map/all_to_all | solution.py:38
  189.1 2.2 collective-permute-start.5
  191.3 5.8 %collective-permute-done.5.source_ref = f32[408,128]{1,0:T(8,128)S(1)} collective-permute-done((f32[408,128]{1,0:T(8,128)S(1)}, f32[408,128]{1,0:T(8,128)S(1)}, u32[]{:S(2)}, u32[]{:S(2)}) %collective-permute-start.5) | collective-permute-done | bytes 208928 | tf_op jit(solution)/shard_map/ppermute | solution.py:34
  197.1 5.7 %all-to-all-done.9 = f32[64,3,4,128]{3,2,1,0:T(4,128)S(1)} async-done(((f32[64,3,4,128]{3,2,1,0:T(4,128)}), f32[64,3,4,128]{3,2,1,0:T(4,128)S(1)}, u32[]{:S(2)}, u32[]{:S(2)}) %all-to-all-start.9) | async-done | bytes 393248 | tf_op jit(solution)/shard_map/all_to_all | solution.py:38
  203.8 3.5 %all-to-all-start.10 = ((f32[4,320,128]{2,1,0:T(8,128)}), f32[4,320,128]{2,1,0:T(8,128)S(1)}, u32[]{:S(2)}, u32[]{:S(2)}) async-start(f32[4,320,128]{2,1,0:T(8,128)} %get-tuple-element.78), calls=%async_computation.10 | async-start | bytes 1310720 | tf_op jit(solution)/shard_map/all_to_all | solution.py:38
  207.3 6.4 %collective-permute-start.6 = (f32[256,128]{1,0:T(8,128)S(1)}, f32[256,128]{1,0:T(8,128)S(1)}, u32[]{:S(2)}, u32[]{:S(2)}) collective-permute-start(f32[256,128]{1,0:T(8,128)S(1)} %get-tuple-element.80), channel_id=1, source_target_pairs={{0,4},{4,0},{1,5},{5,1},{2,6},{6,2},{3,7},{7,3},{8,12},{12,8},{9,1... | collective-permute-start | bytes 393224 | tf_op jit(solution)/shard_map/ppermute | solution.py:34
  213.6 1.0 collective-permute-done.6.other_ref
  215.4 6.9 %collective-permute-start.7 = (f32[1280,128]{1,0:T(8,128)S(1)}, f32[1280,128]{1,0:T(8,128)S(1)}, u32[]{:S(2)}, u32[]{:S(2)}) collective-permute-start(f32[1280,128]{1,0:T(8,128)S(1)} %bitcast.23), channel_id=1, source_target_pairs={{0,4},{4,0},{1,5},{5,1},{2,6},{6,2},{3,7},{7,3},{8,12},{12,8},{9,1... | collective-permute-start | bytes 1966088 | tf_op jit(solution)/shard_map/ppermute | solution.py:34
  222.5 1.5 collective-permute-done.7.other_ref
  224.1 1.3 shard_map.177
  (43 shorter events, 7.8 us)
Async XLA Ops:
  0.6 7.0 %collective-permute-start = (s32[1,1]{1,0:T(1,128)}, s32[1,1]{1,0:T(1,128)}, u32[]{:S(2)}, u32[]{:S(2)}) collective-permute-start(s32[1,1]{1,0:T(1,128)} %param.18), channel_id=1, source_target_pairs={{0,3},{1,0},{2,1},{3,2},{4,7},{5,4},{6,5},{7,6},{8,11},{9,8},{10,9... | collective-permute-start | bytes 20 | tf_op jit(solution)/shard_map/ppermute | solution.py:34
  5.9 0.9 copy-start.2
  6.8 0.7 copy-start.8
  7.4 41.0 %copy-start.1 = (f32[400,128]{1,0:T(8,128)S(1)}, f32[400,128]{1,0:T(8,128)}, u32[]{:S(2)}) copy-start(f32[400,128]{1,0:T(8,128)} %source_ref.1) | copy-start | bytes 614404
  7.4 41.0 %copy-start.3 = (s32[1,1,2048]{2,1,0:T(1,128)S(1)}, s32[1,1,2048]{2,1,0:T(1,128)}, u32[]{:S(2)}) copy-start(s32[1,1,2048]{2,1,0:T(1,128)} %param.23) | copy-start | bytes 24580
  7.5 41.0 %copy-start.4 = (s32[1,1,1024]{2,1,0:T(1,128)S(1)}, s32[1,1,1024]{2,1,0:T(1,128)}, u32[]{:S(2)}) copy-start(s32[1,1,1024]{2,1,0:T(1,128)} %param.20) | copy-start | bytes 12292
  7.5 41.1 %copy-start.5 = (s32[1,1,1024]{2,1,0:T(1,128)S(1)}, s32[1,1,1024]{2,1,0:T(1,128)}, u32[]{:S(2)}) copy-start(s32[1,1,1024]{2,1,0:T(1,128)} %param.21) | copy-start | bytes 12292
  7.5 41.1 %copy-start.6 = (s32[1,1,1024]{2,1,0:T(1,128)S(1)}, s32[1,1,1024]{2,1,0:T(1,128)}, u32[]{:S(2)}) copy-start(s32[1,1,1024]{2,1,0:T(1,128)} %param.22) | copy-start | bytes 12292
  7.5 41.1 %copy-start.7 = (f32[128]{0:T(128)S(1)}, f32[128]{0:T(128)}, u32[]{:S(2)}) copy-start(f32[128]{0:T(128)} %param.13) | copy-start | bytes 1540
  7.6 55.6 %copy-start = (f32[400,768]{1,0:T(8,128)S(1)}, f32[400,768]{1,0:T(8,128)}, u32[]{:S(2)}) copy-start(f32[400,768]{1,0:T(8,128)} %relations_ref.5) | copy-start | bytes 3686404
  42.3 20.9 %all-to-all-start.1 = ((f32[128,4,128]{2,1,0:T(4,128)}), f32[128,4,128]{2,1,0:T(4,128)S(1)}, u32[]{:S(2)}, u32[]{:S(2)}) async-start(f32[128,4,128]{2,1,0:T(4,128)} %bitcast.4), calls=%async_computation.1 | async-start | bytes 524288 | tf_op jit(solution)/shard_map/all_to_all | solution.py:38
  48.6 8.6 %collective-permute-start.1 = (f32[448,128]{1,0:T(8,128)S(1)}, f32[448,128]{1,0:T(8,128)S(1)}, u32[]{:S(2)}, u32[]{:S(2)}) collective-permute-start(f32[448,128]{1,0:T(8,128)S(1)} %shard_map.166), channel_id=1, source_target_pairs={{0,3},{1,0},{2,1},{3,2},{4,7},{5,4},{6,5},{7,6},{8,11},{9,8},{10,9... | collective-permute-start | bytes 688136 | tf_op jit(solution)/shard_map/ppermute | solution.py:34
  66.1 4.0 %collective-permute-start.2 = (f32[1280,128]{1,0:T(8,128)S(1)}, f32[1280,128]{1,0:T(8,128)S(1)}, u32[]{:S(2)}, u32[]{:S(2)}) collective-permute-start(f32[1280,128]{1,0:T(8,128)S(1)} %get-tuple-element.52), channel_id=1, source_target_pairs={{0,4},{4,0},{1,5},{5,1},{2,6},{6,2},{3,7},{7,3},{8,12},{12,8},{9,1... | collective-permute-start | bytes 1966088 | tf_op jit(solution)/shard_map/ppermute | solution.py:34
  110.2 29.4 %copy-start.9 = (f32[768]{0:T(1024)S(1)}, f32[768]{0:T(1024)}, u32[]{:S(2)}) copy-start(f32[768]{0:T(1024)} %param.17) | copy-start | bytes 9220
  130.9 10.4 %collective-permute-start.3 = (f32[1280,128]{1,0:T(8,128)S(1)}, f32[1280,128]{1,0:T(8,128)S(1)}, u32[]{:S(2)}, u32[]{:S(2)}) collective-permute-start(f32[1280,128]{1,0:T(8,128)S(1)} %bitcast.25), channel_id=1, source_target_pairs={{0,4},{4,0},{1,5},{5,1},{2,6},{6,2},{3,7},{7,3},{8,12},{12,8},{9,1... | collective-permute-start | bytes 1966088 | tf_op jit(solution)/shard_map/ppermute | solution.py:34
  145.0 4.2 %collective-permute-start.4 = (f32[1536,128]{1,0:T(8,128)S(1)}, f32[1536,128]{1,0:T(8,128)S(1)}, u32[]{:S(2)}, u32[]{:S(2)}) collective-permute-start(f32[1536,128]{1,0:T(8,128)S(1)} %get-tuple-element.72), channel_id=1, source_target_pairs={{0,4},{4,0},{1,5},{5,1},{2,6},{6,2},{3,7},{7,3},{8,12},{12,8},{9,1... | collective-permute-start | bytes 2359304 | tf_op jit(solution)/shard_map/ppermute | solution.py:34
  182.4 20.4 %all-to-all-start.9 = ((f32[64,3,4,128]{3,2,1,0:T(4,128)}), f32[64,3,4,128]{3,2,1,0:T(4,128)S(1)}, u32[]{:S(2)}, u32[]{:S(2)}) async-start(f32[64,3,4,128]{3,2,1,0:T(4,128)} %bitcast.18), calls=%async_computation.9 | async-start | bytes 786432 | tf_op jit(solution)/shard_map/all_to_all | solution.py:38
  189.1 8.1 %collective-permute-start.5 = (f32[408,128]{1,0:T(8,128)S(1)}, f32[408,128]{1,0:T(8,128)S(1)}, u32[]{:S(2)}, u32[]{:S(2)}) collective-permute-start(f32[408,128]{1,0:T(8,128)S(1)} %shard_map.171), channel_id=1, source_target_pairs={{0,1},{1,2},{2,3},{3,0},{4,5},{5,6},{6,7},{7,4},{8,9},{9,10},{10,1... | collective-permute-start | bytes 626696 | tf_op jit(solution)/shard_map/ppermute | solution.py:34
  203.8 11.7 %all-to-all-start.10 = ((f32[4,320,128]{2,1,0:T(8,128)}), f32[4,320,128]{2,1,0:T(8,128)S(1)}, u32[]{:S(2)}, u32[]{:S(2)}) async-start(f32[4,320,128]{2,1,0:T(8,128)} %get-tuple-element.78), calls=%async_computation.10 | async-start | bytes 1310720 | tf_op jit(solution)/shard_map/all_to_all | solution.py:38
  207.3 7.3 %collective-permute-start.6 = (f32[256,128]{1,0:T(8,128)S(1)}, f32[256,128]{1,0:T(8,128)S(1)}, u32[]{:S(2)}, u32[]{:S(2)}) collective-permute-start(f32[256,128]{1,0:T(8,128)S(1)} %get-tuple-element.80), channel_id=1, source_target_pairs={{0,4},{4,0},{1,5},{5,1},{2,6},{6,2},{3,7},{7,3},{8,12},{12,8},{9,1... | collective-permute-start | bytes 393224 | tf_op jit(solution)/shard_map/ppermute | solution.py:34
  215.4 8.6 %collective-permute-start.7 = (f32[1280,128]{1,0:T(8,128)S(1)}, f32[1280,128]{1,0:T(8,128)S(1)}, u32[]{:S(2)}, u32[]{:S(2)}) collective-permute-start(f32[1280,128]{1,0:T(8,128)S(1)} %bitcast.23), channel_id=1, source_target_pairs={{0,4},{4,0},{1,5},{5,1},{2,6},{6,2},{3,7},{7,3},{8,12},{12,8},{9,1... | collective-permute-start | bytes 1966088 | tf_op jit(solution)/shard_map/ppermute | solution.py:34
